TPU v7x, 32 devices: a whole 2x2x4 slice. The times are simulated.
32 devices in a mesh: gx: 8 (over z, x), gz: 4 (over y, core).
Axes of the slice: x: 2, y: 2, z: 4, core: 2. Of those that a mesh axis runs over, the one named last changes fastest.
Arguments:
- conserved_fields: float32 [6, 128, 128, 128], P(None, 'gx', 'gz'), may hold values from -2 to 62, as said below
- coeff: bfloat16 [2, 1024, 6, 128, 512], P(None, 'gx', None, 'gz'), may hold values from -0.25 to 0.25
- feed_plane: int32 [12], replicated, may hold values from 0 to 2047
Outputs:
- new_state: float32 [6, 128, 128, 128], P(None, 'gx', 'gz')
Inputs may be any that keep to these rules, and one draw needn't show every extreme that they name: `conserved_fields`: each cell is the conserved form of a gas with density 0.5 to 2, temperature 0.5 to 2, streamwise velocity -1 to 7, wall-normal and spanwise velocities -1 to 1 and vibrational energy per unit mass 0.05 to 0.5.
All inputs are finite; a program needn't handle non-finite values.
Results may differ from a plain program's by a relative error of at most 0.00038.
Values sent between devices are 32-bit elements; how exact they have to be, the bound alone decides.
No kernel may reach another device: no remote copies, remote signals or barrier semaphores. Data moves between devices by JAX's collectives and lax.ppermute only.
A program may use at most 256 MiB of HBM per device.

v0:
```python
import math

import jax
import jax.numpy as jnp
from jax import lax
from jax.sharding import PartitionSpec as P

ADIABATIC_INDEX = 1.4
CAPACITY_CONST = 2.5
OSCILLATOR_SCALE = 2.0
VIBRANT_LAG = 0.5
LANDAU_FIT_LAW = 1.5
SURFACE_DIST_SQ = 0.36
TIME_STEP = 0.05
FORCING_RATE = 2.0
WENO_EPSILON = 1e-06


def with_halo(x, sides, width):
    for axis, dim in sides:
        devices, length = (lax.axis_size(axis), x.shape[dim])
        up = [(i, (i + 1) % devices) for i in range(devices)]
        down = [(j, i) for i, j in up]
        last = lax.slice_in_dim(x, length - width, length, axis=dim)
        leading = lax.slice_in_dim(x, 0, width, axis=dim)
        before = lax.ppermute(last, axis, up)
        after = lax.ppermute(leading, axis, down)
        x = jnp.concatenate([before, x, after], axis=dim)
    return x


def caloric_bundle(conserved_fields):
    fluid_rho_field = conserved_fields[0]
    motion_share = (
        0.5
        * (
            jnp.square(conserved_fields[1])
            + jnp.square(conserved_fields[2])
            + jnp.square(conserved_fields[3])
        )
        / jnp.square(fluid_rho_field)
    )
    translational_kelvin = (
        conserved_fields[4] / fluid_rho_field - motion_share - conserved_fields[5] / fluid_rho_field
    ) / CAPACITY_CONST
    thermodynamic_stress = fluid_rho_field * translational_kelvin
    return (fluid_rho_field, translational_kelvin, thermodynamic_stress)


def directional(extended_fields, component):
    fluid_rho_field, translational_kelvin, thermodynamic_stress = caloric_bundle(extended_fields)
    crossflow_flux_field = extended_fields[component] / fluid_rho_field
    flux_rows = []
    for member in range(6):
        entry = extended_fields[member] * crossflow_flux_field
        if member == component:
            entry = entry + thermodynamic_stress
        if member == 4:
            entry = entry + thermodynamic_stress * crossflow_flux_field
        flux_rows.append(entry)
    forcing_samples = jnp.abs(crossflow_flux_field) + jnp.sqrt(
        ADIABATIC_INDEX * translational_kelvin
    )
    return (jnp.stack(flux_rows), forcing_samples)


def weno_face(minus_two, minus_one, centre, plus_one, plus_two):
    low_poly = (2.0 * minus_two - 7.0 * minus_one + 11.0 * centre) / 6.0
    mid_poly = (-minus_one + 5.0 * centre + 2.0 * plus_one) / 6.0
    high_poly = (2.0 * centre + 5.0 * plus_one - plus_two) / 6.0
    low_beta = 13.0 / 12.0 * jnp.square(minus_two - 2.0 * minus_one + centre) + 0.25 * jnp.square(
        minus_two - 4.0 * minus_one + 3.0 * centre
    )
    mid_beta = 13.0 / 12.0 * jnp.square(minus_one - 2.0 * centre + plus_one) + 0.25 * jnp.square(
        minus_one - plus_one
    )
    high_beta = 13.0 / 12.0 * jnp.square(centre - 2.0 * plus_one + plus_two) + 0.25 * jnp.square(
        3.0 * centre - 4.0 * plus_one + plus_two
    )
    low_weight = 0.1 / jnp.square(WENO_EPSILON + low_beta)
    mid_weight = 0.6 / jnp.square(WENO_EPSILON + mid_beta)
    high_weight = 0.3 / jnp.square(WENO_EPSILON + high_beta)
    return (low_weight * low_poly + mid_weight * mid_poly + high_weight * high_poly) / (
        low_weight + mid_weight + high_weight
    )


def sweep_axis(extended_fields, axis, component):
    length = extended_fields.shape[axis] - 6
    fluxes, forcing_samples = directional(extended_fields, component)

    def window(array, offset, dim):
        return lax.slice_in_dim(array, offset, offset + length + 1, axis=dim)

    wave_speed = window(forcing_samples, 0, axis - 1)
    for offset in range(1, 6):
        wave_speed = jnp.maximum(wave_speed, window(forcing_samples, offset, axis - 1))
    wave_speed = wave_speed[None]
    upwind = [
        0.5 * (window(fluxes, offset, axis) + wave_speed * window(extended_fields, offset, axis))
        for offset in range(5)
    ]
    downwind = [
        0.5 * (window(fluxes, offset, axis) - wave_speed * window(extended_fields, offset, axis))
        for offset in (5, 4, 3, 2, 1)
    ]
    face_flux = weno_face(*upwind) + weno_face(*downwind)
    return lax.slice_in_dim(face_flux, 1, length + 1, axis=axis) - lax.slice_in_dim(
        face_flux, 0, length, axis=axis
    )


def wall_pad(conserved_fields):
    reflected_fields = conserved_fields[:, :, :, 2::-1]
    translational_kelvin = caloric_bundle(reflected_fields)[1]
    ghost_layer_kelvin = SURFACE_DIST_SQ / translational_kelvin
    ghost_layer_oscillator = reflected_fields[4] - CAPACITY_CONST * reflected_fields[0] * (
        translational_kelvin - ghost_layer_kelvin
    )
    ghost_cells = jnp.stack(
        [
            reflected_fields[0],
            -reflected_fields[1],
            -reflected_fields[2],
            -reflected_fields[3],
            ghost_layer_oscillator,
            reflected_fields[5],
        ]
    )
    top_cells = jnp.repeat(conserved_fields[:, :, :, -1:], 3, axis=3)
    return jnp.concatenate([ghost_cells, conserved_fields, top_cells], axis=3)


def relaxation(conserved_fields):
    fluid_rho_field, translational_kelvin, thermodynamic_stress = caloric_bundle(conserved_fields)
    balanced_oscillator_share = OSCILLATOR_SCALE / (
        jnp.exp(OSCILLATOR_SCALE / translational_kelvin) - 1.0
    )
    settling_interval = (
        VIBRANT_LAG
        * jnp.exp(LANDAU_FIT_LAW * (jnp.exp(-jnp.log(translational_kelvin) / 3.0) - 1.0))
        / thermodynamic_stress
    )
    return (fluid_rho_field * balanced_oscillator_share - conserved_fields[5]) / settling_interval


def local(conserved_fields, coeff, feed_plane):
    groups_x = lax.axis_size("gx")
    groups_z = lax.axis_size("gz")
    plane_count = conserved_fields.shape[1]
    span_cells = conserved_fields.shape[2]
    span_total = span_cells * groups_z
    kx_local = coeff.shape[1]
    levels_local = coeff.shape[3]
    span_modes = coeff.shape[4]
    stream_points = 2 * kx_local * groups_x
    planes = feed_plane.shape[0]
    span_ids = (
        jnp.arange(span_modes, dtype=jnp.int32)[:, None]
        * jnp.arange(span_total, dtype=jnp.int32)[None, :]
        % span_modes
    )
    span_angle = 2.0 * math.pi / span_modes * span_ids.astype(jnp.float32)
    span_table = jnp.concatenate([jnp.cos(span_angle), jnp.sin(span_angle)], axis=1).astype(
        jnp.bfloat16
    )
    mode_ids = lax.axis_index("gx") * kx_local + jnp.arange(kx_local, dtype=jnp.int32)
    stream_ids = feed_plane[:, None] * mode_ids[None, :] % stream_points
    stream_angle = 2.0 * math.pi / stream_points * stream_ids.astype(jnp.float32)
    stream_table = jnp.concatenate([jnp.cos(stream_angle), -jnp.sin(stream_angle)], axis=1).astype(
        jnp.bfloat16
    )
    coeff_rows = coeff.reshape(2 * kx_local * 6 * levels_local, span_modes)
    product = jnp.dot(coeff_rows, span_table, preferred_element_type=jnp.float32)
    product = product.reshape(2, kx_local, 6, levels_local, 2 * span_total)
    real_part = product[0, :, :, :, :span_total] - product[1, :, :, :, span_total:]
    imag_part = product[0, :, :, :, span_total:] + product[1, :, :, :, :span_total]
    mixed_modes = jnp.concatenate([real_part, imag_part], axis=0).astype(jnp.bfloat16)
    row_block = (6 * planes + groups_x - 1) // groups_x
    total_rows = row_block * groups_x
    table_rows = total_rows // 6 + 3
    padded_table = jnp.concatenate(
        [stream_table, jnp.zeros((table_rows - planes, 2 * kx_local), jnp.bfloat16)], axis=0
    )
    modes_flat = mixed_modes.reshape(2 * kx_local, 6 * levels_local * span_total)
    start = jnp.int32(0)
    plane_span = row_block * lax.axis_size("gx") // 6 + 2
    first_plane = start // 6
    table_block = lax.dynamic_slice_in_dim(padded_table, first_plane, plane_span, 0)
    products = jnp.dot(table_block, modes_flat, preferred_element_type=jnp.float32)
    products = products.reshape(plane_span * 6, levels_local * span_total)
    reduced = lax.psum_scatter(
        lax.dynamic_slice_in_dim(products, start, row_block * lax.axis_size("gx"), 0),
        "gx",
        scatter_dimension=0,
        tiled=True,
    )
    reduced = reduced.reshape(row_block, levels_local, span_total)
    relaid = lax.all_to_all(reduced, "gz", split_axis=2, concat_axis=1, tiled=True)
    collected = lax.all_gather(relaid, "gx", axis=0, tiled=True)
    feed_values = collected[: 6 * planes].reshape(planes, 6, levels_local * groups_z, span_cells)
    target = jnp.transpose(feed_values, (1, 0, 3, 2))
    stream_pad = with_halo(conserved_fields, (("gx", 1),), 3)
    span_pad = with_halo(conserved_fields, (("gz", 2),), 3)
    at_inlet = lax.axis_index("gx") == 0
    at_outlet = lax.axis_index("gx") == groups_x - 1
    lower = jnp.where(at_inlet, jnp.repeat(conserved_fields[:, :1], 3, axis=1), stream_pad[:, :3])
    upper = jnp.where(
        at_outlet, jnp.repeat(conserved_fields[:, -1:], 3, axis=1), stream_pad[:, -3:]
    )
    stream_pad = jnp.concatenate([lower, conserved_fields, upper], axis=1)
    tendency = -(
        sweep_axis(stream_pad, 1, 1)
        + sweep_axis(span_pad, 2, 3)
        + sweep_axis(wall_pad(conserved_fields), 3, 2)
    )
    tendency = tendency.at[5].add(relaxation(conserved_fields))
    plane_global = lax.axis_index("gx") * plane_count + jnp.arange(plane_count, dtype=jnp.int32)
    inside = plane_global < planes
    strength = jnp.where(
        inside, FORCING_RATE * jnp.square(1.0 - plane_global.astype(jnp.float32) / planes), 0.0
    )
    picked = jnp.take(target, jnp.minimum(plane_global, planes - 1), axis=1)
    tendency = tendency + strength[None, :, None, None] * (picked - conserved_fields)
    return conserved_fields + TIME_STEP * tendency


def solution(mesh):
    placed = (P(None, "gx", "gz", None), P(None, "gx", None, "gz", None), P())
    return jax.shard_map(
        local, mesh=mesh, in_specs=placed, out_specs=P(None, "gx", "gz", None), check_vma=False
    )
```

profile of v0, /device:TPU:0, one launch (start us, length us, event | category | flops | bytes accessed | tf_op | source)
XLA Modules:
  0.0 306.0 jit_solution(16158845264084242990)
XLA Ops:
  6.5 1.7 constant_dynamic-update-slice_fusion.1
  9.1 2.4 collective-permute-start.3
  12.3 4.5 %collective-permute-start.1 = (f32[6,3,32,128]{3,2,0,1:T(8,128)}, f32[6,3,32,128]{3,2,0,1:T(8,128)}, u32[]{:S(2)}, u32[]{:S(2)}) collective-permute-start(f32[6,3,32,128]{3,2,0,1:T(8,128)} %get-tuple-element.31), channel_id=1, source_target_pairs={{4,0},{8,4},{12,8},{16,12},{20,16},{24,20},{28,24},{0,28},{5,1},{9... | collective-permute-start | bytes 884744 | tf_op jit(solution)/shard_map/ppermute | solution.py:27
  16.9 1.7 sine_convert_fusion
  18.6 37.8 %convolution_bitcast_fusion = f32[49152,256]{0,1:T(8,128)} fusion(bf16[49152,512]{1,0:T(8,128)(2,1)} %bitcast.49, bf16[512,128]{1,0:T(8,128)(2,1)} %get-tuple-element.44, bf16[512,128]{1,0:T(8,128)(2,1)} %get-tuple-element.45), kind=kOutput, calls=%fused_computation.1 | convolution fusion | flops 12885426176 | bytes 100925440 | tf_op jit(solution)/shard_map/dot_general | solution.py:174
  56.4 48.8 %copy.101 = f32[49152,256]{1,0:T(8,128)} copy(f32[49152,256]{0,1:T(8,128)} %convolution_bitcast_fusion) | data formatting | bytes 100663296 | tf_op jit(solution)/shard_map/dot_general | solution.py:174
  105.3 23.1 %fusion.1 = (bf16[1,128,6,32,128]{4,3,2,1,0:T(8,128)(2,1)}, bf16[1,128,6,32,128]{4,3,2,1,0:T(8,128)(2,1)}) fusion(f32[2,128,6,32,256]{4,3,2,1,0:T(8,128)} %bitcast.48), kind=kLoop, calls=%fused_computation.5 | loop fusion | flops 12582912 | bytes 62914560 | tf_op jit(solution)/shard_map/convert.3
  128.4 9.3 %copy.103 = bf16[1,128,6,32,128]{1,4,3,2,0:T(8,128)(2,1)} copy(bf16[1,128,6,32,128]{4,3,2,1,0:T(8,128)(2,1)} %get-tuple-element.27) | data formatting | bytes 12582912 | tf_op jit(solution)/shard_map/convert.2
  137.7 9.3 %copy.102 = bf16[1,128,6,32,128]{1,4,3,2,0:T(8,128)(2,1)} copy(bf16[1,128,6,32,128]{4,3,2,1,0:T(8,128)(2,1)} %get-tuple-element.26) | data formatting | bytes 12582912 | tf_op jit(solution)/shard_map/convert.3
  147.1 7.3 %fusion.2 = f32[12,24576]{1,0:T(8,128)} fusion(bf16[128,24576]{0,1:T(8,128)(2,1)} %bitcast.51, bf16[128,24576]{0,1:T(8,128)(2,1)} %bitcast.52, bf16[12,128]{1,0:T(8,128)(2,1)S(1)} %get-tuple-element.43, bf16[12,128]{1,0:T(8,128)(2,1)S(1)} %get-tuple-element.42), kind=kOutput, calls=%fused_computation.6 | convolution fusion | flops 176173056 | bytes 13768704 | tf_op jit(solution)/shard_map/dot_general | solution.py:190
  154.4 2.8 dynamic_slice.10
  157.2 3.1 %slice.506 = f32[6,16,32,1]{3,2,1,0:T(8,128)} slice(f32[6,16,32,128]{3,2,1,0:T(8,128)} %param.5), slice={[0:6], [0:16], [0:32], [127:128]} | slice | bytes 24576 | tf_op jit(solution)/shard_map/slice | solution.py:130
  162.2 2.8 copy.120
  165.1 1.7 copy.113
  168.1 1.7 copy.114
  169.9 1.7 copy.115
  171.6 1.7 copy.116
  173.3 1.7 copy.117
  175.1 1.7 copy.118
  180.8 1.5 constant_dynamic-update-slice_fusion.3
  183.6 2.7 copy.90
  191.2 19.7 %divide_add_fusion = f32[6,16,32,129]{3,2,0,1:T(8,128)} fusion(f32[6,16,32,3]{3,2,0,1:T(8,128)S(1)} %reshape.153, f32[6,16,32,128]{3,2,0,1:T(8,128)S(1)} %get-tuple-element.35, f32[6,16,32,134]{3,2,0,1:T(8,128)S(1)} %multiply_dynamic-update-slice_fusion.1, f32[6,16,32,3]{3,2,0,1:T(8,128)S(1)} %copy-done.2, f32[16,32,129]{2,1,0:T(8,128)S(1)} %slice_maximum_fusion), kind=kLoop, calls=%fused_computation.33 | loop fusion | flops 60632064 | bytes 13006848 | tf_op jit(solution)/shard_map/add | solution.py:107
  215.3 13.0 %divide_add_fusion.1 = f32[6,16,33,128]{3,2,0,1:T(8,128)} fusion(f32[6,16,35,128]{3,2,0,1:T(8,128)S(1)} %constant_dynamic-update-slice_fusion, f32[6,16,38,128]{3,2,0,1:T(8,128)S(1)} %multiply_dynamic-update-slice_fusion.11, f32[6,16,32,128]{3,2,0,1:T(8,128)S(1)} %get-tuple-element.35, f32[6,16,3,128]{3,2,0,1:T(4,128)} %collective-permute-done.2, ...), kind=kLoop, calls=%fused_computation.61 | loop fusion | flops 60825600 | bytes 18210816 | tf_op jit(solution)/shard_map/add | solution.py:107
  236.4 2.1 all-reduce.4.cloned.1.call-done
  241.2 3.3 %all-to-all-start = ((f32[4,1,9216]{2,1,0:T(1,128)}), f32[4,1,9216]{2,1,0:T(1,128)S(1)}, u32[]{:S(2)}, u32[]{:S(2)}) async-start(f32[4,1,9216]{2,1,0:T(1,128)} %reshape.201), calls=%async_computation | async-start | bytes 294912 | tf_op jit(solution)/shard_map/all_to_all | solution.py:199
  245.5 3.7 %all-to-all-done = f32[4,1,9216]{2,1,0:T(1,128)S(1)} async-done(((f32[4,1,9216]{2,1,0:T(1,128)}), f32[4,1,9216]{2,1,0:T(1,128)S(1)}, u32[]{:S(2)}, u32[]{:S(2)}) %all-to-all-start) | async-done | bytes 147488 | tf_op jit(solution)/shard_map/all_to_all | solution.py:199
  252.5 11.7 %divide_add_fusion.2 = f32[6,17,32,128]{3,2,0,1:T(8,128)S(1)} fusion(f32[6,3,32,128]{3,2,0,1:T(8,128)S(1)} %copy-done.6, f32[6,16,32,128]{3,2,0,1:T(8,128)S(1)} %get-tuple-element.35, f32[6,22,32,128]{3,2,0,1:T(8,128)} %multiply_dynamic-update-slice_fusion.6, f32[6,3,32,128]{3,2,0,1:T(8,128)} %copy-done.7, f32[17,32,128]{2,1,0:T(8,128)} %fusion.53), kind=kLoop, calls=%fused_computation.86 | loop fusion | flops 63922176 | bytes 14139392 | tf_op jit(solution)/shard_map/add | solution.py:107
  264.3 1.9 fusion.47
  266.1 2.0 fusion.64
  268.2 23.9 %all-gather.2.cloned.1.call-done = f32[72,128,32]{1,2,0:T(8,128)} async-done(((f32[9,128,32]{1,2,0:T(8,128)}), f32[72,128,32]{1,2,0:T(8,128)}) %all-gather.2.cloned.1.call-update) | async-done | bytes 1179664 | tf_op jit(solution)/shard_map/all_gather | solution.py:200
  293.5 1.8 gather_fusion
  295.3 2.5 fusion.52
  (93 shorter events, 36.5 us)
Async XLA Ops:
  6.5 232.0 %all-reduce.4.cloned.1.call-start = ((), (), s32[]{:S(2)}) async-start(), calls=%async_computation.2 | async-start | bytes 2359296
  9.1 203.1 %collective-permute-start.3 = (f32[6,16,3,128]{3,2,0,1:T(4,128)}, f32[6,16,3,128]{3,2,0,1:T(4,128)}, u32[]{:S(2)}, u32[]{:S(2)}) collective-permute-start(f32[6,16,3,128]{3,2,0,1:T(4,128)} %get-tuple-element.33), channel_id=1, source_target_pairs={{1,0},{2,1},{3,2},{0,3},{5,4},{6,5},{7,6},{4,7},{9,8},{10,9},{11,1... | collective-permute-start | bytes 442376 | tf_op jit(solution)/shard_map/ppermute | solution.py:27
  11.5 200.7 %collective-permute-start.2 = (f32[6,16,3,128]{3,2,0,1:T(4,128)}, f32[6,16,3,128]{3,2,0,1:T(4,128)}, u32[]{:S(2)}, u32[]{:S(2)}) collective-permute-start(f32[6,16,3,128]{3,2,0,1:T(4,128)} %get-tuple-element.32), channel_id=1, source_target_pairs={{0,1},{1,2},{2,3},{3,0},{4,5},{5,6},{6,7},{7,4},{8,9},{9,10},{10,1... | collective-permute-start | bytes 442376 | tf_op jit(solution)/shard_map/ppermute | solution.py:26
  12.3 216.0 %collective-permute-start.1 = (f32[6,3,32,128]{3,2,0,1:T(8,128)}, f32[6,3,32,128]{3,2,0,1:T(8,128)}, u32[]{:S(2)}, u32[]{:S(2)}) collective-permute-start(f32[6,3,32,128]{3,2,0,1:T(8,128)} %get-tuple-element.31), channel_id=1, source_target_pairs={{4,0},{8,4},{12,8},{16,12},{20,16},{24,20},{28,24},{0,28},{5,1},{9... | collective-permute-start | bytes 884744 | tf_op jit(solution)/shard_map/ppermute | solution.py:27
  16.9 212.5 %collective-permute-start = (f32[6,3,32,128]{3,2,0,1:T(8,128)}, f32[6,3,32,128]{3,2,0,1:T(8,128)}, u32[]{:S(2)}, u32[]{:S(2)}) collective-permute-start(f32[6,3,32,128]{3,2,0,1:T(8,128)} %get-tuple-element.30), channel_id=1, source_target_pairs={{0,4},{4,8},{8,12},{12,16},{16,20},{20,24},{24,28},{28,0},{1,5},{5... | collective-permute-start | bytes 884744 | tf_op jit(solution)/shard_map/ppermute | solution.py:26
  137.7 9.3 %copy-start.10 = (s32[12]{0:T(128)S(1)}, s32[12]{0:T(128)}, u32[]{:S(2)}) copy-start(s32[12]{0:T(128)} %param.7) | copy-start | bytes 148
  157.2 3.2 %copy-start = (f32[6,16,32,128]{3,2,1,0:T(8,128)S(1)}, f32[6,16,32,128]{3,2,1,0:T(8,128)}, u32[]{:S(2)}) copy-start(f32[6,16,32,128]{3,2,1,0:T(8,128)} %param.5) | copy-start | bytes 4718596
  186.3 1.4 copy-start.2
  191.2 19.7 %copy-start.11 = (u32[32]{0:T(128)S(1)}, u32[32]{0:T(128)}, u32[]{:S(2)}) copy-start(u32[32]{0:T(128)} %constant.299) | copy-start | bytes 388
  215.3 13.0 %copy-start.9 = (f32[6,32,128]{2,1,0:T(8,128)S(1)}, f32[6,32,128]{2,1,0:T(8,128)}, u32[]{:S(2)}) copy-start(f32[6,32,128]{2,1,0:T(8,128)} %get-tuple-element.29) | copy-start | bytes 294916
  215.3 14.0 %copy-start.8 = (f32[6,32,128]{2,1,0:T(8,128)S(1)}, f32[6,32,128]{2,1,0:T(8,128)}, u32[]{:S(2)}) copy-start(f32[6,32,128]{2,1,0:T(8,128)} %get-tuple-element.28) | copy-start | bytes 294916
  229.3 0.7 copy-start.5
  230.0 0.7 copy-start.7
  241.2 8.1 %all-to-all-start = ((f32[4,1,9216]{2,1,0:T(1,128)}), f32[4,1,9216]{2,1,0:T(1,128)S(1)}, u32[]{:S(2)}, u32[]{:S(2)}) async-start(f32[4,1,9216]{2,1,0:T(1,128)} %reshape.201), calls=%async_computation | async-start | bytes 294912 | tf_op jit(solution)/shard_map/all_to_all | solution.py:199
  244.5 47.6 %all-gather.2.cloned.1.call-start = ((), (), s32[]{:S(2)}) async-start(), calls=%async_computation.1 | async-start | bytes 1327104 | tf_op jit(solution)/shard_map/all_gather | solution.py:200
  249.8 2.7 copy-start.6
  252.5 11.7 %copy-start.3 = (f32[6,16,33,128]{3,2,0,1:T(8,128)S(1)}, f32[6,16,33,128]{3,2,0,1:T(8,128)}, u32[]{:S(2)}) copy-start(f32[6,16,33,128]{3,2,0,1:T(8,128)} %divide_add_fusion.1) | copy-start | bytes 4866052
  252.5 11.7 %copy-start.4 = (f32[6,16,32,129]{3,2,0,1:T(8,128)S(1)}, f32[6,16,32,129]{3,2,0,1:T(8,128)}, u32[]{:S(2)}) copy-start(f32[6,16,32,129]{3,2,0,1:T(8,128)} %divide_add_fusion) | copy-start | bytes 4755460
  293.5 1.8 copy-start.1
Sparse Core Ops, SparseCore 0:
  157.3 81.1 all-reduce.3
  252.6 39.4 all-gather.1
where the time goes:
time: 308 us; the launch traced here: 306 us
  local copies, waits for them, and re-layouts  111 us (36%)
  other arithmetic  95.3 us (31%)
  matrix products  45.1 us (15%)
  waiting for transfers between devices  29.8 us (10%)
  between operations  14.4 us (5%)
  starting transfers between devices  10.5 us (3%)
    dot_general x1, local copies, waits for them, and re-layouts, local(): jnp.dot(coeff_rows, span_table, preferred_element_type=jnp.float32)  48.8 us
    add x3, other arithmetic, sweep_axis(): face_flux = weno_face(*upwind) + weno_face(*downwind)  44.4 us
    dot_general x1, matrix products, local(): jnp.dot(coeff_rows, span_table, preferred_element_type=jnp.float32)  37.8 us
    another operation x3, other arithmetic  25 us
    all_gather x1, waiting for transfers between devices, local(): collected = lax.all_gather(relaid, 'gx', axis=0, tiled=True)  23.9 us
    another operation x2, local copies, waits for them, and re-layouts  18.6 us
    unnamed x37, local copies, waits for them, and re-layouts  17.8 us
    unnamed x19, other arithmetic  10.7 us
  transfers between devices with their start and end apart: 7, of which 3 were waited for; matrix products, arithmetic and copies ran while one was open for 77% of the time, Pallas kernels for 0%

commit v1 on v0

v1 whole, which is shorter than its diff:
```python
import functools
import math

import jax
import jax.numpy as jnp
import numpy as np
from jax import lax
from jax.experimental import pallas as pl
from jax.experimental.pallas import tpu as pltpu
from jax.sharding import Mesh, PartitionSpec as P

SUB, LANE = 8, 128
EPS = 3e-6
F32, BF16 = jnp.float32, jnp.bfloat16


def cell_flux(q, comp):
    r, m1, m2, m3, e, ev = q
    rinv = 1.0 / r
    kin = 0.5 * (m1 * m1 + m2 * m2 + m3 * m3) * rinv
    p = 0.4 * (e - kin - ev)
    un = q[comp] * rinv
    c = jnp.sqrt(1.4 * p * rinv)
    flux = [v * un for v in q]
    flux[comp] = flux[comp] + p
    flux[4] = (e + p) * un
    return flux, jnp.abs(un) + c


def correction(gmm, gm, gp, gpp):
    u0 = gmm - 1.375 * gm
    u1 = gm - 0.625 * gp
    u1r = gp - 0.625 * gm
    u2 = gpp - 1.375 * gp
    tm = (0.609375 * gm) * gm + EPS
    tp = (0.609375 * gp) * gp + EPS
    s0 = u0 * u0 + tm
    s1 = u1 * u1 + tp
    s2 = u2 * u2 + tp
    left = u0 + u1r
    right = u2 + u1
    p12 = s1 * s2
    p01 = s0 * s1
    p02 = s0 * s2
    w0 = p12 * p12
    w2 = 3.0 * (p01 * p01)
    w1 = 6.0 * (p02 * p02)
    num = (w0 + w0) * left + w2 * right
    den = w0 + w1 + w2
    return num * pl.reciprocal(den, approx=True)


def sweep(comp, cells, low, mid, high, put, gf_ref, gq_ref, mx_ref):
    def step(j, carry, q):
        flux, s = cell_flux(q, comp)
        pf, pq, ps = carry
        for v in range(6):
            gf_ref[v, j - 1] = flux[v] - pf[v]
            gq_ref[v, j - 1] = q[v] - pq[v]
        mx_ref[j - 1] = jnp.maximum(s, ps)
        return flux, q, s

    q0 = low(0)
    f0, s0 = cell_flux(q0, comp)
    carry = (f0, q0, s0)
    for j in (1, 2):
        carry = step(j, carry, low(j))
    carry = lax.fori_loop(0, cells, lambda j, c: step(j + 3, c, mid(j)), carry)
    for j in range(3):
        carry = step(cells + 3 + j, carry, high(j))

    def face(f):
        a = jnp.maximum(jnp.maximum(mx_ref[f], mx_ref[f + 2]), mx_ref[f + 4])
        out = []
        for v in range(6):
            g = [gf_ref[v, f + k] for k in range(5)]
            h = [a * gq_ref[v, f + k] for k in range(5)]
            up = correction(g[0] + h[0], g[1] + h[1], g[2] + h[2], g[3] + h[3])
            down = correction(g[4] - h[4], g[3] - h[3], g[2] - h[2], g[1] - h[1])
            out.append((h[1] + h[3] - (h[2] + h[2])) + (down - up))
        return out

    def body(f, before):
        after = face(f)
        total = []
        for v in range(6):
            g = [gf_ref[v, f + k] for k in range(4)]
            total.append(7.0 * (g[2] + g[1]) - (g[3] + g[0]) + (after[v] - before[v]))
        put(f - 1, total)
        return after

    lax.fori_loop(1, cells + 1, body, face(0))


def scratch(cells):
    return [
        pltpu.VMEM((6, cells + 5, SUB, LANE), F32),
        pltpu.VMEM((6, cells + 5, SUB, LANE), F32),
        pltpu.VMEM((cells + 5, SUB, LANE), F32),
    ]


def stream_kernel(nx, nz, flags, q_ref, lo_ref, hi_ref, acc_ref, gf, gq, mx):
    first, last = flags[0] == 1, flags[1] == 1

    @pl.loop(0, nz // SUB)
    def _(t):
        base = pl.multiple_of(t * SUB, SUB)

        def mid(j):
            return [q_ref[pl.ds(pl.multiple_of((v * nx + j) * nz + base, SUB), SUB), :] for v in range(6)]

        def side(ref, flag, edge):
            def load(j):
                return [
                    jnp.where(flag, e, ref[pl.ds(pl.multiple_of((v * 3 + j) * nz + base, SUB), SUB), :])
                    for v, e in enumerate(mid(edge))
                ]
            return load

        def put(c, total):
            for v in range(6):
                acc_ref[pl.ds(pl.multiple_of((v * nx + c) * nz + base, SUB), SUB), :] = total[v]

        sweep(1, nx, side(lo_ref, first, 0), mid, side(hi_ref, last, nx - 1), put, gf, gq, mx)


def span_kernel(nx, nz, q_ref, lo_ref, hi_ref, acc_in, acc_ref, gf, gq, mx):
    @pl.loop(0, nx // SUB)
    def _(t):
        base = t * (SUB * nz)
        hbase = pl.multiple_of(t * SUB, SUB)

        def rows(v, j):
            return pl.ds(v * nx * nz + base + j, SUB, stride=nz)

        def mid(j):
            return [q_ref[rows(v, j), :] for v in range(6)]

        def side(ref):
            def load(j):
                return [ref[pl.ds(pl.multiple_of((v * 3 + j) * nx + hbase, SUB), SUB), :] for v in range(6)]
            return load

        def put(c, total):
            for v in range(6):
                acc_ref[rows(v, c), :] = acc_in[rows(v, c), :] + total[v]

        sweep(3, nz, side(lo_ref), mid, side(hi_ref), put, gf, gq, mx)


def wall_kernel(nx, nz, ny, strength, q_ref, acc_in, out_ref, yq, yt, gf, gq, mx):
    seg = ny // SUB
    cells = nx * nz

    @pl.loop(0, cells // LANE)
    def _(t):
        base = pl.multiple_of(t * LANE, LANE)
        for v in range(6):
            block = q_ref[pl.ds(pl.multiple_of(v * cells + base, LANE), LANE), :]
            yq[v, SUB : SUB + ny] = block.T
        q = [yq[v, SUB : 2 * SUB] for v in range(6)]
        rinv = 1.0 / q[0]
        temp = 0.4 * (q[4] - 0.5 * (q[1] * q[1] + q[2] * q[2] + q[3] * q[3]) * rinv - q[5]) * rinv
        ghost = [q[0], -q[1], -q[2], -q[3], q[4] - 2.5 * q[0] * (temp - 0.36 / temp), q[5]]
        for v in range(6):
            top = yq[v, SUB + ny - 1 : SUB + ny]
            for j in range(3):
                yq[v, SUB - 1 - j : SUB - j] = ghost[v][j : j + 1]
                yq[v, SUB + ny + j : SUB + ny + j + 1] = top

        def load(j):
            return [yq[v, pl.ds(SUB + j, SUB, stride=seg), :] for v in range(6)]

        def put(c, total):
            for v in range(6):
                yt[v, pl.ds(c, SUB, stride=seg), :] = total[v]

        sweep(2, seg, lambda j: load(j - 3), load, lambda j: load(seg + j), put, gf, gq, mx)

        for v in range(6):
            yt[v] = yt[v].T

        @pl.loop(0, LANE // SUB)
        def _(i):
            o = pl.multiple_of(i * SUB, SUB)
            rows = [pl.ds(pl.multiple_of(v * cells + base + o, SUB), SUB) for v in range(6)]
            q = [q_ref[rows[v], :] for v in range(6)]
            rinv = 1.0 / q[0]
            p = 0.4 * (q[4] - 0.5 * (q[1] * q[1] + q[2] * q[2] + q[3] * q[3]) * rinv - q[5])
            temp = p * rinv
            share = 2.0 / (jnp.exp(2.0 / temp) - 1.0)
            lag = jnp.exp(1.5 * (jnp.exp(-jnp.log(temp) / 3.0) - 1.0))
            relax = (q[0] * share - q[5]) * (2.0 * p) / lag
            pull = strength[(base + o) // nz]
            for v in range(6):
                rate = (acc_in[rows[v], :] + yt[v, pl.ds(o, SUB), :]) * (-1.0 / 12.0)
                if v == 5:
                    rate = rate + relax
                out_ref[rows[v], :] = q[v] + 0.05 * (rate - pull * q[v])


VM = pl.BlockSpec(memory_space=pltpu.VMEM)


def cost(n):
    return pl.CostEstimate(flops=n * 4000, bytes_accessed=n * 60, transcendentals=n * 12)


def params():
    return pltpu.CompilerParams(vmem_limit_bytes=40 * 2**20)


def rhs(q, xlo, xhi, zlo, zhi, edges, strength):
    _, nx, nz, ny = q.shape
    flat = q.reshape(6 * nx * nz, ny)
    shape = jax.ShapeDtypeStruct(flat.shape, F32)
    acc = pl.pallas_call(
        functools.partial(stream_kernel, nx, nz), out_shape=shape, name="stream_sweep",
        in_specs=[pl.BlockSpec(memory_space=pltpu.SMEM), VM, VM, VM], out_specs=VM,
        scratch_shapes=scratch(nx), compiler_params=params(), cost_estimate=cost(nx * nz * ny),
    )(edges, flat, xlo.reshape(-1, ny), xhi.reshape(-1, ny))
    acc = pl.pallas_call(
        functools.partial(span_kernel, nx, nz), out_shape=shape, name="span_sweep",
        in_specs=[VM] * 4, out_specs=VM,
        scratch_shapes=scratch(nz), compiler_params=params(), cost_estimate=cost(nx * nz * ny),
    )(flat, zlo.reshape(-1, ny), zhi.reshape(-1, ny), acc)
    out = pl.pallas_call(
        functools.partial(wall_kernel, nx, nz, ny), out_shape=shape, name="wall_sweep",
        in_specs=[pl.BlockSpec(memory_space=pltpu.SMEM), VM, VM], out_specs=VM,
        scratch_shapes=[pltpu.VMEM((6, ny + 2 * SUB, LANE), F32), pltpu.VMEM((6, ny, LANE), F32)] + scratch(ny // SUB),
        compiler_params=params(), cost_estimate=cost(nx * nz * ny),
    )(strength, flat, acc)
    return out.reshape(q.shape)


def span_tables(modes, points):
    ids = np.arange(modes)[:, None] * np.arange(points)[None, :] % modes
    angle = 2.0 * np.pi / modes * ids
    cz, sz = np.cos(angle), np.sin(angle)
    return jnp.asarray(np.concatenate([np.concatenate([cz, sz], 1), np.concatenate([-sz, cz], 1)], 0), F32).astype(BF16)


def feed_kernel(planes, parts, z_ref, rep_ref, coeff_ref, out_ref, rhs_ref, acc_ref):
    _, kc, levels, modes = coeff_ref.shape
    groups = levels // SUB
    points = z_ref.shape[1] // 2
    rows = rep_ref.shape[1]
    step = pl.program_id(1)
    prod = jnp.dot(coeff_ref[0].reshape(kc * levels, modes), z_ref[:modes], preferred_element_type=F32)
    prod += jnp.dot(coeff_ref[1].reshape(kc * levels, modes), z_ref[modes:], preferred_element_type=F32)
    prod = prod.reshape(kc, groups, SUB, 2 * points)
    for g in range(groups):
        part = prod[:, g].reshape(kc * SUB, 2 * points).astype(BF16)
        for c in range(2):
            rhs_ref[c * kc * SUB : (c + 1) * kc * SUB, g * points : (g + 1) * points] = part[:, c * points : (c + 1) * points]
    width = kc * SUB
    own = lax.broadcasted_iota(jnp.int32, (rows, SUB, width), 2) % SUB == lax.broadcasted_iota(jnp.int32, (rows, SUB, width), 1)
    left = jnp.concatenate(
        [jnp.where(own, rep_ref[c][:, None, :], 0.0).reshape(rows * SUB, width) for c in range(2)], axis=1
    ).astype(BF16)
    total = jnp.dot(left, rhs_ref[...], preferred_element_type=F32)

    @pl.when(step == 0)
    def _():
        acc_ref[...] = total

    @pl.when(step > 0)
    def _():
        acc_ref[...] += total

    @pl.when(step == pl.num_programs(1) - 1)
    def _():
        per = LANE // levels
        piece = points // parts
        for t in range(rows // per):
            tile = jnp.concatenate(
                [
                    acc_ref[f * SUB : (f + 1) * SUB, g * points : (g + 1) * points]
                    for f in range(t * per, (t + 1) * per)
                    for g in range(groups)
                ],
                axis=0,
            )
            turned = tile.T
            for s in range(parts):
                out_ref[s, t] = turned[s * piece : (s + 1) * piece]


def feed(coeff, rep, table, first, count, parts, chunk):
    _, modes_x, variables, levels, modes = coeff.shape
    points = table.shape[1] // 2
    rows = rep.shape[1]
    groups = levels // SUB
    tiles = rows * levels // LANE
    chunk = min(chunk, modes_x)
    flops = 2 * count * modes_x * levels * (2 * modes * 2 * points + rows * SUB * 2 * points)
    return pl.pallas_call(
        functools.partial(feed_kernel, rows, parts), name="feed",
        out_shape=jax.ShapeDtypeStruct((count, parts, tiles, points // parts, LANE), F32),
        grid=(count, modes_x // chunk),
        in_specs=[
            pl.BlockSpec(table.shape, lambda v, k: (0, 0)),
            pl.BlockSpec((2, rows, chunk * SUB), lambda v, k: (0, 0, k)),
            pl.BlockSpec((2, chunk, None, levels, modes), lambda v, k: (0, k, first + v, 0, 0)),
        ],
        out_specs=pl.BlockSpec((None, parts, tiles, points // parts, LANE), lambda v, k: (v, 0, 0, 0, 0)),
        scratch_shapes=[
            pltpu.VMEM((2 * chunk * SUB, groups * points), BF16),
            pltpu.VMEM((rows * SUB, groups * points), F32),
        ],
        compiler_params=pltpu.CompilerParams(vmem_limit_bytes=40 * 2**20),
        cost_estimate=pl.CostEstimate(flops=flops, bytes_accessed=2 * count * modes_x * levels * modes * 2, transcendentals=0),
    )(table, rep, coeff)


def factors(feed_plane, mode_first, modes_x, stream_points, levels):
    per = LANE // levels
    planes = feed_plane.shape[0]
    rows = -(-planes // per) * per
    padded = jnp.concatenate([feed_plane, jnp.zeros((rows - planes,), jnp.int32)])
    ids = mode_first + lax.broadcasted_iota(jnp.int32, (rows, modes_x * SUB), 1) // SUB
    angle = 2.0 * math.pi / stream_points * (padded[:, None] * ids % stream_points).astype(F32)
    rep = jnp.stack([jnp.cos(angle), -jnp.sin(angle)])
    return rep.astype(BF16).astype(F32)


def force_kernel(per, levels, offset, strength, *refs):
    targets, state, out_ref = refs[:-2], refs[-2], refs[-1]
    parts = targets[0].shape[0]
    first = pl.program_id(0) * per
    lane = lax.broadcasted_iota(jnp.int32, targets[0].shape[1:], 1)
    for v, target in enumerate(targets):
        blocks = [target[s] for s in range(parts)]
        for i in range(per):
            row = blocks[0] if i == 0 else pltpu.roll(blocks[0], (-i * levels) % LANE, 1)
            for s in range(1, parts):
                moved = blocks[s] if s == i else pltpu.roll(blocks[s], ((s - i) * levels) % LANE, 1)
                row = jnp.where(lane >= s * levels, moved, row)
            out_ref[v, i] = state[v, i] + (0.05 * strength[first + i]) * row


def force(state, targets, strength, offset, levels, planes):
    variables, nx, nz, ny = state.shape
    per = LANE // levels
    parts, tiles = targets[0].shape[:2]
    steps = -(-min(planes, nx) // per)

    def tile(t, offset, strength):
        return (0, jnp.minimum(t + offset[0], tiles - 1), 0, 0)

    def plane(t, offset, strength):
        return (0, t, 0, 0)

    blocks = [pl.BlockSpec((parts, None, nz, LANE), tile)] * variables
    cells = pl.BlockSpec((variables, per, nz, ny), plane)
    return pl.pallas_call(
        functools.partial(force_kernel, per, levels), name="force",
        out_shape=jax.ShapeDtypeStruct(state.shape, F32),
        grid_spec=pltpu.PrefetchScalarGridSpec(
            num_scalar_prefetch=2, grid=(steps,), in_specs=blocks + [cells], out_specs=cells),
        input_output_aliases={2 + variables: 0},
        compiler_params=pltpu.CompilerParams(vmem_limit_bytes=20 * 2**20),
    )(offset, strength, *targets, state)


GX = ("gh", "gl")


def local(state, coeff, feed_plane):
    high, pair, parts = lax.axis_size("gh"), lax.axis_size("gl"), lax.axis_size("gz")
    gx = high * pair
    me = lax.axis_index("gh") * pair + lax.axis_index("gl")
    variables, nx, nz, ny = state.shape
    _, modes_x, _, levels, modes = coeff.shape
    planes = feed_plane.shape[0]

    ring = [(i, (i + 1) % parts) for i in range(parts)]
    line = [(i, i + 1) for i in range(gx - 1)]
    zside = [jnp.transpose(state[:, :, k], (0, 2, 1, 3)) for k in (slice(nz - 3, nz), slice(0, 3))]
    xlo = lax.ppermute(state[:, nx - 3 :], GX, line)
    xhi = lax.ppermute(state[:, :3], GX, [(j, i) for i, j in line])
    zlo = lax.ppermute(zside[0], "gz", ring)
    zhi = lax.ppermute(zside[1], "gz", [(j, i) for i, j in ring])

    rep = factors(feed_plane, me * modes_x, modes_x, 2 * modes_x * gx, levels)
    table = span_tables(modes, nz * parts)
    targets = []
    for first in range(0, variables, pair):
        part = feed(coeff, rep, table, first, pair, parts, 32)
        part = lax.all_to_all(part.reshape(-1, *part.shape[2:]), ("gl", "gz"), split_axis=0, concat_axis=0, tiled=True)
        part = part.reshape(pair, parts, *part.shape[1:]).sum(0)
        stride = 1
        while stride < high:
            hops = [(i, i - stride) for i in range(stride, high, 2 * stride)]
            part = part + lax.ppermute(part, "gh", hops)
            stride *= 2
        owned = [part] + [lax.ppermute(part, GX, [(i, 0)]) for i in range(1, pair)]
        for other in range(1, -(-planes // nx)):
            owned = [jnp.where(me == other, lax.ppermute(t, GX, [(0, other)]), t) for t in owned]
        targets += owned

    edges = jnp.stack([me == 0, me == gx - 1]).astype(jnp.int32)
    plane = me * nx + jnp.arange(nx, dtype=jnp.int32)
    strength = jnp.where(plane < planes, 2.0 * jnp.square(1.0 - plane.astype(F32) / planes), 0.0)
    new = rhs(state, xlo, xhi, zlo, zhi, edges, strength)
    offset = jnp.reshape(me * nx // (LANE // levels), (1,))
    return force(new, targets, strength, offset, levels, planes)


def solution(mesh):
    gx, gz = mesh.devices.shape
    pair = 2 if gx % 2 == 0 else 1
    split = Mesh(mesh.devices.reshape(gx // pair, pair, gz), ("gh", "gl", "gz"))
    cells = P(None, GX, "gz", None)
    return jax.shard_map(
        local, mesh=split, in_specs=(cells, P(None, GX, None, "gz", None), P()), out_specs=cells, check_vma=False
    )
```

time: 308 us -> 141 us (0.46)
  local copies, waits for them, and re-layouts: 111 us -> 3.58 us
  other arithmetic: 95.3 us -> 4.15 us
  Pallas kernels: 0 us -> 77.3 us
  matrix products: 45.1 us -> 0 us
  starting transfers between devices: 10.5 us -> 31.9 us
  between operations: 14.4 us -> 0.26 us
  waiting for transfers between devices: 29.8 us -> 22.5 us
    pallas_call x0 -> x7, Pallas kernels: none -> 77.3 us  [the longest x3 39.3 us: feed(): pl.pallas_call(functools.partial(feed_kernel, rows, parts), name='feed',...]
    dot_general x1 -> x0, local copies, waits for them, and re-layouts: 48.8 us -> none  [local(): jnp.dot(coeff_rows, span_table, preferred_element_type=jnp.float32)]
    dot_general x2 -> x0, matrix products: 45.1 us -> none  [the longest x1 37.8 us: local(): jnp.dot(coeff_rows, span_table, preferred_element_type=jnp.float32)]
    add x8 -> x6, other arithmetic: 48 us -> 2.95 us  [local(): part = part + lax.ppermute(part, 'gh', hops)]
    another operation x6 -> x1, other arithmetic: 25.9 us -> 1 us
    all_gather x1 -> x0, waiting for transfers between devices: 23.9 us -> none  [local(): collected = lax.all_gather(relaid, 'gx', axis=0, tiled=True)]
    another operation x4 -> x0, local copies, waits for them, and re-layouts: 22.6 us -> none
    ppermute x4 -> x13, waiting for transfers between devices: 0.01 us -> 17.7 us  [the longest x6 13.2 us: local(): part = part + lax.ppermute(part, 'gh', hops)]
  transfers between devices with their start and end apart: 7 -> 16, of which waited for: 3 -> 4; matrix products, arithmetic and copies ran while one was open for 77% -> 4% of each run, Pallas kernels for 0% -> 43%
where the time goes in v1:
time: 141 us; the launch traced here: 140 us
  Pallas kernels  77.3 us (55%)
  starting transfers between devices  31.9 us (23%)
  waiting for transfers between devices  22.5 us (16%)
  other arithmetic  4.15 us (3%)
  local copies, waits for them, and re-layouts  3.58 us (3%)
    pallas_call x3, Pallas kernels, feed(): pl.pallas_call(functools.partial(feed_kernel, rows, parts), name='feed',...  39.3 us
    pallas_call x1, Pallas kernels, rhs(): pl.pallas_call(functools.partial(wall_kernel, nx, nz, ny), out_shape=shap...  15 us
    all_to_all x3, starting transfers between devices, local(): lax.all_to_all(part.reshape(-1, *part.shape[2:]), ('gl', 'gz'), split_axi...  13.7 us
    ppermute x6, waiting for transfers between devices, local(): part = part + lax.ppermute(part, 'gh', hops)  13.2 us
    pallas_call x1, Pallas kernels, rhs(): pl.pallas_call(functools.partial(span_kernel, nx, nz), out_shape=shape, n...  9.96 us
    pallas_call x1, Pallas kernels, rhs(): pl.pallas_call(functools.partial(stream_kernel, nx, nz), out_shape=shape,...  8.75 us
    ppermute x6, starting transfers between devices, local(): part = part + lax.ppermute(part, 'gh', hops)  7.75 us
    all_to_all x3, waiting for transfers between devices, local(): lax.all_to_all(part.reshape(-1, *part.shape[2:]), ('gl', 'gz'), split_axi...  4.82 us
  transfers between devices with their start and end apart: 16, of which 4 were waited for; matrix products, arithmetic and copies ran while one was open for 4% of the time, Pallas kernels for 43%

profile of v1, /device:TPU:0, one launch (start us, length us, event | category | flops | bytes accessed | tf_op | source)
XLA Modules:
  0.0 139.6 jit_solution(4634991003401628387)
XLA Ops:
  0.0 1.0 cosine_convert_fusion
  1.1 1.0 copy-done.1
  2.1 13.1 %feed.5 = f32[2,4,3,32,128]{4,3,2,1,0:T(8,128)} custom-call(bf16[1024,256]{1,0:T(8,128)(2,1)S(1)} %copy-done.1, f32[2,12,1024]{2,1,0:T(8,128)S(1)} %maximum_convert_fusion.rep_ref, bf16[2,128,6,32,512]{4,3,2,1,0:T(8,128)(2,1)} %coeff_ref.5), custom_call_target="tpu_custom_call" | custom-call | flops 4697620480 | bytes 16777216 | tf_op jit(solution)/shard_map/feed/pallas_call | solution.py:298
  15.2 5.2 %all-to-all-start.2 = ((f32[8,3,32,128]{3,2,1,0:T(8,128)}), f32[8,3,32,128]{3,2,1,0:T(8,128)S(1)}, u32[]{:S(2)}, u32[]{:S(2)}) async-start(f32[8,3,32,128]{3,2,1,0:T(8,128)} %bitcast.5), calls=%async_computation.2 | async-start | bytes 786432 | tf_op jit(solution)/shard_map/all_to_all | solution.py:391
  20.4 13.1 %feed.4 = f32[2,4,3,32,128]{4,3,2,1,0:T(8,128)} custom-call(bf16[1024,256]{1,0:T(8,128)(2,1)S(1)} %copy-done.2, f32[2,12,1024]{2,1,0:T(8,128)S(1)} %maximum_convert_fusion.rep_ref, bf16[2,128,6,32,512]{4,3,2,1,0:T(8,128)(2,1)} %coeff_ref.5), custom_call_target="tpu_custom_call" | custom-call | flops 4697620480 | bytes 16777216 | tf_op jit(solution)/shard_map/feed/pallas_call | solution.py:298
  33.5 4.2 %all-to-all-start.1 = ((f32[8,3,32,128]{3,2,1,0:T(8,128)}), f32[8,3,32,128]{3,2,1,0:T(8,128)S(1)}, u32[]{:S(2)}, u32[]{:S(2)}) async-start(f32[8,3,32,128]{3,2,1,0:T(8,128)} %bitcast.3), calls=%async_computation.1 | async-start | bytes 786432 | tf_op jit(solution)/shard_map/all_to_all | solution.py:391
  37.7 13.1 %feed.3 = f32[2,4,3,32,128]{4,3,2,1,0:T(8,128)} custom-call(bf16[1024,256]{1,0:T(8,128)(2,1)S(1)} %copy-done.2, f32[2,12,1024]{2,1,0:T(8,128)S(1)} %maximum_convert_fusion.rep_ref, bf16[2,128,6,32,512]{4,3,2,1,0:T(8,128)(2,1)} %coeff_ref.5), custom_call_target="tpu_custom_call" | custom-call | flops 4697620480 | bytes 16777216 | tf_op jit(solution)/shard_map/feed/pallas_call | solution.py:298
  50.8 4.3 %all-to-all-start = ((f32[8,3,32,128]{3,2,1,0:T(8,128)}), f32[8,3,32,128]{3,2,1,0:T(8,128)S(1)}, u32[]{:S(2)}, u32[]{:S(2)}) async-start(f32[8,3,32,128]{3,2,1,0:T(8,128)} %bitcast.1), calls=%async_computation | async-start | bytes 786432 | tf_op jit(solution)/shard_map/all_to_all | solution.py:391
  55.2 1.3 collective-permute-start.6
  56.5 1.3 collective-permute-start.3
  57.8 4.8 %all-to-all-done = f32[8,3,32,128]{3,2,1,0:T(8,128)S(1)} async-done(((f32[8,3,32,128]{3,2,1,0:T(8,128)}), f32[8,3,32,128]{3,2,1,0:T(8,128)S(1)}, u32[]{:S(2)}, u32[]{:S(2)}) %all-to-all-start) | async-done | bytes 393248 | tf_op jit(solution)/shard_map/all_to_all | solution.py:391
  62.6 1.3 collective-permute-start
  65.4 1.3 collective-permute-start.7
  66.7 2.2 %collective-permute-done.3 = f32[4,3,32,128]{3,2,1,0:T(8,128)S(1)} collective-permute-done((f32[4,3,32,128]{3,2,1,0:T(8,128)S(1)}, f32[4,3,32,128]{3,2,1,0:T(8,128)S(1)}, u32[]{:S(2)}, u32[]{:S(2)}) %collective-permute-start.3) | collective-permute-done | bytes 196640 | tf_op jit(solution)/shard_map/ppermute | solution.py:396
  69.0 1.3 collective-permute-start.4
  70.3 10.9 %collective-permute-done = f32[4,3,32,128]{3,2,1,0:T(8,128)S(1)} collective-permute-done((f32[4,3,32,128]{3,2,1,0:T(8,128)S(1)}, f32[4,3,32,128]{3,2,1,0:T(8,128)S(1)}, u32[]{:S(2)}, u32[]{:S(2)}) %collective-permute-start) | collective-permute-done | bytes 196640 | tf_op jit(solution)/shard_map/ppermute | solution.py:396
  81.2 1.3 collective-permute-start.1
  82.5 0.8 fusion.6
  83.4 1.3 collective-permute-start.12
  84.7 4.6 %collective-permute-start.11 = (f32[6,3,32,128]{3,2,1,0:T(8,128)}, f32[6,3,32,128]{3,2,1,0:T(8,128)S(1)}, u32[]{:S(2)}, u32[]{:S(2)}) collective-permute-start(f32[6,3,32,128]{3,2,1,0:T(8,128)} %get-tuple-element.6), channel_id=1, source_target_pairs={{0,4},{4,8},{8,12},{12,16},{16,20},{20,24},{24,28},{1,5},{5,9},{9,... | collective-permute-start | bytes 884744 | tf_op jit(solution)/shard_map/ppermute | solution.py:381
  89.3 1.0 add.75.refs_4_
  90.2 1.0 add.73.refs_2_
  91.2 1.3 collective-permute-start.8
  92.5 1.0 add.71.refs_0_
  93.5 1.3 collective-permute-start.5
  94.8 1.3 collective-permute-start.2
  96.2 0.9 copy.6
  97.2 4.5 %collective-permute-done.11 = f32[6,3,32,128]{3,2,1,0:T(8,128)S(1)} collective-permute-done((f32[6,3,32,128]{3,2,1,0:T(8,128)}, f32[6,3,32,128]{3,2,1,0:T(8,128)S(1)}, u32[]{:S(2)}, u32[]{:S(2)}) %collective-permute-start.11) | collective-permute-done | bytes 294944 | tf_op jit(solution)/shard_map/ppermute | solution.py:381
  101.7 8.7 %stream_sweep.1.acc_in = f32[3072,128]{1,0:T(8,128)S(1)} custom-call(s32[2]{0:T(128)S(1)} %add_convert_fusion.flags, f32[3072,128]{1,0:T(8,128)S(1)} %bitcast.19, f32[576,128]{1,0:T(8,128)S(1)} %bitcast.25, f32[576,128]{1,0:T(8,128)S(1)} %bitcast.24), custom_call_target="tpu_custom_call" | custom-call | flops 262144000 | bytes 3932160 | tf_op jit(solution)/shard_map/stream_sweep/pallas_call | solution.py:218
  110.4 10.0 %span_sweep.1.acc_in = f32[3072,128]{1,0:T(8,128)S(1)} custom-call(f32[3072,128]{1,0:T(8,128)S(1)} %bitcast.20, f32[288,128]{1,0:T(8,128)S(1)} %bitcast.23, f32[288,128]{1,0:T(8,128)S(1)} %bitcast.22, f32[3072,128]{1,0:T(8,128)S(1)} %stream_sweep.1.acc_in), custom_call_target="tpu_custom_call" | custom-call | flops 262144000 | bytes 3932160 | tf_op jit(solution)/shard_map/span_sweep/pallas_call | solution.py:223
  120.4 15.0 %wall_sweep.1 = f32[3072,128]{1,0:T(8,128)} custom-call(f32[16]{0:T(128)S(1)} %compare_select_fusion.strength, f32[3072,128]{1,0:T(8,128)S(1)} %bitcast.21, f32[3072,128]{1,0:T(8,128)S(1)} %span_sweep.1.acc_in), custom_call_target="tpu_custom_call" | custom-call | flops 262144000 | bytes 3932160 | tf_op jit(solution)/shard_map/wall_sweep/pallas_call | solution.py:228
  135.3 4.3 %force.1 = f32[6,16,32,128]{3,2,1,0:T(8,128)} custom-call(s32[1]{0:T(128)} %bitcast.offset, f32[16]{0:T(128)S(1)} %compare_select_fusion.strength, f32[4,3,32,128]{3,2,1,0:T(8,128)S(1)} %add.71.refs_0_, f32[4,3,32,128]{3,2,1,0:T(8,128)S(1)} %collective-permute-done.2.refs_1_, f32[4,3,32,128]{3,2,1,0:T(8,128)S(1)} %add.73.refs_2_, ...), custom_call_target="tpu_custom_call", output_to_operand_aliasing={{}: (8, {})} | custom-call | tf_op jit(solution)/shard_map/force/pallas_call | solution.py:357
  (32 shorter events, 1.8 us)
Async XLA Ops:
  1.0 1.0 copy-start.1
  2.1 18.3 %copy-start.2 = (bf16[1024,256]{1,0:T(8,128)(2,1)S(1)}, bf16[1024,256]{1,0:T(8,128)(2,1)}, u32[]{:S(2)}) copy-start(bf16[1024,256]{1,0:T(8,128)(2,1)} %constant.79.z_ref) | copy-start | bytes 1572868
  15.2 18.3 %all-to-all-start.2 = ((f32[8,3,32,128]{3,2,1,0:T(8,128)}), f32[8,3,32,128]{3,2,1,0:T(8,128)S(1)}, u32[]{:S(2)}, u32[]{:S(2)}) async-start(f32[8,3,32,128]{3,2,1,0:T(8,128)} %bitcast.5), calls=%async_computation.2 | async-start | bytes 786432 | tf_op jit(solution)/shard_map/all_to_all | solution.py:391
  33.5 17.3 %all-to-all-start.1 = ((f32[8,3,32,128]{3,2,1,0:T(8,128)}), f32[8,3,32,128]{3,2,1,0:T(8,128)S(1)}, u32[]{:S(2)}, u32[]{:S(2)}) async-start(f32[8,3,32,128]{3,2,1,0:T(8,128)} %bitcast.3), calls=%async_computation.1 | async-start | bytes 786432 | tf_op jit(solution)/shard_map/all_to_all | solution.py:391
  50.8 13.1 %copy-start = (f32[6,16,32,128]{3,2,1,0:T(8,128)S(1)}, f32[6,16,32,128]{3,2,1,0:T(8,128)}, u32[]{:S(2)}) copy-start(f32[6,16,32,128]{3,2,1,0:T(8,128)} %param.4) | copy-start | bytes 4718596
  50.8 11.8 %all-to-all-start = ((f32[8,3,32,128]{3,2,1,0:T(8,128)}), f32[8,3,32,128]{3,2,1,0:T(8,128)S(1)}, u32[]{:S(2)}, u32[]{:S(2)}) async-start(f32[8,3,32,128]{3,2,1,0:T(8,128)} %bitcast.1), calls=%async_computation | async-start | bytes 786432 | tf_op jit(solution)/shard_map/all_to_all | solution.py:391
  55.2 10.3 %collective-permute-start.6 = (f32[4,3,32,128]{3,2,1,0:T(8,128)S(1)}, f32[4,3,32,128]{3,2,1,0:T(8,128)S(1)}, u32[]{:S(2)}, u32[]{:S(2)}) collective-permute-start(f32[4,3,32,128]{3,2,1,0:T(8,128)S(1)} %reduce_sum.29), channel_id=1, source_target_pairs={{8,0},{24,16},{9,1},{25,17},{10,2},{26,18},{11,3},{27,19},{12,4},{... | collective-permute-start | bytes 589832 | tf_op jit(solution)/shard_map/ppermute | solution.py:396
  56.5 12.5 %collective-permute-start.3 = (f32[4,3,32,128]{3,2,1,0:T(8,128)S(1)}, f32[4,3,32,128]{3,2,1,0:T(8,128)S(1)}, u32[]{:S(2)}, u32[]{:S(2)}) collective-permute-start(f32[4,3,32,128]{3,2,1,0:T(8,128)S(1)} %reduce_sum.28), channel_id=1, source_target_pairs={{8,0},{24,16},{9,1},{25,17},{10,2},{26,18},{11,3},{27,19},{12,4},{... | collective-permute-start | bytes 589832 | tf_op jit(solution)/shard_map/ppermute | solution.py:396
  62.6 18.6 %collective-permute-start = (f32[4,3,32,128]{3,2,1,0:T(8,128)S(1)}, f32[4,3,32,128]{3,2,1,0:T(8,128)S(1)}, u32[]{:S(2)}, u32[]{:S(2)}) collective-permute-start(f32[4,3,32,128]{3,2,1,0:T(8,128)S(1)} %reduce_sum.27), channel_id=1, source_target_pairs={{8,0},{24,16},{9,1},{25,17},{10,2},{26,18},{11,3},{27,19},{12,4},{... | collective-permute-start | bytes 589832 | tf_op jit(solution)/shard_map/ppermute | solution.py:396
  64.7 28.8 %collective-permute-start.10 = (f32[6,3,16,128]{3,1,2,0:T(4,128)}, f32[6,3,16,128]{3,1,2,0:T(4,128)S(1)}, u32[]{:S(2)}, u32[]{:S(2)}) collective-permute-start(f32[6,3,16,128]{3,1,2,0:T(4,128)} %get-tuple-element.7), channel_id=1, source_target_pairs={{1,0},{2,1},{3,2},{0,3},{5,4},{6,5},{7,6},{4,7},{9,8},{10,9},{11,1... | collective-permute-start | bytes 442376 | tf_op jit(solution)/shard_map/ppermute | solution.py:384
  65.4 29.4 %collective-permute-start.9 = (f32[6,3,16,128]{3,1,2,0:T(4,128)S(1)}, f32[6,3,16,128]{3,1,2,0:T(4,128)}, u32[]{:S(2)}, u32[]{:S(2)}) collective-permute-start(f32[6,3,16,128]{3,1,2,0:T(4,128)S(1)} %get-tuple-element.8), channel_id=1, source_target_pairs={{0,1},{1,2},{2,3},{3,0},{4,5},{5,6},{6,7},{7,4},{8,9},{9,10},{10,1... | collective-permute-start | bytes 442376 | tf_op jit(solution)/shard_map/ppermute | solution.py:383
  65.4 18.0 %collective-permute-start.7 = (f32[4,3,32,128]{3,2,1,0:T(8,128)S(1)}, f32[4,3,32,128]{3,2,1,0:T(8,128)}, u32[]{:S(2)}, u32[]{:S(2)}) collective-permute-start(f32[4,3,32,128]{3,2,1,0:T(8,128)S(1)} %add.74), channel_id=1, source_target_pairs={{16,0},{17,1},{18,2},{19,3},{20,4},{21,5},{22,6},{23,7}} | collective-permute-start | bytes 589832 | tf_op jit(solution)/shard_map/ppermute | solution.py:396
  69.0 15.7 %collective-permute-start.4 = (f32[4,3,32,128]{3,2,1,0:T(8,128)S(1)}, f32[4,3,32,128]{3,2,1,0:T(8,128)}, u32[]{:S(2)}, u32[]{:S(2)}) collective-permute-start(f32[4,3,32,128]{3,2,1,0:T(8,128)S(1)} %add.72), channel_id=1, source_target_pairs={{16,0},{17,1},{18,2},{19,3},{20,4},{21,5},{22,6},{23,7}} | collective-permute-start | bytes 589832 | tf_op jit(solution)/shard_map/ppermute | solution.py:396
  81.2 9.9 %collective-permute-start.1 = (f32[4,3,32,128]{3,2,1,0:T(8,128)S(1)}, f32[4,3,32,128]{3,2,1,0:T(8,128)}, u32[]{:S(2)}, u32[]{:S(2)}) collective-permute-start(f32[4,3,32,128]{3,2,1,0:T(8,128)S(1)} %add.70), channel_id=1, source_target_pairs={{16,0},{17,1},{18,2},{19,3},{20,4},{21,5},{22,6},{23,7}} | collective-permute-start | bytes 589832 | tf_op jit(solution)/shard_map/ppermute | solution.py:396
  83.4 13.7 %collective-permute-start.12 = (f32[6,3,32,128]{3,2,1,0:T(8,128)}, f32[6,3,32,128]{3,2,1,0:T(8,128)S(1)}, u32[]{:S(2)}, u32[]{:S(2)}) collective-permute-start(f32[6,3,32,128]{3,2,1,0:T(8,128)} %get-tuple-element.5), channel_id=1, source_target_pairs={{4,0},{8,4},{12,8},{16,12},{20,16},{24,20},{28,24},{5,1},{9,5},{13... | collective-permute-start | bytes 884744 | tf_op jit(solution)/shard_map/ppermute | solution.py:382
  84.7 16.9 %collective-permute-start.11 = (f32[6,3,32,128]{3,2,1,0:T(8,128)}, f32[6,3,32,128]{3,2,1,0:T(8,128)S(1)}, u32[]{:S(2)}, u32[]{:S(2)}) collective-permute-start(f32[6,3,32,128]{3,2,1,0:T(8,128)} %get-tuple-element.6), channel_id=1, source_target_pairs={{0,4},{4,8},{8,12},{12,16},{16,20},{20,24},{24,28},{1,5},{5,9},{9,... | collective-permute-start | bytes 884744 | tf_op jit(solution)/shard_map/ppermute | solution.py:381
  91.2 44.1 %collective-permute-start.8 = (f32[4,3,32,128]{3,2,1,0:T(8,128)S(1)}, f32[4,3,32,128]{3,2,1,0:T(8,128)S(1)}, u32[]{:S(2)}, u32[]{:S(2)}) collective-permute-start(f32[4,3,32,128]{3,2,1,0:T(8,128)S(1)} %add.75.refs_4_), channel_id=1, source_target_pairs={{4,0},{5,1},{6,2},{7,3}} | collective-permute-start | bytes 589832 | tf_op jit(solution)/shard_map/ppermute | solution.py:398
  93.5 41.9 %collective-permute-start.5 = (f32[4,3,32,128]{3,2,1,0:T(8,128)S(1)}, f32[4,3,32,128]{3,2,1,0:T(8,128)S(1)}, u32[]{:S(2)}, u32[]{:S(2)}) collective-permute-start(f32[4,3,32,128]{3,2,1,0:T(8,128)S(1)} %add.73.refs_2_), channel_id=1, source_target_pairs={{4,0},{5,1},{6,2},{7,3}} | collective-permute-start | bytes 589832 | tf_op jit(solution)/shard_map/ppermute | solution.py:398
  94.8 40.6 %collective-permute-start.2 = (f32[4,3,32,128]{3,2,1,0:T(8,128)S(1)}, f32[4,3,32,128]{3,2,1,0:T(8,128)S(1)}, u32[]{:S(2)}, u32[]{:S(2)}) collective-permute-start(f32[4,3,32,128]{3,2,1,0:T(8,128)S(1)} %add.71.refs_0_), channel_id=1, source_target_pairs={{4,0},{5,1},{6,2},{7,3}} | collective-permute-start | bytes 589832 | tf_op jit(solution)/shard_map/ppermute | solution.py:398

commit v2 on v1

v2 whole, which is shorter than its diff:
```python
import functools
import math

import jax
import jax.numpy as jnp
import numpy as np
from jax import lax
from jax.experimental import pallas as pl
from jax.experimental.pallas import tpu as pltpu
from jax.sharding import Mesh, PartitionSpec as P

SUB, LANE = 8, 128
EPS = 3e-6
F32, BF16 = jnp.float32, jnp.bfloat16


U1, U2 = 16, 4
TALL = 64


def cell_flux(q, comp):
    r, m1, m2, m3, e, ev = q
    rinv = 1.0 / r
    kin = 0.5 * (m1 * m1 + m2 * m2 + m3 * m3) * rinv
    p = 0.4 * (e - kin - ev)
    un = q[comp] * rinv
    c = jnp.sqrt(1.4 * p * rinv)
    flux = [v * un for v in q]
    flux[comp] = flux[comp] + p
    flux[4] = (e + p) * un
    return flux, jnp.abs(un) + c


def correction(gmm, gm, gp, gpp):
    u0 = gmm - 1.375 * gm
    u1 = gm - 0.625 * gp
    u1r = gp - 0.625 * gm
    u2 = gpp - 1.375 * gp
    tm = (0.609375 * gm) * gm + EPS
    tp = (0.609375 * gp) * gp + EPS
    s0 = u0 * u0 + tm
    s1 = u1 * u1 + tp
    s2 = u2 * u2 + tp
    left = u0 + u1r
    right = u2 + u1
    p12 = s1 * s2
    p01 = s0 * s1
    p02 = s0 * s2
    w0 = p12 * p12
    w2 = 3.0 * (p01 * p01)
    w1 = 6.0 * (p02 * p02)
    num = (w0 + w0) * left + w2 * right
    den = w0 + w1 + w2
    return num * pl.reciprocal(den, approx=True)


def sweep(comp, cells, low, mid, high, put, gf_ref, gq_ref, mx_ref):
    def step(j, carry, q):
        flux, s = cell_flux(q, comp)
        pf, pq, ps = carry
        for v in range(6):
            gf_ref[v, j - 1] = flux[v] - pf[v]
            gq_ref[v, j - 1] = q[v] - pq[v]
        mx_ref[j - 1] = jnp.maximum(s, ps)
        return flux, q, s

    q0 = low(0)
    f0, s0 = cell_flux(q0, comp)
    carry = (f0, q0, s0)
    for j in (1, 2):
        carry = step(j, carry, low(j))
    carry = lax.fori_loop(0, cells, lambda j, c: step(j + 3, c, mid(j)), carry, unroll=U1)
    for j in range(3):
        carry = step(cells + 3 + j, carry, high(j))

    def face(f):
        a = jnp.maximum(jnp.maximum(mx_ref[f], mx_ref[f + 2]), mx_ref[f + 4])
        out = []
        for v in range(6):
            g = [gf_ref[v, f + k] for k in range(5)]
            h = [a * gq_ref[v, f + k] for k in range(5)]
            up = correction(g[0] + h[0], g[1] + h[1], g[2] + h[2], g[3] + h[3])
            down = correction(g[4] - h[4], g[3] - h[3], g[2] - h[2], g[1] - h[1])
            out.append((h[1] + h[3] - (h[2] + h[2])) + (down - up))
        return out

    def body(f, before):
        after = face(f)
        total = []
        for v in range(6):
            g = [gf_ref[v, f + k] for k in range(4)]
            total.append(7.0 * (g[2] + g[1]) - (g[3] + g[0]) + (after[v] - before[v]))
        put(f - 1, total)
        return after

    lax.fori_loop(1, cells + 1, body, face(0), unroll=U2)


def scratch(cells):
    return [
        pltpu.VMEM((6, cells + 5, SUB, LANE), F32),
        pltpu.VMEM((6, cells + 5, SUB, LANE), F32),
        pltpu.VMEM((cells + 5, SUB, LANE), F32),
    ]


def stream_kernel(flags, q_ref, lo_ref, hi_ref, acc_ref, gf, gq, mx):
    nx = q_ref.shape[1]

    def mid(j):
        return [q_ref[v, j] for v in range(6)]

    def side(ref, flag, edge):
        def load(j):
            return [jnp.where(flag == 1, e, ref[v, j]) for v, e in enumerate(mid(edge))]
        return load

    def put(c, total):
        for v in range(6):
            acc_ref[v, c] = total[v]

    sweep(1, nx, side(lo_ref, flags[0], 0), mid, side(hi_ref, flags[1], nx - 1), put, gf, gq, mx)


def span_kernel(nz, q_ref, lo_ref, hi_ref, acc_in, acc_ref, gf, gq, mx):
    def rows(j):
        return pl.ds(j, SUB, stride=nz)

    def mid(j):
        return [q_ref[v, rows(j), :] for v in range(6)]

    def side(ref):
        return lambda j: [ref[j, v] for v in range(6)]

    def put(c, total):
        for v in range(6):
            acc_ref[v, rows(c), :] = acc_in[v, rows(c), :] + total[v]

    sweep(3, nz, side(lo_ref), mid, side(hi_ref), put, gf, gq, mx)


def wall_kernel(nz, strength, q_ref, acc_in, out_ref, yq, yt, gf, gq, mx):
    ny = q_ref.shape[2]
    seg = ny // SUB
    for v in range(6):
        yq[v, SUB : SUB + ny] = q_ref[v].T
    q = [yq[v, SUB : 2 * SUB] for v in range(6)]
    rinv = 1.0 / q[0]
    temp = 0.4 * (q[4] - 0.5 * (q[1] * q[1] + q[2] * q[2] + q[3] * q[3]) * rinv - q[5]) * rinv
    ghost = [q[0], -q[1], -q[2], -q[3], q[4] - 2.5 * q[0] * (temp - 0.36 / temp), q[5]]
    for v in range(6):
        top = yq[v, SUB + ny - 1 : SUB + ny]
        for j in range(3):
            yq[v, SUB - 1 - j : SUB - j] = ghost[v][j : j + 1]
            yq[v, SUB + ny + j : SUB + ny + j + 1] = top

    def load(j):
        return [yq[v, pl.ds(SUB + j, SUB, stride=seg), :] for v in range(6)]

    def put(c, total):
        for v in range(6):
            yt[v, pl.ds(c, SUB, stride=seg), :] = total[v]

    sweep(2, seg, lambda j: load(j - 3), load, lambda j: load(seg + j), put, gf, gq, mx)

    for v in range(6):
        yt[v] = yt[v].T

    @pl.loop(0, LANE // TALL)
    def _(i):
        o = pl.multiple_of(i * TALL, TALL)
        rows = pl.ds(o, TALL)
        q = [q_ref[v, rows, :] for v in range(6)]
        rinv = 1.0 / q[0]
        p = 0.4 * (q[4] - 0.5 * (q[1] * q[1] + q[2] * q[2] + q[3] * q[3]) * rinv - q[5])
        temp = p * rinv
        share = 2.0 / (jnp.exp(2.0 / temp) - 1.0)
        lag = jnp.exp(1.5 * (jnp.exp(-jnp.log(temp) / 3.0) - 1.0))
        relax = (q[0] * share - q[5]) * (2.0 * p) / lag
        pull = jnp.zeros((TALL, ny), F32)
        for k in range(TALL // nz):
            pull = jnp.where(lax.broadcasted_iota(jnp.int32, (TALL, ny), 0) >= k * nz, strength[(pl.program_id(0) * LANE + o) // nz + k], pull)
        for v in range(6):
            rate = (acc_in[v, rows, :] + yt[v, rows, :]) * (-1.0 / 12.0)
            if v == 5:
                rate = rate + relax
            out_ref[v, rows, :] = q[v] + 0.05 * (rate - pull * q[v])


def far(x):
    return pltpu.with_memory_space_constraint(x, pltpu.HBM)


def call(kernel, name, q, grid, in_specs, out_spec, shapes):
    return pl.pallas_call(
        kernel, out_shape=pltpu.HBM(q.shape, F32), name=name, grid=(grid,), in_specs=in_specs, out_specs=out_spec,
        scratch_shapes=shapes, compiler_params=pltpu.CompilerParams(vmem_limit_bytes=16 * 2**20),
        cost_estimate=pl.CostEstimate(flops=q.size * 700, bytes_accessed=q.size * 8, transcendentals=q.size * 2),
    )


SCALARS = pl.BlockSpec(memory_space=pltpu.SMEM)


def stream_sweep(q, xlo, xhi, edges):
    _, nx, nz, ny = q.shape
    cells = pl.BlockSpec((6, nx, SUB, ny), lambda t: (0, 0, t, 0))
    side = pl.BlockSpec((6, 3, SUB, ny), lambda t: (0, 0, t, 0))
    return call(stream_kernel, "stream_sweep", q, nz // SUB, [SCALARS, cells, side, side], cells, scratch(nx))(
        edges, far(q), xlo, xhi)


def span_sweep(q, zlo, zhi, acc):
    _, nx, nz, ny = q.shape
    flat = q.reshape(6, nx * nz, ny)
    cells = pl.BlockSpec((6, SUB * nz, ny), lambda t: (0, t, 0))
    side = pl.BlockSpec((3, 6, SUB, ny), lambda t: (0, 0, t, 0))
    return call(functools.partial(span_kernel, nz), "span_sweep", flat, nx // SUB, [cells, side, side, cells], cells, scratch(nz))(
        far(flat), zlo, zhi, far(acc.reshape(flat.shape))).reshape(q.shape)


def wall_sweep(q, acc, strength):
    _, nx, nz, ny = q.shape
    flat = q.reshape(6, nx * nz, ny)
    cells = pl.BlockSpec((6, LANE, ny), lambda t: (0, t, 0))
    shapes = [pltpu.VMEM((6, ny + 2 * SUB, LANE), F32), pltpu.VMEM((6, ny, LANE), F32)] + scratch(ny // SUB)
    return call(functools.partial(wall_kernel, nz), "wall_sweep", flat, nx * nz // LANE, [SCALARS, cells, cells], cells, shapes)(
        strength, far(flat), far(acc.reshape(flat.shape))).reshape(q.shape)


def span_tables(modes, points):
    ids = np.arange(modes)[:, None] * np.arange(points)[None, :] % modes
    angle = 2.0 * np.pi / modes * ids
    cz, sz = np.cos(angle), np.sin(angle)
    return jnp.asarray(np.concatenate([np.concatenate([cz, sz], 1), np.concatenate([-sz, cz], 1)], 0), F32).astype(BF16)


def feed_kernel(first, count, chunk, depth, rep_ref, z_ref, coeff_ref, out_ref, buf, left_ref, rhs_ref, acc_ref, sems):
    _, modes_x, _, levels, modes = coeff_ref.shape
    groups = levels // SUB
    points = z_ref.shape[1] // 2
    rows = rep_ref.shape[1]
    steps = modes_x // chunk
    total = count * steps
    width = chunk * SUB
    sub = min(8, chunk)

    def copies(n, slot):
        k, v = lax.rem(n, steps) * chunk, first + lax.div(n, steps)
        return [
            pltpu.make_async_copy(coeff_ref.at[c, pl.ds(k, chunk), v], buf.at[slot, c], sems.at[slot, c]) for c in range(2)
        ]

    for n in range(min(depth - 1, total)):
        for copy in copies(n, n):
            copy.start()

    own = lax.broadcasted_iota(jnp.int32, (rows, SUB, width), 2) % SUB == lax.broadcasted_iota(
        jnp.int32, (rows, SUB, width), 1
    )
    for k in range(steps):
        for c in range(2):
            spread = jnp.where(own, rep_ref[c, :, k * width : (k + 1) * width][:, None, :], 0.0)
            left_ref[k, :, c * width : (c + 1) * width] = spread.reshape(rows * SUB, width).astype(BF16)

    def body(n, _):
        slot = lax.rem(n, depth)
        ahead = n + depth - 1

        @pl.when(ahead < total)
        def _():
            for copy in copies(ahead, lax.rem(ahead, depth)):
                copy.start()

        for copy in copies(n, slot):
            copy.wait()
        for i in range(0, chunk, sub):
            both = jnp.concatenate([buf[slot, c, i : i + sub].reshape(sub * levels, modes) for c in range(2)], axis=1)
            prod = jnp.dot(both, z_ref[...], preferred_element_type=F32).reshape(sub, groups, SUB, 2 * points)
            for g in range(groups):
                part = prod[:, g].reshape(sub * SUB, 2 * points).astype(BF16)
                for c in range(2):
                    row = c * width + i * SUB
                    rhs_ref[row : row + sub * SUB, g * points : (g + 1) * points] = part[:, c * points : (c + 1) * points]
        k = lax.rem(n, steps)
        term = jnp.dot(left_ref[k], rhs_ref[...], preferred_element_type=F32)
        acc_ref[...] = jnp.where(k == 0, 0.0, acc_ref[...]) + term

        @pl.when(k == steps - 1)
        def _():
            v = lax.div(n, steps)
            per = LANE // levels
            blocks, parts = out_ref.shape[:2]
            piece = points // parts
            short = piece // blocks
            for t in range(rows // per):
                tile = jnp.concatenate(
                    [
                        acc_ref[f * SUB : (f + 1) * SUB, g * points : (g + 1) * points]
                        for f in range(t * per, (t + 1) * per)
                        for g in range(groups)
                    ],
                    axis=0,
                )
                turned = tile.T
                for s in range(parts):
                    for b in range(blocks):
                        low = s * piece + b * short
                        out_ref[b, s, v, t] = turned[low : low + short]

        return 0

    lax.fori_loop(0, total, body, 0)


def feed(coeff, rep, table, first, count, blocks, parts, chunk, depth):
    _, modes_x, _, levels, modes = coeff.shape
    points = table.shape[1] // 2
    rows = rep.shape[1]
    groups = levels // SUB
    tiles = rows * levels // LANE
    chunk = min(chunk, modes_x)
    steps = modes_x // chunk
    flops = 2 * count * modes_x * levels * (2 * modes * 2 * points + rows * SUB * 2 * points)
    vmem = pl.BlockSpec(memory_space=pltpu.VMEM)
    return pl.pallas_call(
        functools.partial(feed_kernel, first, count, chunk, depth), name="feed",
        out_shape=jax.ShapeDtypeStruct((blocks, parts, count, tiles, points // parts // blocks, LANE), F32),
        in_specs=[vmem, vmem, pl.BlockSpec(memory_space=pl.ANY)], out_specs=vmem,
        scratch_shapes=[
            pltpu.VMEM((depth, 2, chunk, levels, modes), BF16),
            pltpu.VMEM((steps, rows * SUB, 2 * chunk * SUB), BF16),
            pltpu.VMEM((2 * chunk * SUB, groups * points), BF16),
            pltpu.VMEM((rows * SUB, groups * points), F32),
            pltpu.SemaphoreType.DMA((depth, 2)),
        ],
        compiler_params=pltpu.CompilerParams(vmem_limit_bytes=24 * 2**20),
        cost_estimate=pl.CostEstimate(flops=flops, bytes_accessed=2 * count * modes_x * levels * modes * 2, transcendentals=0),
    )(rep, table, coeff)


def factors(feed_plane, mode_first, modes_x, stream_points, levels):
    per = LANE // levels
    planes = feed_plane.shape[0]
    rows = -(-planes // per) * per
    padded = jnp.concatenate([feed_plane, jnp.zeros((rows - planes,), jnp.int32)])
    ids = mode_first + lax.broadcasted_iota(jnp.int32, (rows, modes_x * SUB), 1) // SUB
    angle = 2.0 * math.pi / stream_points * (padded[:, None] * ids % stream_points).astype(F32)
    rep = jnp.stack([jnp.cos(angle), -jnp.sin(angle)])
    return rep.astype(BF16).astype(F32)


def force_kernel(steps, per, levels, owners, offset, strength, *refs):
    far, state, out_ref = refs[:owners], refs[owners], refs[owners + 1]
    near, cells, sems = refs[owners + 2 : 2 * owners + 2], refs[-2], refs[-1]
    parts, variables, tiles, short, _ = near[0].shape

    def planes(t):
        return pl.ds(t * per, per)

    loads = [pltpu.make_async_copy(far[b], near[b], sems.at[b]) for b in range(owners)]
    reads = [pltpu.make_async_copy(state.at[:, planes(t)], cells.at[:, planes(t)], sems.at[owners + t]) for t in range(steps)]
    writes = [
        pltpu.make_async_copy(cells.at[:, planes(t)], out_ref.at[:, planes(t)], sems.at[owners + steps + t])
        for t in range(steps)
    ]
    for copy in loads + reads:
        copy.start()
    for copy in loads:
        copy.wait()
    lane = lax.broadcasted_iota(jnp.int32, (short, LANE), 1)
    for t in range(steps):
        reads[t].wait()
        tile = jnp.minimum(t + offset[0], tiles - 1)

        @pl.loop(0, variables)
        def _(v):
            for b in range(owners):
                blocks = [near[b][s, v, tile] for s in range(parts)]
                for i in range(per):
                    row = blocks[0] if i == 0 else pltpu.roll(blocks[0], (-i * levels) % LANE, 1)
                    for s in range(1, parts):
                        moved = blocks[s] if s == i else pltpu.roll(blocks[s], ((s - i) * levels) % LANE, 1)
                        row = jnp.where(lane >= s * levels, moved, row)
                    some = pl.ds(b * short, short)
                    cells[v, t * per + i, some] = cells[v, t * per + i, some] + (0.05 * strength[t * per + i]) * row

        writes[t].start()
    for copy in writes:
        copy.wait()


def force(state, targets, strength, offset, levels, planes):
    variables, nx, nz, ny = state.shape
    per = LANE // levels
    steps = -(-min(planes, nx) // per)
    owners = len(targets)
    anywhere = pl.BlockSpec(memory_space=pl.ANY)
    return pl.pallas_call(
        functools.partial(force_kernel, steps, per, levels, owners), name="force",
        out_shape=jax.ShapeDtypeStruct(state.shape, F32),
        in_specs=[SCALARS, SCALARS] + [anywhere] * (owners + 1), out_specs=anywhere,
        scratch_shapes=[pltpu.VMEM(t.shape, F32) for t in targets]
        + [pltpu.VMEM((variables, steps * per, nz, ny), F32), pltpu.SemaphoreType.DMA((owners + 2 * steps,))],
        input_output_aliases={2 + owners: 0},
        compiler_params=pltpu.CompilerParams(vmem_limit_bytes=16 * 2**20),
    )(offset, strength, *targets, state)


GX = ("gh", "gl")
LATE = 3


def local(state, coeff, feed_plane):
    high, low, parts = lax.axis_size("gh"), lax.axis_size("gl"), lax.axis_size("gz")
    gx = high * low
    me = lax.axis_index("gh") * low + lax.axis_index("gl")
    variables, nx, nz, ny = state.shape
    _, modes_x, _, levels, modes = coeff.shape
    planes = feed_plane.shape[0]

    ring = [(i, (i + 1) % parts) for i in range(parts)]
    line = [(i, i + 1) for i in range(gx - 1)]
    zside = [jnp.stack([state[:, :, k + j] for j in range(3)]) for k in (nz - 3, 0)]
    xlo = lax.ppermute(state[:, nx - 3 :], GX, line)
    xhi = lax.ppermute(state[:, :3], GX, [(j, i) for i, j in line])
    zlo = lax.ppermute(zside[0], "gz", ring)
    zhi = lax.ppermute(zside[1], "gz", [(j, i) for i, j in ring])

    rep = factors(feed_plane, me * modes_x, modes_x, 2 * modes_x * gx, levels)
    table = span_tables(modes, nz * parts)
    edges = jnp.stack([me == 0, me == gx - 1]).astype(jnp.int32)
    plane = me * nx + jnp.arange(nx, dtype=jnp.int32)
    strength = jnp.where(plane < planes, 2.0 * jnp.square(1.0 - plane.astype(F32) / planes), 0.0)

    def spread(part):
        part = part.reshape(-1, *part.shape[2:])
        part = lax.all_to_all(part, ("gl", "gz"), split_axis=0, concat_axis=0, tiled=True)
        return part.reshape(low, parts, *part.shape[1:]).sum(0)

    def gather(part):
        stride = 1
        while stride < high:
            hops = [(i, i - stride) for i in range(stride, high, 2 * stride)]
            part = part + lax.ppermute(part, "gh", hops)
            stride *= 2
        return part

    early = variables - LATE
    one = feed(coeff, rep, table, 0, early, low, parts, 64, 3)
    one, xlo, xhi, zlo, zhi, rep = lax.optimization_barrier((one, xlo, xhi, zlo, zhi, rep))
    one = spread(one)
    two = feed(coeff, rep, table, early, LATE, low, parts, 64, 3)
    one, two, xlo = lax.optimization_barrier((one, two, xlo))
    one = gather(one)
    two = spread(two)
    acc = stream_sweep(state, xlo, xhi, edges)
    one, two, acc = lax.optimization_barrier((one, two, acc))
    two = gather(two)
    acc = span_sweep(state, zlo, zhi, acc)
    part = jnp.concatenate([one, two], axis=1)
    part, acc = lax.optimization_barrier((part, acc))
    owned = [part] + [lax.ppermute(part, GX, [(i, 0)]) for i in range(1, low)]
    new = wall_sweep(state, acc, strength)
    for other in range(1, -(-planes // nx)):
        owned = [jnp.where(me == other, lax.ppermute(t, GX, [(0, other)]), t) for t in owned]
    offset = jnp.reshape(me * nx // (LANE // levels), (1,))
    return force(new, owned, strength, offset, levels, planes)


def solution(mesh):
    gx, gz = mesh.devices.shape
    low = next(n for n in (4, 2, 1) if gx % n == 0)
    split = Mesh(mesh.devices.reshape(gx // low, low, gz), ("gh", "gl", "gz"))
    cells = P(None, GX, "gz", None)
    return jax.shard_map(
        local, mesh=split, in_specs=(cells, P(None, GX, None, "gz", None), P()), out_specs=cells, check_vma=False
    )
```

time: 141 us -> 97.8 us (0.69)
  Pallas kernels: 77.3 us -> 59.3 us
  waiting for transfers between devices: 22.5 us -> 7.4 us
  starting transfers between devices: 31.9 us -> 26.5 us
  other arithmetic: 4.15 us -> 0.6 us
    pallas_call x7 -> x6, Pallas kernels: 77.3 us -> 59.3 us  [the longest x2 25.1 us: feed(): pl.pallas_call(functools.partial(feed_kernel, first, count, chunk, depth)...]
    ppermute x9 -> x5, waiting for transfers between devices: 13.2 us -> 2.46 us  [the longest x3 2.45 us: local(): owned = [part] + [lax.ppermute(part, GX, [(i, 0)]) for i in range(1, low)]]
    ppermute x9 -> x5, starting transfers between devices: 11.6 us -> 6.46 us  [the longest x3 3.88 us: local(): owned = [part] + [lax.ppermute(part, GX, [(i, 0)]) for i in range(1, low)]]
    ppermute x1, waiting for transfers between devices: 4.49 us -> 0.01 us  [local(): xlo = lax.ppermute(state[:, nx - 3:], GX, line)]
    add x6 -> x2, other arithmetic: 2.95 us -> 0.03 us  [gather(): part = part + lax.ppermute(part, 'gh', hops)]
    all_to_all x3 -> x2, starting transfers between devices: 13.7 us -> 11.4 us  [spread(): lax.all_to_all(part, ('gl', 'gz'), split_axis=0, concat_axis=0, tiled=True)]
    slice x0 -> x1, local copies, waits for them, and re-layouts: none -> 2.02 us  [local(): state[:, :, k + j]]
    all_to_all x3 -> x2, waiting for transfers between devices: 4.82 us -> 4.93 us  [spread(): lax.all_to_all(part, ('gl', 'gz'), split_axis=0, concat_axis=0, tiled=True)]
  transfers between devices with their start and end apart: 16 -> 11, of which waited for: 4 -> 2; matrix products, arithmetic and copies ran while one was open for 4% -> 2% of each run, Pallas kernels for 43% -> 56%
where the time goes in v2:
time: 97.8 us; the launch traced here: 97.2 us
  Pallas kernels  59.3 us (61%)
  starting transfers between devices  26.5 us (27%)
  waiting for transfers between devices  7.4 us (8%)
  local copies, waits for them, and re-layouts  3.12 us (3%)
    pallas_call x2, Pallas kernels, feed(): pl.pallas_call(functools.partial(feed_kernel, first, count, chunk, depth)...  25.1 us
    all_to_all x2, starting transfers between devices, spread(): lax.all_to_all(part, ('gl', 'gz'), split_axis=0, concat_axis=0, tiled=True)  11.4 us
    pallas_call x1, Pallas kernels, wall_sweep(): call(functools.partial(wall_kernel, nz), 'wall_sweep', flat, nx * nz // L...  11 us
    pallas_call x1, Pallas kernels, span_sweep(): call(functools.partial(span_kernel, nz), 'span_sweep', flat, nx // SUB, [...  10.4 us
    pallas_call x1, Pallas kernels, stream_sweep(): call(stream_kernel, 'stream_sweep', q, nz // SUB, [SCALARS, cells, side,...  8.07 us
    all_to_all x2, waiting for transfers between devices, spread(): lax.all_to_all(part, ('gl', 'gz'), split_axis=0, concat_axis=0, tiled=True)  4.93 us
    ppermute x1, starting transfers between devices, local(): xlo = lax.ppermute(state[:, nx - 3:], GX, line)  4.81 us
    pallas_call x1, Pallas kernels, force(): pl.pallas_call(functools.partial(force_kernel, steps, per, levels, owners...  4.78 us
  transfers between devices with their start and end apart: 11, of which 2 were waited for; matrix products, arithmetic and copies ran while one was open for 2% of the time, Pallas kernels for 56%

profile of v2, /device:TPU:0, one launch (start us, length us, event | category | flops | bytes accessed | tf_op | source)
XLA Modules:
  0.0 97.2 jit_solution(1100784794640774381)
XLA Ops:
  0.0 2.0 %fusion.6 = (f32[6,16,1,128]{3,2,1,0:T(1,128)S(1)}, f32[6,16,1,128]{3,2,1,0:T(1,128)S(1)}, f32[6,16,1,128]{3,2,1,0:T(1,128)S(1)}, f32[6,16,1,128]{3,2,1,0:T(1,12...) fusion(f32[6,16,32,128]{3,2,1,0:T(8,128)} %q_ref.1), kind=kLoop, calls=%fused_computation.21 | loop fusion | bytes 589824 | tf_op jit(solution)/shard_map/slice | solution.py:424
  2.1 0.5 collective-permute-start.2
  2.6 2.0 %collective-permute-start.3 = (f32[3,6,16,128]{3,2,1,0:T(8,128)S(1)}, f32[3,6,16,128]{3,2,1,0:T(8,128)S(1)}, u32[]{:S(2)}, u32[]{:S(2)}) collective-permute-start(f32[3,6,16,128]{3,2,1,0:T(8,128)S(1)} %pad_maximum_fusion.2), channel_id=1, source_target_pairs={{1,0},{2,1},{3,2},{0,3},{5,4},{6,5},{7,6},{4,7},{9,8},{10,9},{11,1... | collective-permute-start | bytes 442376 | tf_op jit(solution)/shard_map/ppermute | solution.py:428
  4.6 1.1 %fusion.7 = (f32[6,3,32,128]{3,2,1,0:T(8,128)S(1)}, f32[6,3,32,128]{3,2,1,0:T(8,128)S(1)}) fusion(f32[6,16,32,128]{3,2,1,0:T(8,128)} %q_ref.1), kind=kLoop, calls=%fused_computation.22 | loop fusion | bytes 1179648 | tf_op jit(solution)/shard_map/slice | solution.py:426
  5.7 1.3 %collective-permute-start.1 = (f32[6,3,32,128]{3,2,1,0:T(8,128)S(1)}, f32[6,3,32,128]{3,2,1,0:T(8,128)S(1)}, u32[]{:S(2)}, u32[]{:S(2)}) collective-permute-start(f32[6,3,32,128]{3,2,1,0:T(8,128)S(1)} %get-tuple-element.39), channel_id=1, source_target_pairs={{4,0},{8,4},{12,8},{16,12},{20,16},{24,20},{28,24},{5,1},{9,5},{13... | collective-permute-start | bytes 884744 | tf_op jit(solution)/shard_map/ppermute | solution.py:426
  7.0 4.8 %collective-permute-start = (f32[6,3,32,128]{3,2,1,0:T(8,128)S(1)}, f32[6,3,32,128]{3,2,1,0:T(8,128)S(1)}, u32[]{:S(2)}, u32[]{:S(2)}) collective-permute-start(f32[6,3,32,128]{3,2,1,0:T(8,128)S(1)} %get-tuple-element.40), channel_id=1, source_target_pairs={{0,4},{4,8},{8,12},{12,16},{16,20},{20,24},{24,28},{1,5},{5,9},{9,... | collective-permute-start | bytes 884744 | tf_op jit(solution)/shard_map/ppermute | solution.py:425
  11.9 0.3 cosine_convert_fusion
  12.2 12.5 %feed.2 = f32[4,4,3,3,8,128]{5,4,3,2,1,0:T(8,128)} custom-call(f32[2,12,1024]{2,1,0:T(8,128)S(1)} %maximum_convert_fusion.rep_ref, bf16[1024,256]{1,0:T(8,128)(2,1)S(1)} %copy-done, bf16[2,128,6,32,512]{4,3,2,1,0:T(8,128)(2,1)} %coeff_ref.3), custom_call_target="tpu_custom_call" | custom-call | flops 7046430720 | bytes 25165824 | tf_op jit(solution)/shard_map/feed/pallas_call | solution.py:326
  24.8 0.0 collective-permute-done.2.lo_ref
  24.8 0.0 collective-permute-done.3.hi_ref
  24.8 0.0 collective-permute-done.1.hi_ref
  24.8 0.0 collective-permute-done.lo_ref
  24.8 6.3 %all-to-all-start = ((f32[16,3,3,8,128]{4,3,2,1,0:T(8,128)}), f32[16,3,3,8,128]{4,3,2,1,0:T(8,128)S(1)}, u32[]{:S(2)}, u32[]{:S(2)}) async-start(f32[16,3,3,8,128]{4,3,2,1,0:T(8,128)} %bitcast.7), calls=%async_computation | async-start | bytes 1179648 | tf_op jit(solution)/shard_map/all_to_all | solution.py:438
  31.1 12.5 %feed.3 = f32[4,4,3,3,8,128]{5,4,3,2,1,0:T(8,128)} custom-call(f32[2,12,1024]{2,1,0:T(8,128)S(1)} %maximum_convert_fusion.rep_ref, bf16[1024,256]{1,0:T(8,128)(2,1)S(1)} %copy-done, bf16[2,128,6,32,512]{4,3,2,1,0:T(8,128)(2,1)} %coeff_ref.3), custom_call_target="tpu_custom_call" | custom-call | flops 7046430720 | bytes 25165824 | tf_op jit(solution)/shard_map/feed/pallas_call | solution.py:326
  43.6 0.0 all-to-all-done
  43.7 5.1 %all-to-all-start.1 = ((f32[16,3,3,8,128]{4,3,2,1,0:T(8,128)}), f32[16,3,3,8,128]{4,3,2,1,0:T(8,128)S(1)}, u32[]{:S(2)}, u32[]{:S(2)}) async-start(f32[16,3,3,8,128]{4,3,2,1,0:T(8,128)} %bitcast.9), calls=%async_computation.1 | async-start | bytes 1179648 | tf_op jit(solution)/shard_map/all_to_all | solution.py:438
  48.8 1.3 %collective-permute-start.4 = (f32[4,3,3,8,128]{4,3,2,1,0:T(8,128)S(1)}, f32[4,3,3,8,128]{4,3,2,1,0:T(8,128)S(1)}, u32[]{:S(2)}, u32[]{:S(2)}) collective-permute-start(f32[4,3,3,8,128]{4,3,2,1,0:T(8,128)S(1)} %reduce_sum.18), channel_id=1, source_target_pairs={{16,0},{17,1},{18,2},{19,3},{20,4},{21,5},{22,6},{23,7},{24,8},{25... | collective-permute-start | bytes 442376 | tf_op jit(solution)/shard_map/ppermute | solution.py:445
  50.1 0.1 add_convert_fusion.flags
  50.2 8.1 %stream_sweep.1 = f32[6,16,32,128]{3,2,1,0:T(8,128)} custom-call(s32[2]{0:T(128)S(1)} %add_convert_fusion.flags, f32[6,16,32,128]{3,2,1,0:T(8,128)} %q_ref.1, f32[6,3,32,128]{3,2,1,0:T(8,128)S(1)} %collective-permute-done.lo_ref, f32[6,3,32,128]{3,2,1,0:T(8,128)S(1)} %collective-permute-done.1.hi_ref), custom_call_target="tpu_custom_call" | custom-call | flops 275251200 | bytes 3145728 | tf_op jit(solution)/shard_map/stream_sweep/pallas_call | solution.py:209
  58.3 0.0 collective-permute-done.4
  58.3 4.9 %all-to-all-done.1 = f32[16,3,3,8,128]{4,3,2,1,0:T(8,128)S(1)} async-done(((f32[16,3,3,8,128]{4,3,2,1,0:T(8,128)}), f32[16,3,3,8,128]{4,3,2,1,0:T(8,128)S(1)}, u32[]{:S(2)}, u32[]{:S(2)}) %all-to-all-start.1) | async-done | bytes 589856 | tf_op jit(solution)/shard_map/all_to_all | solution.py:438
  63.3 1.3 %collective-permute-start.5 = (f32[4,3,3,8,128]{4,3,2,1,0:T(8,128)S(1)}, f32[4,3,3,8,128]{4,3,2,1,0:T(8,128)S(1)}, u32[]{:S(2)}, u32[]{:S(2)}) collective-permute-start(f32[4,3,3,8,128]{4,3,2,1,0:T(8,128)S(1)} %reduce_sum.19), channel_id=1, source_target_pairs={{16,0},{17,1},{18,2},{19,3},{20,4},{21,5},{22,6},{23,7},{24,8},{25... | collective-permute-start | bytes 442376 | tf_op jit(solution)/shard_map/ppermute | solution.py:445
  64.6 10.4 %span_sweep.1 = f32[6,512,128]{2,1,0:T(8,128)} custom-call(f32[6,512,128]{2,1,0:T(8,128)} %bitcast.30, f32[3,6,16,128]{3,2,1,0:T(8,128)S(1)} %collective-permute-done.2.lo_ref, f32[3,6,16,128]{3,2,1,0:T(8,128)S(1)} %collective-permute-done.3.hi_ref, f32[6,512,128]{2,1,0:T(8,128)} %bitcast.32), custom_call_target="tpu_custom_call" | custom-call | flops 275251200 | bytes 3145728 | tf_op jit(solution)/shard_map/span_sweep/pallas_call | solution.py:218
  75.0 0.0 collective-permute-done.5
  75.0 1.3 %collective-permute-start.8 = (f32[4,6,3,8,128]{4,3,2,1,0:T(8,128)S(1)}, f32[4,6,3,8,128]{4,3,2,1,0:T(8,128)S(1)}, u32[]{:S(2)}, u32[]{:S(2)}) collective-permute-start(f32[4,6,3,8,128]{4,3,2,1,0:T(8,128)S(1)} %pad_maximum_fusion.refs_0_), channel_id=1, source_target_pairs={{12,0},{13,1},{14,2},{15,3}} | collective-permute-start | bytes 884744 | tf_op jit(solution)/shard_map/ppermute | solution.py:463
  76.3 1.3 %collective-permute-start.7 = (f32[4,6,3,8,128]{4,3,2,1,0:T(8,128)S(1)}, f32[4,6,3,8,128]{4,3,2,1,0:T(8,128)S(1)}, u32[]{:S(2)}, u32[]{:S(2)}) collective-permute-start(f32[4,6,3,8,128]{4,3,2,1,0:T(8,128)S(1)} %pad_maximum_fusion.refs_0_), channel_id=1, source_target_pairs={{8,0},{9,1},{10,2},{11,3}} | collective-permute-start | bytes 884744 | tf_op jit(solution)/shard_map/ppermute | solution.py:463
  77.6 1.3 %collective-permute-start.6 = (f32[4,6,3,8,128]{4,3,2,1,0:T(8,128)S(1)}, f32[4,6,3,8,128]{4,3,2,1,0:T(8,128)S(1)}, u32[]{:S(2)}, u32[]{:S(2)}) collective-permute-start(f32[4,6,3,8,128]{4,3,2,1,0:T(8,128)S(1)} %pad_maximum_fusion.refs_0_), channel_id=1, source_target_pairs={{4,0},{5,1},{6,2},{7,3}} | collective-permute-start | bytes 884744 | tf_op jit(solution)/shard_map/ppermute | solution.py:463
  79.0 11.0 %wall_sweep.1 = f32[6,512,128]{2,1,0:T(8,128)} custom-call(f32[16]{0:T(128)S(1)} %compare_select_fusion.strength, f32[6,512,128]{2,1,0:T(8,128)} %bitcast.31, f32[6,512,128]{2,1,0:T(8,128)} %span_sweep.1), custom_call_target="tpu_custom_call" | custom-call | flops 275251200 | bytes 3145728 | tf_op jit(solution)/shard_map/wall_sweep/pallas_call | solution.py:227
  90.0 0.0 collective-permute-done.8.refs_3_
  90.0 0.0 collective-permute-done.7.refs_2_
  90.0 2.4 %collective-permute-done.6.refs_1_ = f32[4,6,3,8,128]{4,3,2,1,0:T(8,128)S(1)} collective-permute-done((f32[4,6,3,8,128]{4,3,2,1,0:T(8,128)S(1)}, f32[4,6,3,8,128]{4,3,2,1,0:T(8,128)S(1)}, u32[]{:S(2)}, u32[]{:S(2)}) %collective-permute-start.6) | collective-permute-done | bytes 294944 | tf_op jit(solution)/shard_map/ppermute | solution.py:463
  92.4 4.8 %force.1 = f32[6,16,32,128]{3,2,1,0:T(8,128)} custom-call(s32[1]{0:T(128)} %bitcast.offset, f32[16]{0:T(128)S(1)} %compare_select_fusion.strength, f32[4,6,3,8,128]{4,3,2,1,0:T(8,128)S(1)} %pad_maximum_fusion.refs_0_, f32[4,6,3,8,128]{4,3,2,1,0:T(8,128)S(1)} %collective-permute-done.6.refs_1_, ...), custom_call_target="tpu_custom_call", output_to_operand_aliasing={{}: (6, {})} | custom-call | tf_op jit(solution)/shard_map/force/pallas_call | solution.py:399
  (15 shorter events, 0.2 us)
Async XLA Ops:
  0.0 12.2 %copy-start = (bf16[1024,256]{1,0:T(8,128)(2,1)S(1)}, bf16[1024,256]{1,0:T(8,128)(2,1)}, u32[]{:S(2)}) copy-start(bf16[1024,256]{1,0:T(8,128)(2,1)} %constant.80.z_ref) | copy-start | bytes 1572868
  0.0 11.8 %copy-start.1 = (s32[12]{0:T(128)S(1)}, s32[12]{0:T(128)}, u32[]{:S(2)}) copy-start(s32[12]{0:T(128)} %param.6) | copy-start | bytes 148
  2.1 22.7 %collective-permute-start.2 = (f32[3,6,16,128]{3,2,1,0:T(8,128)S(1)}, f32[3,6,16,128]{3,2,1,0:T(8,128)S(1)}, u32[]{:S(2)}, u32[]{:S(2)}) collective-permute-start(f32[3,6,16,128]{3,2,1,0:T(8,128)S(1)} %pad_maximum_fusion.1), channel_id=1, source_target_pairs={{0,1},{1,2},{2,3},{3,0},{4,5},{5,6},{6,7},{7,4},{8,9},{9,10},{10,1... | collective-permute-start | bytes 442376 | tf_op jit(solution)/shard_map/ppermute | solution.py:427
  2.6 22.2 %collective-permute-start.3 = (f32[3,6,16,128]{3,2,1,0:T(8,128)S(1)}, f32[3,6,16,128]{3,2,1,0:T(8,128)S(1)}, u32[]{:S(2)}, u32[]{:S(2)}) collective-permute-start(f32[3,6,16,128]{3,2,1,0:T(8,128)S(1)} %pad_maximum_fusion.2), channel_id=1, source_target_pairs={{1,0},{2,1},{3,2},{0,3},{5,4},{6,5},{7,6},{4,7},{9,8},{10,9},{11,1... | collective-permute-start | bytes 442376 | tf_op jit(solution)/shard_map/ppermute | solution.py:428
  5.7 19.1 %collective-permute-start.1 = (f32[6,3,32,128]{3,2,1,0:T(8,128)S(1)}, f32[6,3,32,128]{3,2,1,0:T(8,128)S(1)}, u32[]{:S(2)}, u32[]{:S(2)}) collective-permute-start(f32[6,3,32,128]{3,2,1,0:T(8,128)S(1)} %get-tuple-element.39), channel_id=1, source_target_pairs={{4,0},{8,4},{12,8},{16,12},{20,16},{24,20},{28,24},{5,1},{9,5},{13... | collective-permute-start | bytes 884744 | tf_op jit(solution)/shard_map/ppermute | solution.py:426
  7.0 17.8 %collective-permute-start = (f32[6,3,32,128]{3,2,1,0:T(8,128)S(1)}, f32[6,3,32,128]{3,2,1,0:T(8,128)S(1)}, u32[]{:S(2)}, u32[]{:S(2)}) collective-permute-start(f32[6,3,32,128]{3,2,1,0:T(8,128)S(1)} %get-tuple-element.40), channel_id=1, source_target_pairs={{0,4},{4,8},{8,12},{12,16},{16,20},{20,24},{24,28},{1,5},{5,9},{9,... | collective-permute-start | bytes 884744 | tf_op jit(solution)/shard_map/ppermute | solution.py:425
  24.8 18.8 %all-to-all-start = ((f32[16,3,3,8,128]{4,3,2,1,0:T(8,128)}), f32[16,3,3,8,128]{4,3,2,1,0:T(8,128)S(1)}, u32[]{:S(2)}, u32[]{:S(2)}) async-start(f32[16,3,3,8,128]{4,3,2,1,0:T(8,128)} %bitcast.7), calls=%async_computation | async-start | bytes 1179648 | tf_op jit(solution)/shard_map/all_to_all | solution.py:438
  43.7 19.5 %all-to-all-start.1 = ((f32[16,3,3,8,128]{4,3,2,1,0:T(8,128)}), f32[16,3,3,8,128]{4,3,2,1,0:T(8,128)S(1)}, u32[]{:S(2)}, u32[]{:S(2)}) async-start(f32[16,3,3,8,128]{4,3,2,1,0:T(8,128)} %bitcast.9), calls=%async_computation.1 | async-start | bytes 1179648 | tf_op jit(solution)/shard_map/all_to_all | solution.py:438
  48.8 9.5 %collective-permute-start.4 = (f32[4,3,3,8,128]{4,3,2,1,0:T(8,128)S(1)}, f32[4,3,3,8,128]{4,3,2,1,0:T(8,128)S(1)}, u32[]{:S(2)}, u32[]{:S(2)}) collective-permute-start(f32[4,3,3,8,128]{4,3,2,1,0:T(8,128)S(1)} %reduce_sum.18), channel_id=1, source_target_pairs={{16,0},{17,1},{18,2},{19,3},{20,4},{21,5},{22,6},{23,7},{24,8},{25... | collective-permute-start | bytes 442376 | tf_op jit(solution)/shard_map/ppermute | solution.py:445
  63.3 11.7 %collective-permute-start.5 = (f32[4,3,3,8,128]{4,3,2,1,0:T(8,128)S(1)}, f32[4,3,3,8,128]{4,3,2,1,0:T(8,128)S(1)}, u32[]{:S(2)}, u32[]{:S(2)}) collective-permute-start(f32[4,3,3,8,128]{4,3,2,1,0:T(8,128)S(1)} %reduce_sum.19), channel_id=1, source_target_pairs={{16,0},{17,1},{18,2},{19,3},{20,4},{21,5},{22,6},{23,7},{24,8},{25... | collective-permute-start | bytes 442376 | tf_op jit(solution)/shard_map/ppermute | solution.py:445
  75.0 14.9 %collective-permute-start.8 = (f32[4,6,3,8,128]{4,3,2,1,0:T(8,128)S(1)}, f32[4,6,3,8,128]{4,3,2,1,0:T(8,128)S(1)}, u32[]{:S(2)}, u32[]{:S(2)}) collective-permute-start(f32[4,6,3,8,128]{4,3,2,1,0:T(8,128)S(1)} %pad_maximum_fusion.refs_0_), channel_id=1, source_target_pairs={{12,0},{13,1},{14,2},{15,3}} | collective-permute-start | bytes 884744 | tf_op jit(solution)/shard_map/ppermute | solution.py:463
  76.3 13.6 %collective-permute-start.7 = (f32[4,6,3,8,128]{4,3,2,1,0:T(8,128)S(1)}, f32[4,6,3,8,128]{4,3,2,1,0:T(8,128)S(1)}, u32[]{:S(2)}, u32[]{:S(2)}) collective-permute-start(f32[4,6,3,8,128]{4,3,2,1,0:T(8,128)S(1)} %pad_maximum_fusion.refs_0_), channel_id=1, source_target_pairs={{8,0},{9,1},{10,2},{11,3}} | collective-permute-start | bytes 884744 | tf_op jit(solution)/shard_map/ppermute | solution.py:463
  77.6 14.8 %collective-permute-start.6 = (f32[4,6,3,8,128]{4,3,2,1,0:T(8,128)S(1)}, f32[4,6,3,8,128]{4,3,2,1,0:T(8,128)S(1)}, u32[]{:S(2)}, u32[]{:S(2)}) collective-permute-start(f32[4,6,3,8,128]{4,3,2,1,0:T(8,128)S(1)} %pad_maximum_fusion.refs_0_), channel_id=1, source_target_pairs={{4,0},{5,1},{6,2},{7,3}} | collective-permute-start | bytes 884744 | tf_op jit(solution)/shard_map/ppermute | solution.py:463

commit v3 on v2

--- a/solution.py
+++ b/solution.py
@@ -15,7 +15,6 @@
 
 
 U1, U2 = 16, 4
-TALL = 64
 
 
 def cell_flux(q, comp):
@@ -104,7 +103,7 @@
     ]
 
 
-def stream_kernel(flags, q_ref, lo_ref, hi_ref, acc_ref, gf, gq, mx):
+def stream_kernel(flags, strength, q_ref, lo_ref, hi_ref, acc_in, out_ref, gf, gq, mx):
     nx = q_ref.shape[1]
 
     def mid(j):
@@ -116,8 +115,17 @@
         return load
 
     def put(c, total):
-        for v in range(6):
-            acc_ref[v, c] = total[v]
+        q = mid(c)
+        rinv = 1.0 / q[0]
+        p = 0.4 * (q[4] - 0.5 * (q[1] * q[1] + q[2] * q[2] + q[3] * q[3]) * rinv - q[5])
+        temp = p * rinv
+        share = 2.0 / (jnp.exp(2.0 / temp) - 1.0)
+        lag = jnp.exp(1.5 * (jnp.exp(-jnp.log(temp) / 3.0) - 1.0))
+        relax = (q[0] * share - q[5]) * (2.0 * p) / lag
+        keep = 1.0 - 0.05 * strength[c]
+        for v in range(6):
+            new = keep * q[v] - (0.05 / 12.0) * (acc_in[v, c] + total[v])
+            out_ref[v, c] = new + 0.05 * relax if v == 5 else new
 
     sweep(1, nx, side(lo_ref, flags[0], 0), mid, side(hi_ref, flags[1], nx - 1), put, gf, gq, mx)
 
@@ -139,7 +147,7 @@
     sweep(3, nz, side(lo_ref), mid, side(hi_ref), put, gf, gq, mx)
 
 
-def wall_kernel(nz, strength, q_ref, acc_in, out_ref, yq, yt, gf, gq, mx):
+def wall_kernel(after, q_ref, out_ref, yq, yt, gf, gq, mx):
     ny = q_ref.shape[2]
     seg = ny // SUB
     for v in range(6):
@@ -164,27 +172,7 @@
     sweep(2, seg, lambda j: load(j - 3), load, lambda j: load(seg + j), put, gf, gq, mx)
 
     for v in range(6):
-        yt[v] = yt[v].T
-
-    @pl.loop(0, LANE // TALL)
-    def _(i):
-        o = pl.multiple_of(i * TALL, TALL)
-        rows = pl.ds(o, TALL)
-        q = [q_ref[v, rows, :] for v in range(6)]
-        rinv = 1.0 / q[0]
-        p = 0.4 * (q[4] - 0.5 * (q[1] * q[1] + q[2] * q[2] + q[3] * q[3]) * rinv - q[5])
-        temp = p * rinv
-        share = 2.0 / (jnp.exp(2.0 / temp) - 1.0)
-        lag = jnp.exp(1.5 * (jnp.exp(-jnp.log(temp) / 3.0) - 1.0))
-        relax = (q[0] * share - q[5]) * (2.0 * p) / lag
-        pull = jnp.zeros((TALL, ny), F32)
-        for k in range(TALL // nz):
-            pull = jnp.where(lax.broadcasted_iota(jnp.int32, (TALL, ny), 0) >= k * nz, strength[(pl.program_id(0) * LANE + o) // nz + k], pull)
-        for v in range(6):
-            rate = (acc_in[v, rows, :] + yt[v, rows, :]) * (-1.0 / 12.0)
-            if v == 5:
-                rate = rate + relax
-            out_ref[v, rows, :] = q[v] + 0.05 * (rate - pull * q[v])
+        out_ref[v] = yt[v].T
 
 
 def far(x):
@@ -202,12 +190,13 @@
 SCALARS = pl.BlockSpec(memory_space=pltpu.SMEM)
 
 
-def stream_sweep(q, xlo, xhi, edges):
+def wall_sweep(q, after):
     _, nx, nz, ny = q.shape
-    cells = pl.BlockSpec((6, nx, SUB, ny), lambda t: (0, 0, t, 0))
-    side = pl.BlockSpec((6, 3, SUB, ny), lambda t: (0, 0, t, 0))
-    return call(stream_kernel, "stream_sweep", q, nz // SUB, [SCALARS, cells, side, side], cells, scratch(nx))(
-        edges, far(q), xlo, xhi)
+    flat = q.reshape(6, nx * nz, ny)
+    cells = pl.BlockSpec((6, LANE, ny), lambda t: (0, t, 0))
+    shapes = [pltpu.VMEM((6, ny + 2 * SUB, LANE), F32), pltpu.VMEM((6, ny, LANE), F32)] + scratch(ny // SUB)
+    return call(wall_kernel, "wall_sweep", flat, nx * nz // LANE, [SCALARS, cells], cells, shapes)(
+        after, far(flat)).reshape(q.shape)
 
 
 def span_sweep(q, zlo, zhi, acc):
@@ -219,13 +208,12 @@
         far(flat), zlo, zhi, far(acc.reshape(flat.shape))).reshape(q.shape)
 
 
-def wall_sweep(q, acc, strength):
+def stream_sweep(q, xlo, xhi, acc, edges, strength):
     _, nx, nz, ny = q.shape
-    flat = q.reshape(6, nx * nz, ny)
-    cells = pl.BlockSpec((6, LANE, ny), lambda t: (0, t, 0))
-    shapes = [pltpu.VMEM((6, ny + 2 * SUB, LANE), F32), pltpu.VMEM((6, ny, LANE), F32)] + scratch(ny // SUB)
-    return call(functools.partial(wall_kernel, nz), "wall_sweep", flat, nx * nz // LANE, [SCALARS, cells, cells], cells, shapes)(
-        strength, far(flat), far(acc.reshape(flat.shape))).reshape(q.shape)
+    cells = pl.BlockSpec((6, nx, SUB, ny), lambda t: (0, 0, t, 0))
+    side = pl.BlockSpec((6, 3, SUB, ny), lambda t: (0, 0, t, 0))
+    return call(stream_kernel, "stream_sweep", q, nz // SUB, [SCALARS, SCALARS, cells, side, side, cells], cells, scratch(nx))(
+        edges, strength, far(q), xlo, xhi, far(acc))
 
 
 def span_tables(modes, points):
@@ -235,11 +223,10 @@
     return jnp.asarray(np.concatenate([np.concatenate([cz, sz], 1), np.concatenate([-sz, cz], 1)], 0), F32).astype(BF16)
 
 
-def feed_kernel(first, count, chunk, depth, rep_ref, z_ref, coeff_ref, out_ref, buf, left_ref, rhs_ref, acc_ref, sems):
+def feed_kernel(first, count, chunk, depth, rows, stream_points, scalars, z_far, coeff_ref, out_ref, z_ref, buf, left_ref, rhs_a, rhs_b, acc_ref, sems):
     _, modes_x, _, levels, modes = coeff_ref.shape
     groups = levels // SUB
-    points = z_ref.shape[1] // 2
-    rows = rep_ref.shape[1]
+    points = z_far.shape[1] // 2
     steps = modes_x // chunk
     total = count * steps
     width = chunk * SUB
@@ -251,19 +238,27 @@
             pltpu.make_async_copy(coeff_ref.at[c, pl.ds(k, chunk), v], buf.at[slot, c], sems.at[slot, c]) for c in range(2)
         ]
 
+    table = pltpu.make_async_copy(z_far, z_ref, sems.at[depth, 0])
+    table.start()
     for n in range(min(depth - 1, total)):
         for copy in copies(n, n):
             copy.start()
 
+    plane = lax.broadcasted_iota(jnp.int32, (rows, width), 0)
+    mode = scalars[0] + lax.broadcasted_iota(jnp.int32, (rows, width), 1) // SUB
+    station = jnp.zeros((rows, width), jnp.int32)
+    for f in range(scalars.shape[0] - 1):
+        station = jnp.where(plane == f, scalars[1 + f], station)
     own = lax.broadcasted_iota(jnp.int32, (rows, SUB, width), 2) % SUB == lax.broadcasted_iota(
         jnp.int32, (rows, SUB, width), 1
     )
     for k in range(steps):
-        for c in range(2):
-            spread = jnp.where(own, rep_ref[c, :, k * width : (k + 1) * width][:, None, :], 0.0)
+        angle = (2.0 * math.pi / stream_points) * ((station * (mode + k * chunk)) % stream_points).astype(F32)
+        for c, factor in enumerate((jnp.cos(angle), -jnp.sin(angle))):
+            spread = jnp.where(own, factor[:, None, :], 0.0)
             left_ref[k, :, c * width : (c + 1) * width] = spread.reshape(rows * SUB, width).astype(BF16)
 
-    def body(n, _):
+    def fetch(n):
         slot = lax.rem(n, depth)
         ahead = n + depth - 1
 
@@ -274,6 +269,9 @@
 
         for copy in copies(n, slot):
             copy.wait()
+        return slot
+
+    def span(slot, rhs_ref):
         for i in range(0, chunk, sub):
             both = jnp.concatenate([buf[slot, c, i : i + sub].reshape(sub * levels, modes) for c in range(2)], axis=1)
             prod = jnp.dot(both, z_ref[...], preferred_element_type=F32).reshape(sub, groups, SUB, 2 * points)
@@ -282,11 +280,14 @@
                 for c in range(2):
                     row = c * width + i * SUB
                     rhs_ref[row : row + sub * SUB, g * points : (g + 1) * points] = part[:, c * points : (c + 1) * points]
+
+    def stream(n, rhs_ref):
         k = lax.rem(n, steps)
         term = jnp.dot(left_ref[k], rhs_ref[...], preferred_element_type=F32)
         acc_ref[...] = jnp.where(k == 0, 0.0, acc_ref[...]) + term
 
-        @pl.when(k == steps - 1)
+    def give(n):
+        @pl.when(lax.rem(n, steps) == steps - 1)
         def _():
             v = lax.div(n, steps)
             per = LANE // levels
@@ -308,15 +309,31 @@
                         low = s * piece + b * short
                         out_ref[b, s, v, t] = turned[low : low + short]
 
-        return 0
-
-    lax.fori_loop(0, total, body, 0)
-
-
-def feed(coeff, rep, table, first, count, blocks, parts, chunk, depth):
+    def both_stages(n, fill, drain):
+        slot = fetch(n)
+        stream(n - 1, drain)
+        span(slot, fill)
+        give(n - 1)
+
+    table.wait()
+    span(fetch(0), rhs_a)
+
+    @pl.loop(0, (total - 1) // 2)
+    def _(m):
+        both_stages(2 * m + 1, rhs_b, rhs_a)
+        both_stages(2 * m + 2, rhs_a, rhs_b)
+
+    last = rhs_a
+    if total % 2 == 0:
+        both_stages(total - 1, rhs_b, rhs_a)
+        last = rhs_b
+    stream(total - 1, last)
+    give(total - 1)
+
+
+def feed(coeff, scalars, rows, stream_points, table, first, count, blocks, parts, chunk, depth):
     _, modes_x, _, levels, modes = coeff.shape
     points = table.shape[1] // 2
-    rows = rep.shape[1]
     groups = levels // SUB
     tiles = rows * levels // LANE
     chunk = min(chunk, modes_x)
@@ -324,30 +341,21 @@
     flops = 2 * count * modes_x * levels * (2 * modes * 2 * points + rows * SUB * 2 * points)
     vmem = pl.BlockSpec(memory_space=pltpu.VMEM)
     return pl.pallas_call(
-        functools.partial(feed_kernel, first, count, chunk, depth), name="feed",
+        functools.partial(feed_kernel, first, count, chunk, depth, rows, stream_points), name="feed",
         out_shape=jax.ShapeDtypeStruct((blocks, parts, count, tiles, points // parts // blocks, LANE), F32),
-        in_specs=[vmem, vmem, pl.BlockSpec(memory_space=pl.ANY)], out_specs=vmem,
+        in_specs=[SCALARS, pl.BlockSpec(memory_space=pl.ANY), pl.BlockSpec(memory_space=pl.ANY)], out_specs=vmem,
         scratch_shapes=[
+            pltpu.VMEM(table.shape, BF16),
             pltpu.VMEM((depth, 2, chunk, levels, modes), BF16),
             pltpu.VMEM((steps, rows * SUB, 2 * chunk * SUB), BF16),
             pltpu.VMEM((2 * chunk * SUB, groups * points), BF16),
+            pltpu.VMEM((2 * chunk * SUB, groups * points), BF16),
             pltpu.VMEM((rows * SUB, groups * points), F32),
-            pltpu.SemaphoreType.DMA((depth, 2)),
+            pltpu.SemaphoreType.DMA((depth + 1, 2)),
         ],
         compiler_params=pltpu.CompilerParams(vmem_limit_bytes=24 * 2**20),
         cost_estimate=pl.CostEstimate(flops=flops, bytes_accessed=2 * count * modes_x * levels * modes * 2, transcendentals=0),
-    )(rep, table, coeff)
-
-
-def factors(feed_plane, mode_first, modes_x, stream_points, levels):
-    per = LANE // levels
-    planes = feed_plane.shape[0]
-    rows = -(-planes // per) * per
-    padded = jnp.concatenate([feed_plane, jnp.zeros((rows - planes,), jnp.int32)])
-    ids = mode_first + lax.broadcasted_iota(jnp.int32, (rows, modes_x * SUB), 1) // SUB
-    angle = 2.0 * math.pi / stream_points * (padded[:, None] * ids % stream_points).astype(F32)
-    rep = jnp.stack([jnp.cos(angle), -jnp.sin(angle)])
-    return rep.astype(BF16).astype(F32)
+    )(scalars, far(table), coeff)
 
 
 def force_kernel(steps, per, levels, owners, offset, strength, *refs):
@@ -373,8 +381,7 @@
         reads[t].wait()
         tile = jnp.minimum(t + offset[0], tiles - 1)
 
-        @pl.loop(0, variables)
-        def _(v):
+        for v in range(variables):
             for b in range(owners):
                 blocks = [near[b][s, v, tile] for s in range(parts)]
                 for i in range(per):
@@ -408,7 +415,6 @@
 
 
 GX = ("gh", "gl")
-LATE = 3
 
 
 def local(state, coeff, feed_plane):
@@ -419,15 +425,11 @@
     _, modes_x, _, levels, modes = coeff.shape
     planes = feed_plane.shape[0]
 
+    per = LANE // levels
+    rows = -(-planes // per) * per
+    scalars = jnp.concatenate([jnp.reshape(me * modes_x, (1,)), feed_plane])
     ring = [(i, (i + 1) % parts) for i in range(parts)]
     line = [(i, i + 1) for i in range(gx - 1)]
-    zside = [jnp.stack([state[:, :, k + j] for j in range(3)]) for k in (nz - 3, 0)]
-    xlo = lax.ppermute(state[:, nx - 3 :], GX, line)
-    xhi = lax.ppermute(state[:, :3], GX, [(j, i) for i, j in line])
-    zlo = lax.ppermute(zside[0], "gz", ring)
-    zhi = lax.ppermute(zside[1], "gz", [(j, i) for i, j in ring])
-
-    rep = factors(feed_plane, me * modes_x, modes_x, 2 * modes_x * gx, levels)
     table = span_tables(modes, nz * parts)
     edges = jnp.stack([me == 0, me == gx - 1]).astype(jnp.int32)
     plane = me * nx + jnp.arange(nx, dtype=jnp.int32)
@@ -446,25 +448,24 @@
             stride *= 2
         return part
 
-    early = variables - LATE
-    one = feed(coeff, rep, table, 0, early, low, parts, 64, 3)
-    one, xlo, xhi, zlo, zhi, rep = lax.optimization_barrier((one, xlo, xhi, zlo, zhi, rep))
-    one = spread(one)
-    two = feed(coeff, rep, table, early, LATE, low, parts, 64, 3)
-    one, two, xlo = lax.optimization_barrier((one, two, xlo))
-    one = gather(one)
-    two = spread(two)
-    acc = stream_sweep(state, xlo, xhi, edges)
-    one, two, acc = lax.optimization_barrier((one, two, acc))
-    two = gather(two)
+    part = feed(coeff, scalars, rows, 2 * modes_x * gx, table, 0, variables, low, parts, 64, 3)
+    part, edges, late = lax.optimization_barrier((part, edges, state))
+    slabs = [late[:, nx - 3 :], late[:, :3]] + [jnp.stack([late[:, :, k + j] for j in range(3)]) for k in (nz - 3, 0)]
+    part = spread(part)
+    zlo = lax.ppermute(slabs[2], "gz", ring)
+    zhi = lax.ppermute(slabs[3], "gz", [(j, i) for i, j in ring])
+    acc = wall_sweep(state, edges)
+    part, acc, zlo, zhi, *slabs = lax.optimization_barrier((part, acc, zlo, zhi, *slabs[:2]))
+    xlo = lax.ppermute(slabs[0], GX, line)
+    xhi = lax.ppermute(slabs[1], GX, [(j, i) for i, j in line])
+    part = gather(part)
     acc = span_sweep(state, zlo, zhi, acc)
-    part = jnp.concatenate([one, two], axis=1)
     part, acc = lax.optimization_barrier((part, acc))
     owned = [part] + [lax.ppermute(part, GX, [(i, 0)]) for i in range(1, low)]
-    new = wall_sweep(state, acc, strength)
+    new = stream_sweep(state, xlo, xhi, acc, edges, strength)
     for other in range(1, -(-planes // nx)):
         owned = [jnp.where(me == other, lax.ppermute(t, GX, [(0, other)]), t) for t in owned]
-    offset = jnp.reshape(me * nx // (LANE // levels), (1,))
+    offset = jnp.reshape(me * nx // per, (1,))
     return force(new, owned, strength, offset, levels, planes)
 
 

time: 97.8 us -> 87.6 us (0.90)
  starting transfers between devices: 26.5 us -> 18.1 us
  Pallas kernels: 59.3 us -> 54.8 us
  waiting for transfers between devices: 7.4 us -> 11.1 us
  local copies, waits for them, and re-layouts: 3.12 us -> 2.03 us
    all_to_all x2 -> x1, starting transfers between devices: 11.4 us -> 6.44 us  [spread(): lax.all_to_all(part, ('gl', 'gz'), split_axis=0, concat_axis=0, tiled=True)]
    pallas_call x4 -> x3, Pallas kernels: 44.1 us -> 40.7 us  [the longest x1 21.9 us: feed(): pl.pallas_call(functools.partial(feed_kernel, first, count, chunk, depth,...]
    ppermute x2 -> x1, waiting for transfers between devices: 0.01 us -> 2.58 us  [gather(): part = part + lax.ppermute(part, 'gh', hops)]
    ppermute x4, starting transfers between devices: 8.63 us -> 6.53 us  [the longest x1 3.39 us: local(): xlo = lax.ppermute(slabs[0], GX, line)]
    slice x2 -> x1, local copies, waits for them, and re-layouts: 3.11 us -> 1.09 us  [local(): late[:, :3]]
    ppermute x3, waiting for transfers between devices: 2.45 us -> 4.11 us  [local(): owned = [part] + [lax.ppermute(part, GX, [(i, 0)]) for i in range(1, low)]]
    ppermute x2 -> x1, starting transfers between devices: 2.58 us -> 1.28 us  [gather(): part = part + lax.ppermute(part, 'gh', hops)]
    pallas_call x1, Pallas kernels: 4.78 us -> 3.74 us  [force(): pl.pallas_call(functools.partial(force_kernel, steps, per, levels, owners...]
  transfers between devices with their start and end apart: 11 -> 9, of which waited for: 2 -> 4; matrix products, arithmetic and copies ran while one was open for 2% -> 2% of each run, Pallas kernels for 56% -> 34%
where the time goes in v3:
time: 87.6 us; the launch traced here: 87.2 us
  Pallas kernels  54.8 us (63%)
  starting transfers between devices  18.1 us (21%)
  waiting for transfers between devices  11.1 us (13%)
  local copies, waits for them, and re-layouts  2.03 us (2%)
  other arithmetic  0.95 us (1%)
    pallas_call x1, Pallas kernels, feed(): pl.pallas_call(functools.partial(feed_kernel, first, count, chunk, depth,...  21.9 us
    pallas_call x1, Pallas kernels, span_sweep(): call(functools.partial(span_kernel, nz), 'span_sweep', flat, nx // SUB, [...  10.4 us
    pallas_call x1, Pallas kernels, wall_sweep(): call(wall_kernel, 'wall_sweep', flat, nx * nz // LANE, [SCALARS, cells],...  10 us
    pallas_call x1, Pallas kernels, stream_sweep(): call(stream_kernel, 'stream_sweep', q, nz // SUB, [SCALARS, SCALARS, cell...  8.82 us
    all_to_all x1, starting transfers between devices, spread(): lax.all_to_all(part, ('gl', 'gz'), split_axis=0, concat_axis=0, tiled=True)  6.44 us
    ppermute x3, waiting for transfers between devices, local(): owned = [part] + [lax.ppermute(part, GX, [(i, 0)]) for i in range(1, low)]  4.11 us
    all_to_all x1, waiting for transfers between devices, spread(): lax.all_to_all(part, ('gl', 'gz'), split_axis=0, concat_axis=0, tiled=True)  4.02 us
    ppermute x3, starting transfers between devices, local(): owned = [part] + [lax.ppermute(part, GX, [(i, 0)]) for i in range(1, low)]  3.88 us
  transfers between devices with their start and end apart: 9, of which 4 were waited for; matrix products, arithmetic and copies ran while one was open for 2% of the time, Pallas kernels for 34%

profile of v3, /device:TPU:0, one launch (start us, length us, event | category | flops | bytes accessed | tf_op | source)
XLA Modules:
  0.0 87.2 jit_solution(2508984569819258587)
XLA Ops:
  0.0 0.1 add_convert_fusion.after.flags
  0.1 0.7 pad_add_fusion.scalars
  0.8 21.9 %feed.1 = f32[4,4,6,3,8,128]{5,4,3,2,1,0:T(8,128)} custom-call(s32[13]{0:T(128)S(1)} %pad_add_fusion.scalars, bf16[1024,256]{1,0:T(8,128)(2,1)} %constant.49.z_far, bf16[2,128,6,32,512]{4,3,2,1,0:T(8,128)(2,1)} %coeff_ref.1), custom_call_target="tpu_custom_call" | custom-call | flops 14092861440 | bytes 50331648 | tf_op jit(solution)/shard_map/feed/pallas_call | solution.py:343
  22.7 0.0 copy-start
  22.7 6.4 %all-to-all-start = ((f32[16,6,3,8,128]{4,3,2,1,0:T(8,128)}), f32[16,6,3,8,128]{4,3,2,1,0:T(8,128)S(1)}, u32[]{:S(2)}, u32[]{:S(2)}) async-start(f32[16,6,3,8,128]{4,3,2,1,0:T(8,128)} %bitcast.4), calls=%async_computation | async-start | bytes 2359296 | tf_op jit(solution)/shard_map/all_to_all | solution.py:440
  29.1 0.0 copy-done
  29.1 0.9 %copy.6 = f32[6,16,32,128]{3,1,0,2:T(8,128)S(1)} copy(f32[6,16,32,128]{3,2,1,0:T(8,128)S(1)} %copy-done) | data formatting | bytes 3145728 | tf_op jit(solution)/shard_map/optimization_barrier | solution.py:452
  30.1 0.5 collective-permute-start
  30.6 1.4 %collective-permute-start.1 = (f32[3,6,16,128]{3,2,1,0:T(8,128)S(1)}, f32[3,6,16,128]{3,2,1,0:T(8,128)S(1)}, u32[]{:S(2)}, u32[]{:S(2)}) collective-permute-start(f32[3,6,16,128]{3,2,1,0:T(8,128)S(1)} %pad_maximum_fusion.1), channel_id=1, source_target_pairs={{1,0},{2,1},{3,2},{0,3},{5,4},{6,5},{7,6},{4,7},{9,8},{10,9},{11,1... | collective-permute-start | bytes 442376 | tf_op jit(solution)/shard_map/ppermute | solution.py:456
  32.0 10.0 %wall_sweep.1 = f32[6,512,128]{2,1,0:T(8,128)} custom-call(s32[2]{0:T(128)S(1)} %add_convert_fusion.after.flags, f32[6,512,128]{2,1,0:T(8,128)} %bitcast.22), custom_call_target="tpu_custom_call" | custom-call | flops 275251200 | bytes 3145728 | tf_op jit(solution)/shard_map/wall_sweep/pallas_call | solution.py:198
  42.0 1.1 %fusion = (f32[6,3,32,128]{3,2,1,0:T(8,128)S(1)}, f32[6,3,32,128]{3,2,1,0:T(8,128)S(1)}) fusion(f32[6,16,32,128]{3,2,1,0:T(8,128)} %q_ref.1), kind=kLoop, calls=%fused_computation.11 | loop fusion | bytes 1179648 | tf_op jit(solution)/shard_map/slice | solution.py:453
  43.1 4.0 %all-to-all-done = f32[16,6,3,8,128]{4,3,2,1,0:T(8,128)S(1)} async-done(((f32[16,6,3,8,128]{4,3,2,1,0:T(8,128)}), f32[16,6,3,8,128]{4,3,2,1,0:T(8,128)S(1)}, u32[]{:S(2)}, u32[]{:S(2)}) %all-to-all-start) | async-done | bytes 1179680 | tf_op jit(solution)/shard_map/all_to_all | solution.py:440
  47.1 0.1 reduce_sum.9
  47.2 0.4 collective-permute-done.lo_ref
  47.6 0.0 collective-permute-done.1.hi_ref
  47.6 1.3 %collective-permute-start.2 = (f32[4,6,3,8,128]{4,3,2,1,0:T(8,128)S(1)}, f32[4,6,3,8,128]{4,3,2,1,0:T(8,128)S(1)}, u32[]{:S(2)}, u32[]{:S(2)}) collective-permute-start(f32[4,6,3,8,128]{4,3,2,1,0:T(8,128)S(1)} %reduce_sum.9), channel_id=1, source_target_pairs={{16,0},{17,1},{18,2},{19,3},{20,4},{21,5},{22,6},{23,7},{24,8},{25... | collective-permute-start | bytes 884744 | tf_op jit(solution)/shard_map/ppermute | solution.py:447
  48.9 3.4 %collective-permute-start.6 = (f32[6,3,32,128]{3,2,1,0:T(8,128)S(1)}, f32[6,3,32,128]{3,2,1,0:T(8,128)S(1)}, u32[]{:S(2)}, u32[]{:S(2)}) collective-permute-start(f32[6,3,32,128]{3,2,1,0:T(8,128)S(1)} %get-tuple-element.24), channel_id=1, source_target_pairs={{0,4},{4,8},{8,12},{12,16},{16,20},{20,24},{24,28},{1,5},{5,9},{9,... | collective-permute-start | bytes 884744 | tf_op jit(solution)/shard_map/ppermute | solution.py:459
  52.3 1.3 %collective-permute-start.7 = (f32[6,3,32,128]{3,2,1,0:T(8,128)S(1)}, f32[6,3,32,128]{3,2,1,0:T(8,128)S(1)}, u32[]{:S(2)}, u32[]{:S(2)}) collective-permute-start(f32[6,3,32,128]{3,2,1,0:T(8,128)S(1)} %get-tuple-element.25), channel_id=1, source_target_pairs={{4,0},{8,4},{12,8},{16,12},{20,16},{24,20},{28,24},{5,1},{9,5},{13... | collective-permute-start | bytes 884744 | tf_op jit(solution)/shard_map/ppermute | solution.py:460
  53.6 10.4 %span_sweep.1 = f32[6,512,128]{2,1,0:T(8,128)} custom-call(f32[6,512,128]{2,1,0:T(8,128)} %bitcast.23, f32[3,6,16,128]{3,2,1,0:T(8,128)S(1)} %collective-permute-done.lo_ref, f32[3,6,16,128]{3,2,1,0:T(8,128)S(1)} %collective-permute-done.1.hi_ref, f32[6,512,128]{2,1,0:T(8,128)} %wall_sweep.1), custom_call_target="tpu_custom_call" | custom-call | flops 275251200 | bytes 3145728 | tf_op jit(solution)/shard_map/span_sweep/pallas_call | solution.py:207
  64.0 2.6 %collective-permute-done.2 = f32[4,6,3,8,128]{4,3,2,1,0:T(8,128)S(1)} collective-permute-done((f32[4,6,3,8,128]{4,3,2,1,0:T(8,128)S(1)}, f32[4,6,3,8,128]{4,3,2,1,0:T(8,128)S(1)}, u32[]{:S(2)}, u32[]{:S(2)}) %collective-permute-start.2) | collective-permute-done | bytes 294944 | tf_op jit(solution)/shard_map/ppermute | solution.py:447
  66.6 1.3 %collective-permute-start.5 = (f32[4,6,3,8,128]{4,3,2,1,0:T(8,128)S(1)}, f32[4,6,3,8,128]{4,3,2,1,0:T(8,128)S(1)}, u32[]{:S(2)}, u32[]{:S(2)}) collective-permute-start(f32[4,6,3,8,128]{4,3,2,1,0:T(8,128)S(1)} %add.16.refs_0_), channel_id=1, source_target_pairs={{12,0},{13,1},{14,2},{15,3}} | collective-permute-start | bytes 884744 | tf_op jit(solution)/shard_map/ppermute | solution.py:464
  67.9 1.3 %collective-permute-start.4 = (f32[4,6,3,8,128]{4,3,2,1,0:T(8,128)S(1)}, f32[4,6,3,8,128]{4,3,2,1,0:T(8,128)S(1)}, u32[]{:S(2)}, u32[]{:S(2)}) collective-permute-start(f32[4,6,3,8,128]{4,3,2,1,0:T(8,128)S(1)} %add.16.refs_0_), channel_id=1, source_target_pairs={{8,0},{9,1},{10,2},{11,3}} | collective-permute-start | bytes 884744 | tf_op jit(solution)/shard_map/ppermute | solution.py:464
  69.2 1.3 %collective-permute-start.3 = (f32[4,6,3,8,128]{4,3,2,1,0:T(8,128)S(1)}, f32[4,6,3,8,128]{4,3,2,1,0:T(8,128)S(1)}, u32[]{:S(2)}, u32[]{:S(2)}) collective-permute-start(f32[4,6,3,8,128]{4,3,2,1,0:T(8,128)S(1)} %add.16.refs_0_), channel_id=1, source_target_pairs={{4,0},{5,1},{6,2},{7,3}} | collective-permute-start | bytes 884744 | tf_op jit(solution)/shard_map/ppermute | solution.py:464
  70.5 0.0 collective-permute-done.6.lo_ref
  70.5 0.0 collective-permute-done.7.hi_ref
  70.5 8.8 %stream_sweep.1.refs_4_ = f32[6,16,32,128]{3,2,1,0:T(8,128)} custom-call(s32[2]{0:T(128)S(1)} %add_convert_fusion.after.flags, f32[16]{0:T(128)S(1)} %compare_select_fusion.strength, f32[6,16,32,128]{3,2,1,0:T(8,128)} %q_ref.1, f32[6,3,32,128]{3,2,1,0:T(8,128)S(1)} %collective-permute-done.6.lo_ref, f32[6,3,32,128]{3,2,1,0:T(8,128)S(1)} %collective-permute-done.7.hi_ref, ...), custom_call_target="tpu_custom_call" | custom-call | flops 275251200 | bytes 3145728 | tf_op jit(solution)/shard_map/stream_sweep/pallas_call | solution.py:215
  79.4 0.0 collective-permute-done.5.refs_3_
  79.4 0.0 collective-permute-done.4.refs_2_
  79.4 4.1 %collective-permute-done.3.refs_1_ = f32[4,6,3,8,128]{4,3,2,1,0:T(8,128)S(1)} collective-permute-done((f32[4,6,3,8,128]{4,3,2,1,0:T(8,128)S(1)}, f32[4,6,3,8,128]{4,3,2,1,0:T(8,128)S(1)}, u32[]{:S(2)}, u32[]{:S(2)}) %collective-permute-start.3) | collective-permute-done | bytes 294944 | tf_op jit(solution)/shard_map/ppermute | solution.py:464
  83.5 3.7 %force.1 = f32[6,16,32,128]{3,2,1,0:T(8,128)} custom-call(s32[1]{0:T(128)} %bitcast.offset, f32[16]{0:T(128)S(1)} %compare_select_fusion.strength, f32[4,6,3,8,128]{4,3,2,1,0:T(8,128)S(1)} %add.16.refs_0_, f32[4,6,3,8,128]{4,3,2,1,0:T(8,128)S(1)} %collective-permute-done.3.refs_1_, ...), custom_call_target="tpu_custom_call", output_to_operand_aliasing={{}: (6, {})} | custom-call | tf_op jit(solution)/shard_map/force/pallas_call | solution.py:406
  (5 shorter events, 0.1 us)
Async XLA Ops:
  22.7 6.5 %copy-start = (f32[6,16,32,128]{3,2,1,0:T(8,128)S(1)}, f32[6,16,32,128]{3,2,1,0:T(8,128)}, u32[]{:S(2)}) copy-start(f32[6,16,32,128]{3,2,1,0:T(8,128)} %q_ref.1) | copy-start | bytes 4718596
  22.7 24.4 %all-to-all-start = ((f32[16,6,3,8,128]{4,3,2,1,0:T(8,128)}), f32[16,6,3,8,128]{4,3,2,1,0:T(8,128)S(1)}, u32[]{:S(2)}, u32[]{:S(2)}) async-start(f32[16,6,3,8,128]{4,3,2,1,0:T(8,128)} %bitcast.4), calls=%async_computation | async-start | bytes 2359296 | tf_op jit(solution)/shard_map/all_to_all | solution.py:440
  30.1 17.5 %collective-permute-start = (f32[3,6,16,128]{3,2,1,0:T(8,128)S(1)}, f32[3,6,16,128]{3,2,1,0:T(8,128)S(1)}, u32[]{:S(2)}, u32[]{:S(2)}) collective-permute-start(f32[3,6,16,128]{3,2,1,0:T(8,128)S(1)} %pad_maximum_fusion), channel_id=1, source_target_pairs={{0,1},{1,2},{2,3},{3,0},{4,5},{5,6},{6,7},{7,4},{8,9},{9,10},{10,1... | collective-permute-start | bytes 442376 | tf_op jit(solution)/shard_map/ppermute | solution.py:455
  30.6 17.0 %collective-permute-start.1 = (f32[3,6,16,128]{3,2,1,0:T(8,128)S(1)}, f32[3,6,16,128]{3,2,1,0:T(8,128)S(1)}, u32[]{:S(2)}, u32[]{:S(2)}) collective-permute-start(f32[3,6,16,128]{3,2,1,0:T(8,128)S(1)} %pad_maximum_fusion.1), channel_id=1, source_target_pairs={{1,0},{2,1},{3,2},{0,3},{5,4},{6,5},{7,6},{4,7},{9,8},{10,9},{11,1... | collective-permute-start | bytes 442376 | tf_op jit(solution)/shard_map/ppermute | solution.py:456
  47.6 19.0 %collective-permute-start.2 = (f32[4,6,3,8,128]{4,3,2,1,0:T(8,128)S(1)}, f32[4,6,3,8,128]{4,3,2,1,0:T(8,128)S(1)}, u32[]{:S(2)}, u32[]{:S(2)}) collective-permute-start(f32[4,6,3,8,128]{4,3,2,1,0:T(8,128)S(1)} %reduce_sum.9), channel_id=1, source_target_pairs={{16,0},{17,1},{18,2},{19,3},{20,4},{21,5},{22,6},{23,7},{24,8},{25... | collective-permute-start | bytes 884744 | tf_op jit(solution)/shard_map/ppermute | solution.py:447
  48.9 21.7 %collective-permute-start.6 = (f32[6,3,32,128]{3,2,1,0:T(8,128)S(1)}, f32[6,3,32,128]{3,2,1,0:T(8,128)S(1)}, u32[]{:S(2)}, u32[]{:S(2)}) collective-permute-start(f32[6,3,32,128]{3,2,1,0:T(8,128)S(1)} %get-tuple-element.24), channel_id=1, source_target_pairs={{0,4},{4,8},{8,12},{12,16},{16,20},{20,24},{24,28},{1,5},{5,9},{9,... | collective-permute-start | bytes 884744 | tf_op jit(solution)/shard_map/ppermute | solution.py:459
  52.3 18.3 %collective-permute-start.7 = (f32[6,3,32,128]{3,2,1,0:T(8,128)S(1)}, f32[6,3,32,128]{3,2,1,0:T(8,128)S(1)}, u32[]{:S(2)}, u32[]{:S(2)}) collective-permute-start(f32[6,3,32,128]{3,2,1,0:T(8,128)S(1)} %get-tuple-element.25), channel_id=1, source_target_pairs={{4,0},{8,4},{12,8},{16,12},{20,16},{24,20},{28,24},{5,1},{9,5},{13... | collective-permute-start | bytes 884744 | tf_op jit(solution)/shard_map/ppermute | solution.py:460
  66.6 12.8 %collective-permute-start.5 = (f32[4,6,3,8,128]{4,3,2,1,0:T(8,128)S(1)}, f32[4,6,3,8,128]{4,3,2,1,0:T(8,128)S(1)}, u32[]{:S(2)}, u32[]{:S(2)}) collective-permute-start(f32[4,6,3,8,128]{4,3,2,1,0:T(8,128)S(1)} %add.16.refs_0_), channel_id=1, source_target_pairs={{12,0},{13,1},{14,2},{15,3}} | collective-permute-start | bytes 884744 | tf_op jit(solution)/shard_map/ppermute | solution.py:464
  67.9 11.5 %collective-permute-start.4 = (f32[4,6,3,8,128]{4,3,2,1,0:T(8,128)S(1)}, f32[4,6,3,8,128]{4,3,2,1,0:T(8,128)S(1)}, u32[]{:S(2)}, u32[]{:S(2)}) collective-permute-start(f32[4,6,3,8,128]{4,3,2,1,0:T(8,128)S(1)} %add.16.refs_0_), channel_id=1, source_target_pairs={{8,0},{9,1},{10,2},{11,3}} | collective-permute-start | bytes 884744 | tf_op jit(solution)/shard_map/ppermute | solution.py:464
  69.2 14.3 %collective-permute-start.3 = (f32[4,6,3,8,128]{4,3,2,1,0:T(8,128)S(1)}, f32[4,6,3,8,128]{4,3,2,1,0:T(8,128)S(1)}, u32[]{:S(2)}, u32[]{:S(2)}) collective-permute-start(f32[4,6,3,8,128]{4,3,2,1,0:T(8,128)S(1)} %add.16.refs_0_), channel_id=1, source_target_pairs={{4,0},{5,1},{6,2},{7,3}} | collective-permute-start | bytes 884744 | tf_op jit(solution)/shard_map/ppermute | solution.py:464

commit v4 on v3

--- a/solution.py
+++ b/solution.py
@@ -179,9 +179,9 @@
     return pltpu.with_memory_space_constraint(x, pltpu.HBM)
 
 
-def call(kernel, name, q, grid, in_specs, out_spec, shapes):
+def call(kernel, name, q, grid, in_specs, out_spec, shapes, place=pltpu.HBM):
     return pl.pallas_call(
-        kernel, out_shape=pltpu.HBM(q.shape, F32), name=name, grid=(grid,), in_specs=in_specs, out_specs=out_spec,
+        kernel, out_shape=place(q.shape, F32), name=name, grid=(grid,), in_specs=in_specs, out_specs=out_spec,
         scratch_shapes=shapes, compiler_params=pltpu.CompilerParams(vmem_limit_bytes=16 * 2**20),
         cost_estimate=pl.CostEstimate(flops=q.size * 700, bytes_accessed=q.size * 8, transcendentals=q.size * 2),
     )
@@ -212,8 +212,11 @@
     _, nx, nz, ny = q.shape
     cells = pl.BlockSpec((6, nx, SUB, ny), lambda t: (0, 0, t, 0))
     side = pl.BlockSpec((6, 3, SUB, ny), lambda t: (0, 0, t, 0))
-    return call(stream_kernel, "stream_sweep", q, nz // SUB, [SCALARS, SCALARS, cells, side, side, cells], cells, scratch(nx))(
+    return call(stream_kernel, "stream_sweep", q, nz // SUB, [SCALARS, SCALARS, cells, side, side, cells], cells, scratch(nx), pltpu.VMEM)(
         edges, strength, far(q), xlo, xhi, far(acc))
+
+
+BIT = 32
 
 
 def span_tables(modes, points):
@@ -223,7 +226,7 @@
     return jnp.asarray(np.concatenate([np.concatenate([cz, sz], 1), np.concatenate([-sz, cz], 1)], 0), F32).astype(BF16)
 
 
-def feed_kernel(first, count, chunk, depth, rows, stream_points, scalars, z_far, coeff_ref, out_ref, z_ref, buf, left_ref, rhs_a, rhs_b, acc_ref, sems):
+def feed_kernel(first, count, chunk, depth, rows, stream_points, base, stations, z_far, coeff_ref, out_ref, z_ref, buf, left_ref, rhs_a, rhs_b, acc_ref, sems):
     _, modes_x, _, levels, modes = coeff_ref.shape
     groups = levels // SUB
     points = z_far.shape[1] // 2
@@ -231,6 +234,7 @@
     total = count * steps
     width = chunk * SUB
     sub = min(8, chunk)
+    bit = min(BIT, chunk)
 
     def copies(n, slot):
         k, v = lax.rem(n, steps) * chunk, first + lax.div(n, steps)
@@ -240,23 +244,21 @@
 
     table = pltpu.make_async_copy(z_far, z_ref, sems.at[depth, 0])
     table.start()
-    for n in range(min(depth - 1, total)):
+    pieces = [
+        [
+            pltpu.make_async_copy(
+                coeff_ref.at[c, i * bit : (i + 1) * bit, first], buf.at[0, c, i * bit : (i + 1) * bit], sems.at[depth + 1 + i, c]
+            )
+            for c in range(2)
+        ]
+        for i in range(chunk // bit)
+    ]
+    for pair in pieces:
+        for copy in pair:
+            copy.start()
+    for n in range(1, min(depth, total)):
         for copy in copies(n, n):
             copy.start()
-
-    plane = lax.broadcasted_iota(jnp.int32, (rows, width), 0)
-    mode = scalars[0] + lax.broadcasted_iota(jnp.int32, (rows, width), 1) // SUB
-    station = jnp.zeros((rows, width), jnp.int32)
-    for f in range(scalars.shape[0] - 1):
-        station = jnp.where(plane == f, scalars[1 + f], station)
-    own = lax.broadcasted_iota(jnp.int32, (rows, SUB, width), 2) % SUB == lax.broadcasted_iota(
-        jnp.int32, (rows, SUB, width), 1
-    )
-    for k in range(steps):
-        angle = (2.0 * math.pi / stream_points) * ((station * (mode + k * chunk)) % stream_points).astype(F32)
-        for c, factor in enumerate((jnp.cos(angle), -jnp.sin(angle))):
-            spread = jnp.where(own, factor[:, None, :], 0.0)
-            left_ref[k, :, c * width : (c + 1) * width] = spread.reshape(rows * SUB, width).astype(BF16)
 
     def fetch(n):
         slot = lax.rem(n, depth)
@@ -271,8 +273,11 @@
             copy.wait()
         return slot
 
-    def span(slot, rhs_ref):
+    def span(slot, rhs_ref, pieces=()):
         for i in range(0, chunk, sub):
+            if pieces and i % bit == 0:
+                for copy in pieces[i // bit]:
+                    copy.wait()
             both = jnp.concatenate([buf[slot, c, i : i + sub].reshape(sub * levels, modes) for c in range(2)], axis=1)
             prod = jnp.dot(both, z_ref[...], preferred_element_type=F32).reshape(sub, groups, SUB, 2 * points)
             for g in range(groups):
@@ -316,7 +321,20 @@
         give(n - 1)
 
     table.wait()
-    span(fetch(0), rhs_a)
+    span(0, rhs_a, pieces)
+    plane = lax.broadcasted_iota(jnp.int32, (rows, width), 0)
+    mode = base[0] + lax.broadcasted_iota(jnp.int32, (rows, width), 1) // SUB
+    station = jnp.zeros((rows, width), jnp.int32)
+    for f in range(stations.shape[0]):
+        station = jnp.where(plane == f, stations[f], station)
+    own = lax.broadcasted_iota(jnp.int32, (rows, SUB, width), 2) % SUB == lax.broadcasted_iota(
+        jnp.int32, (rows, SUB, width), 1
+    )
+    for k in range(steps):
+        angle = (2.0 * math.pi / stream_points) * ((station * (mode + k * chunk)) % stream_points).astype(F32)
+        for c, factor in enumerate((jnp.cos(angle), -jnp.sin(angle))):
+            spread = jnp.where(own, factor[:, None, :], 0.0)
+            left_ref[k, :, c * width : (c + 1) * width] = spread.reshape(rows * SUB, width).astype(BF16)
 
     @pl.loop(0, (total - 1) // 2)
     def _(m):
@@ -331,7 +349,7 @@
     give(total - 1)
 
 
-def feed(coeff, scalars, rows, stream_points, table, first, count, blocks, parts, chunk, depth):
+def feed(coeff, base, stations, rows, stream_points, table, first, count, blocks, parts, chunk, depth):
     _, modes_x, _, levels, modes = coeff.shape
     points = table.shape[1] // 2
     groups = levels // SUB
@@ -343,7 +361,7 @@
     return pl.pallas_call(
         functools.partial(feed_kernel, first, count, chunk, depth, rows, stream_points), name="feed",
         out_shape=jax.ShapeDtypeStruct((blocks, parts, count, tiles, points // parts // blocks, LANE), F32),
-        in_specs=[SCALARS, pl.BlockSpec(memory_space=pl.ANY), pl.BlockSpec(memory_space=pl.ANY)], out_specs=vmem,
+        in_specs=[SCALARS, SCALARS, pl.BlockSpec(memory_space=pl.ANY), pl.BlockSpec(memory_space=pl.ANY)], out_specs=vmem,
         scratch_shapes=[
             pltpu.VMEM(table.shape, BF16),
             pltpu.VMEM((depth, 2, chunk, levels, modes), BF16),
@@ -351,65 +369,54 @@
             pltpu.VMEM((2 * chunk * SUB, groups * points), BF16),
             pltpu.VMEM((2 * chunk * SUB, groups * points), BF16),
             pltpu.VMEM((rows * SUB, groups * points), F32),
-            pltpu.SemaphoreType.DMA((depth + 1, 2)),
+            pltpu.SemaphoreType.DMA((depth + 1 + chunk // min(BIT, chunk), 2)),
         ],
         compiler_params=pltpu.CompilerParams(vmem_limit_bytes=24 * 2**20),
         cost_estimate=pl.CostEstimate(flops=flops, bytes_accessed=2 * count * modes_x * levels * modes * 2, transcendentals=0),
-    )(scalars, far(table), coeff)
-
-
-def force_kernel(steps, per, levels, owners, offset, strength, *refs):
-    far, state, out_ref = refs[:owners], refs[owners], refs[owners + 1]
-    near, cells, sems = refs[owners + 2 : 2 * owners + 2], refs[-2], refs[-1]
-    parts, variables, tiles, short, _ = near[0].shape
-
-    def planes(t):
-        return pl.ds(t * per, per)
-
-    loads = [pltpu.make_async_copy(far[b], near[b], sems.at[b]) for b in range(owners)]
-    reads = [pltpu.make_async_copy(state.at[:, planes(t)], cells.at[:, planes(t)], sems.at[owners + t]) for t in range(steps)]
-    writes = [
-        pltpu.make_async_copy(cells.at[:, planes(t)], out_ref.at[:, planes(t)], sems.at[owners + steps + t])
-        for t in range(steps)
-    ]
-    for copy in loads + reads:
-        copy.start()
-    for copy in loads:
-        copy.wait()
+    )(base, stations, far(table), coeff)
+
+
+def force_kernel(steps, per, levels, where, offset, strength, *refs):
+    *near, state, out_ref, cells, sems = refs
+    parts, _, tiles, short, _ = near[0].shape
+    variables = state.shape[0]
+    forced = steps * per
+    copies = []
+    if forced < state.shape[1]:
+        copies.append(pltpu.make_async_copy(state.at[:, forced:], out_ref.at[:, forced:], sems.at[steps]))
+        copies[0].start()
     lane = lax.broadcasted_iota(jnp.int32, (short, LANE), 1)
     for t in range(steps):
-        reads[t].wait()
         tile = jnp.minimum(t + offset[0], tiles - 1)
-
         for v in range(variables):
-            for b in range(owners):
-                blocks = [near[b][s, v, tile] for s in range(parts)]
+            for b, places in enumerate(where):
+                source, row = places[v]
+                blocks = [near[source][s, row, tile] for s in range(parts)]
                 for i in range(per):
                     row = blocks[0] if i == 0 else pltpu.roll(blocks[0], (-i * levels) % LANE, 1)
                     for s in range(1, parts):
                         moved = blocks[s] if s == i else pltpu.roll(blocks[s], ((s - i) * levels) % LANE, 1)
                         row = jnp.where(lane >= s * levels, moved, row)
                     some = pl.ds(b * short, short)
-                    cells[v, t * per + i, some] = cells[v, t * per + i, some] + (0.05 * strength[t * per + i]) * row
-
-        writes[t].start()
-    for copy in writes:
+                    cells[v, t * per + i, some] = state[v, t * per + i, some] + (0.05 * strength[t * per + i]) * row
+        planes = pl.ds(t * per, per)
+        copies.append(pltpu.make_async_copy(cells.at[:, planes], out_ref.at[:, planes], sems.at[t]))
+        copies[-1].start()
+    for copy in copies:
         copy.wait()
 
 
-def force(state, targets, strength, offset, levels, planes):
+def force(state, targets, where, strength, offset, levels, planes):
     variables, nx, nz, ny = state.shape
     per = LANE // levels
     steps = -(-min(planes, nx) // per)
     owners = len(targets)
-    anywhere = pl.BlockSpec(memory_space=pl.ANY)
+    vmem = pl.BlockSpec(memory_space=pltpu.VMEM)
     return pl.pallas_call(
-        functools.partial(force_kernel, steps, per, levels, owners), name="force",
+        functools.partial(force_kernel, steps, per, levels, where), name="force",
         out_shape=jax.ShapeDtypeStruct(state.shape, F32),
-        in_specs=[SCALARS, SCALARS] + [anywhere] * (owners + 1), out_specs=anywhere,
-        scratch_shapes=[pltpu.VMEM(t.shape, F32) for t in targets]
-        + [pltpu.VMEM((variables, steps * per, nz, ny), F32), pltpu.SemaphoreType.DMA((owners + 2 * steps,))],
-        input_output_aliases={2 + owners: 0},
+        in_specs=[SCALARS, SCALARS] + [vmem] * (owners + 1), out_specs=pl.BlockSpec(memory_space=pl.ANY),
+        scratch_shapes=[pltpu.VMEM((variables, steps * per, nz, ny), F32), pltpu.SemaphoreType.DMA((steps + 1,))],
         compiler_params=pltpu.CompilerParams(vmem_limit_bytes=16 * 2**20),
     )(offset, strength, *targets, state)
 
@@ -427,7 +434,7 @@
 
     per = LANE // levels
     rows = -(-planes // per) * per
-    scalars = jnp.concatenate([jnp.reshape(me * modes_x, (1,)), feed_plane])
+    base = jnp.reshape(me * modes_x, (1,))
     ring = [(i, (i + 1) % parts) for i in range(parts)]
     line = [(i, i + 1) for i in range(gx - 1)]
     table = span_tables(modes, nz * parts)
@@ -440,15 +447,25 @@
         part = lax.all_to_all(part, ("gl", "gz"), split_axis=0, concat_axis=0, tiled=True)
         return part.reshape(low, parts, *part.shape[1:]).sum(0)
 
+    relay = low == 4 and high > 1 and high & (high - 1) == 0 and variables % 2 == 0
+    half = variables // 2
+
     def gather(part):
         stride = 1
-        while stride < high:
+        while stride < (high // 2 if relay else high):
             hops = [(i, i - stride) for i in range(stride, high, 2 * stride)]
             part = part + lax.ppermute(part, "gh", hops)
             stride *= 2
-        return part
-
-    part = feed(coeff, scalars, rows, 2 * modes_x * gx, table, 0, variables, low, parts, 64, 3)
+        if not relay:
+            return part
+        top = stride * low
+        upper = lax.axis_index("gh") == stride
+        main = lax.ppermute(part, GX, [(top + i, i) for i in range(3)])
+        left = lax.ppermute(jnp.where(upper, part[:, half:], part[:, :half]), GX, [(3, 1), (top + 3, 2)])
+        right = lax.ppermute(jnp.where(upper, part[:, :half], part[:, half:]), GX, [(3, 2), (top + 3, 1)])
+        return part + main, left + right
+
+    part = feed(coeff, base, feed_plane, rows, 2 * modes_x * gx, table, 0, variables, low, parts, 64, 3)
     part, edges, late = lax.optimization_barrier((part, edges, state))
     slabs = [late[:, nx - 3 :], late[:, :3]] + [jnp.stack([late[:, :, k + j] for j in range(3)]) for k in (nz - 3, 0)]
     part = spread(part)
@@ -461,12 +478,19 @@
     part = gather(part)
     acc = span_sweep(state, zlo, zhi, acc)
     part, acc = lax.optimization_barrier((part, acc))
-    owned = [part] + [lax.ppermute(part, GX, [(i, 0)]) for i in range(1, low)]
+    if relay:
+        part, extra = part
+        owned = [part] + [lax.ppermute(t, GX, [(i, 0)]) for t in (part, extra) for i in (1, 2)]
+    else:
+        owned = [part] + [lax.ppermute(part, GX, [(i, 0)]) for i in range(1, low)]
     new = stream_sweep(state, xlo, xhi, acc, edges, strength)
     for other in range(1, -(-planes // nx)):
         owned = [jnp.where(me == other, lax.ppermute(t, GX, [(0, other)]), t) for t in owned]
     offset = jnp.reshape(me * nx // per, (1,))
-    return force(new, owned, strength, offset, levels, planes)
+    where = [[(b, v) for v in range(variables)] for b in range(low)]
+    if relay:
+        where[3] = [(3 + v // half, v % half) for v in range(variables)]
+    return force(new, owned, where, strength, offset, levels, planes)
 
 
 def solution(mesh):

time: 87.6 us -> 84.7 us (0.967)
  waiting for transfers between devices: 11.1 us -> 6.2 us
  starting transfers between devices: 18.1 us -> 22 us
  Pallas kernels: 54.8 us -> 52.9 us
    ppermute x4 -> x7, waiting for transfers between devices: 6.69 us -> 1.79 us  [the longest x4 1.78 us: local(): lax.ppermute(t, GX, [(i, 0)])]
    ppermute x4 -> x7, starting transfers between devices: 5.16 us -> 7.79 us  [the longest x4 5.17 us: local(): lax.ppermute(t, GX, [(i, 0)])]
    pallas_call x1, Pallas kernels: 3.74 us -> 2.3 us  [force(): pl.pallas_call(functools.partial(force_kernel, steps, per, levels, where)...]
    ppermute x1, starting transfers between devices: 3.39 us -> 4.63 us  [local(): xlo = lax.ppermute(slabs[0], GX, line)]
  transfers between devices with their start and end apart: 9 -> 12, of which waited for: 4 -> 4; matrix products, arithmetic and copies ran while one was open for 2% -> 3% of each run, Pallas kernels for 34% -> 34%
where the time goes in v4:
time: 84.7 us; the launch traced here: 84.3 us
  Pallas kernels  52.9 us (62%)
  starting transfers between devices  22 us (26%)
  waiting for transfers between devices  6.2 us (7%)
  local copies, waits for them, and re-layouts  2.69 us (3%)
    pallas_call x1, Pallas kernels, feed(): pl.pallas_call(functools.partial(feed_kernel, first, count, chunk, depth,...  21.9 us
    pallas_call x1, Pallas kernels, span_sweep(): call(functools.partial(span_kernel, nz), 'span_sweep', flat, nx // SUB, [...  10.4 us
    pallas_call x1, Pallas kernels, wall_sweep(): call(wall_kernel, 'wall_sweep', flat, nx * nz // LANE, [SCALARS, cells],...  10 us
    pallas_call x1, Pallas kernels, stream_sweep(): call(stream_kernel, 'stream_sweep', q, nz // SUB, [SCALARS, SCALARS, cell...  8.25 us
    all_to_all x1, starting transfers between devices, spread(): lax.all_to_all(part, ('gl', 'gz'), split_axis=0, concat_axis=0, tiled=True)  6.43 us
    ppermute x4, starting transfers between devices, local(): lax.ppermute(t, GX, [(i, 0)])  5.17 us
    ppermute x1, starting transfers between devices, local(): xlo = lax.ppermute(slabs[0], GX, line)  4.63 us
    all_to_all x1, waiting for transfers between devices, spread(): lax.all_to_all(part, ('gl', 'gz'), split_axis=0, concat_axis=0, tiled=True)  4.02 us
  transfers between devices with their start and end apart: 12, of which 4 were waited for; matrix products, arithmetic and copies ran while one was open for 3% of the time, Pallas kernels for 34%

profile of v4, /device:TPU:0, one launch (start us, length us, event | category | flops | bytes accessed | tf_op | source)
XLA Modules:
  0.0 84.3 jit_solution(4773531707750262398)
XLA Ops:
  0.0 0.1 add_convert_fusion.after.flags
  0.1 0.7 copy-done
  0.7 21.9 %feed.1 = f32[4,4,6,3,8,128]{5,4,3,2,1,0:T(8,128)} custom-call(s32[1]{0:T(128)} %bitcast.1.base, s32[12]{0:T(128)S(1)} %copy-done, bf16[1024,256]{1,0:T(8,128)(2,1)} %constant.50.z_far, bf16[2,128,6,32,512]{4,3,2,1,0:T(8,128)(2,1)} %coeff_ref.1), custom_call_target="tpu_custom_call" | custom-call | flops 14092861440 | bytes 50331648 | tf_op jit(solution)/shard_map/feed/pallas_call | solution.py:361
  22.6 0.0 copy-start.1
  22.6 6.4 %all-to-all-start = ((f32[16,6,3,8,128]{4,3,2,1,0:T(8,128)}), f32[16,6,3,8,128]{4,3,2,1,0:T(8,128)S(1)}, u32[]{:S(2)}, u32[]{:S(2)}) async-start(f32[16,6,3,8,128]{4,3,2,1,0:T(8,128)} %bitcast.4), calls=%async_computation | async-start | bytes 2359296 | tf_op jit(solution)/shard_map/all_to_all | solution.py:447
  29.1 0.9 %copy.5 = f32[6,16,32,128]{3,1,0,2:T(8,128)S(1)} copy(f32[6,16,32,128]{3,2,1,0:T(8,128)S(1)} %copy-done.1) | data formatting | bytes 3145728 | tf_op jit(solution)/shard_map/optimization_barrier | solution.py:469
  30.1 0.5 collective-permute-start
  30.5 1.4 %collective-permute-start.1 = (f32[3,6,16,128]{3,2,1,0:T(8,128)S(1)}, f32[3,6,16,128]{3,2,1,0:T(8,128)S(1)}, u32[]{:S(2)}, u32[]{:S(2)}) collective-permute-start(f32[3,6,16,128]{3,2,1,0:T(8,128)S(1)} %pad_maximum_fusion.1), channel_id=1, source_target_pairs={{1,0},{2,1},{3,2},{0,3},{5,4},{6,5},{7,6},{4,7},{9,8},{10,9},{11,1... | collective-permute-start | bytes 442376 | tf_op jit(solution)/shard_map/ppermute | solution.py:473
  31.9 10.0 %wall_sweep.1 = f32[6,512,128]{2,1,0:T(8,128)} custom-call(s32[2]{0:T(128)S(1)} %add_convert_fusion.after.flags, f32[6,512,128]{2,1,0:T(8,128)} %bitcast.22), custom_call_target="tpu_custom_call" | custom-call | flops 275251200 | bytes 3145728 | tf_op jit(solution)/shard_map/wall_sweep/pallas_call | solution.py:198
  41.9 1.1 %fusion = (f32[6,3,32,128]{3,2,1,0:T(8,128)S(1)}, f32[6,3,32,128]{3,2,1,0:T(8,128)S(1)}) fusion(f32[6,16,32,128]{3,2,1,0:T(8,128)} %q_ref.1), kind=kLoop, calls=%fused_computation.12 | loop fusion | bytes 1179648 | tf_op jit(solution)/shard_map/slice | solution.py:470
  43.0 4.0 %all-to-all-done = f32[16,6,3,8,128]{4,3,2,1,0:T(8,128)S(1)} async-done(((f32[16,6,3,8,128]{4,3,2,1,0:T(8,128)}), f32[16,6,3,8,128]{4,3,2,1,0:T(8,128)S(1)}, u32[]{:S(2)}, u32[]{:S(2)}) %all-to-all-start) | async-done | bytes 1179680 | tf_op jit(solution)/shard_map/all_to_all | solution.py:447
  47.1 0.1 reduce_sum.9
  47.1 0.4 collective-permute-done.lo_ref
  47.5 0.0 collective-permute-done.1.hi_ref
  47.5 1.3 %collective-permute-start.2 = (f32[4,6,3,8,128]{4,3,2,1,0:T(8,128)S(1)}, f32[4,6,3,8,128]{4,3,2,1,0:T(8,128)S(1)}, u32[]{:S(2)}, u32[]{:S(2)}) collective-permute-start(f32[4,6,3,8,128]{4,3,2,1,0:T(8,128)S(1)} %reduce_sum.9), channel_id=1, source_target_pairs={{16,0},{20,4},{24,8},{17,1},{21,5},{25,9},{18,2},{22,6},{26,10},{1... | collective-permute-start | bytes 884744 | tf_op jit(solution)/shard_map/ppermute | solution.py:463
  48.9 0.7 collective-permute-start.4
  49.5 0.7 collective-permute-start.3
  50.2 4.6 %collective-permute-start.9 = (f32[6,3,32,128]{3,2,1,0:T(8,128)S(1)}, f32[6,3,32,128]{3,2,1,0:T(8,128)S(1)}, u32[]{:S(2)}, u32[]{:S(2)}) collective-permute-start(f32[6,3,32,128]{3,2,1,0:T(8,128)S(1)} %get-tuple-element.26), channel_id=1, source_target_pairs={{0,4},{4,8},{8,12},{12,16},{16,20},{20,24},{24,28},{1,5},{5,9},{9,... | collective-permute-start | bytes 884744 | tf_op jit(solution)/shard_map/ppermute | solution.py:476
  54.9 1.3 %collective-permute-start.10 = (f32[6,3,32,128]{3,2,1,0:T(8,128)S(1)}, f32[6,3,32,128]{3,2,1,0:T(8,128)S(1)}, u32[]{:S(2)}, u32[]{:S(2)}) collective-permute-start(f32[6,3,32,128]{3,2,1,0:T(8,128)S(1)} %get-tuple-element.27), channel_id=1, source_target_pairs={{4,0},{8,4},{12,8},{16,12},{20,16},{24,20},{28,24},{5,1},{9,5},{13... | collective-permute-start | bytes 884744 | tf_op jit(solution)/shard_map/ppermute | solution.py:477
  56.2 10.4 %span_sweep.1 = f32[6,512,128]{2,1,0:T(8,128)} custom-call(f32[6,512,128]{2,1,0:T(8,128)} %bitcast.23, f32[3,6,16,128]{3,2,1,0:T(8,128)S(1)} %collective-permute-done.lo_ref, f32[3,6,16,128]{3,2,1,0:T(8,128)S(1)} %collective-permute-done.1.hi_ref, f32[6,512,128]{2,1,0:T(8,128)} %wall_sweep.1), custom_call_target="tpu_custom_call" | custom-call | flops 275251200 | bytes 3145728 | tf_op jit(solution)/shard_map/span_sweep/pallas_call | solution.py:207
  66.6 0.0 collective-permute-done.4
  66.7 1.3 %collective-permute-start.6 = (f32[4,6,3,8,128]{4,3,2,1,0:T(8,128)S(1)}, f32[4,6,3,8,128]{4,3,2,1,0:T(8,128)S(1)}, u32[]{:S(2)}, u32[]{:S(2)}) collective-permute-start(f32[4,6,3,8,128]{4,3,2,1,0:T(8,128)S(1)} %add.19.refs_0_), channel_id=1, source_target_pairs={{8,0},{9,1},{10,2},{11,3}} | collective-permute-start | bytes 884744 | tf_op jit(solution)/shard_map/ppermute | solution.py:483
  68.0 1.3 %collective-permute-start.5 = (f32[4,6,3,8,128]{4,3,2,1,0:T(8,128)S(1)}, f32[4,6,3,8,128]{4,3,2,1,0:T(8,128)S(1)}, u32[]{:S(2)}, u32[]{:S(2)}) collective-permute-start(f32[4,6,3,8,128]{4,3,2,1,0:T(8,128)S(1)} %add.19.refs_0_), channel_id=1, source_target_pairs={{4,0},{5,1},{6,2},{7,3}} | collective-permute-start | bytes 884744 | tf_op jit(solution)/shard_map/ppermute | solution.py:483
  69.3 1.3 %collective-permute-start.8 = (f32[4,3,3,8,128]{4,3,2,1,0:T(8,128)S(1)}, f32[4,3,3,8,128]{4,3,2,1,0:T(8,128)S(1)}, u32[]{:S(2)}, u32[]{:S(2)}) collective-permute-start(f32[4,3,3,8,128]{4,3,2,1,0:T(8,128)S(1)} %add.20), channel_id=1, source_target_pairs={{8,0},{9,1},{10,2},{11,3}} | collective-permute-start | bytes 442376 | tf_op jit(solution)/shard_map/ppermute | solution.py:483
  70.6 0.0 collective-permute-done.9.lo_ref
  70.6 1.3 %collective-permute-start.7 = (f32[4,3,3,8,128]{4,3,2,1,0:T(8,128)S(1)}, f32[4,3,3,8,128]{4,3,2,1,0:T(8,128)S(1)}, u32[]{:S(2)}, u32[]{:S(2)}) collective-permute-start(f32[4,3,3,8,128]{4,3,2,1,0:T(8,128)S(1)} %add.20), channel_id=1, source_target_pairs={{4,0},{5,1},{6,2},{7,3}} | collective-permute-start | bytes 442376 | tf_op jit(solution)/shard_map/ppermute | solution.py:483
  71.9 8.2 %stream_sweep.1.refs_5_ = f32[6,16,32,128]{3,2,1,0:T(8,128)S(1)} custom-call(s32[2]{0:T(128)S(1)} %add_convert_fusion.after.flags, f32[16]{0:T(128)S(1)} %compare_select_fusion.strength, f32[6,16,32,128]{3,2,1,0:T(8,128)} %q_ref.1, f32[6,3,32,128]{3,2,1,0:T(8,128)S(1)} %collective-permute-done.9.lo_ref, ...), custom_call_target="tpu_custom_call" | custom-call | flops 275251200 | bytes 3145728 | tf_op jit(solution)/shard_map/stream_sweep/pallas_call | solution.py:215
  80.2 1.6 %collective-permute-done.8.refs_4_ = f32[4,3,3,8,128]{4,3,2,1,0:T(8,128)S(1)} collective-permute-done((f32[4,3,3,8,128]{4,3,2,1,0:T(8,128)S(1)}, f32[4,3,3,8,128]{4,3,2,1,0:T(8,128)S(1)}, u32[]{:S(2)}, u32[]{:S(2)}) %collective-permute-start.8) | collective-permute-done | bytes 147488 | tf_op jit(solution)/shard_map/ppermute | solution.py:483
  81.8 0.2 collective-permute-done.7.refs_3_
  82.0 0.0 collective-permute-done.6.refs_2_
  82.0 0.0 collective-permute-done.5.refs_1_
  82.0 2.3 %force.1 = f32[6,16,32,128]{3,2,1,0:T(8,128)} custom-call(s32[1]{0:T(128)} %bitcast.offset, f32[16]{0:T(128)S(1)} %compare_select_fusion.strength, f32[4,6,3,8,128]{4,3,2,1,0:T(8,128)S(1)} %add.19.refs_0_, f32[4,6,3,8,128]{4,3,2,1,0:T(8,128)S(1)} %collective-permute-done.5.refs_1_, f32[4,6,3,8,128]{4,3,2,1,0:T(8,128)S(1)} %collective-permute-done.6.refs_2_, ...), custom_call_target="tpu_custom_call" | custom-call | tf_op jit(solution)/shard_map/force/pallas_call | solution.py:415
  (12 shorter events, 0.1 us)
Async XLA Ops:
  0.1 0.7 copy-start
  22.6 6.5 %copy-start.1 = (f32[6,16,32,128]{3,2,1,0:T(8,128)S(1)}, f32[6,16,32,128]{3,2,1,0:T(8,128)}, u32[]{:S(2)}) copy-start(f32[6,16,32,128]{3,2,1,0:T(8,128)} %q_ref.1) | copy-start | bytes 4718596
  22.6 24.4 %all-to-all-start = ((f32[16,6,3,8,128]{4,3,2,1,0:T(8,128)}), f32[16,6,3,8,128]{4,3,2,1,0:T(8,128)S(1)}, u32[]{:S(2)}, u32[]{:S(2)}) async-start(f32[16,6,3,8,128]{4,3,2,1,0:T(8,128)} %bitcast.4), calls=%async_computation | async-start | bytes 2359296 | tf_op jit(solution)/shard_map/all_to_all | solution.py:447
  30.1 17.5 %collective-permute-start = (f32[3,6,16,128]{3,2,1,0:T(8,128)S(1)}, f32[3,6,16,128]{3,2,1,0:T(8,128)S(1)}, u32[]{:S(2)}, u32[]{:S(2)}) collective-permute-start(f32[3,6,16,128]{3,2,1,0:T(8,128)S(1)} %pad_maximum_fusion), channel_id=1, source_target_pairs={{0,1},{1,2},{2,3},{3,0},{4,5},{5,6},{6,7},{7,4},{8,9},{9,10},{10,1... | collective-permute-start | bytes 442376 | tf_op jit(solution)/shard_map/ppermute | solution.py:472
  30.5 17.0 %collective-permute-start.1 = (f32[3,6,16,128]{3,2,1,0:T(8,128)S(1)}, f32[3,6,16,128]{3,2,1,0:T(8,128)S(1)}, u32[]{:S(2)}, u32[]{:S(2)}) collective-permute-start(f32[3,6,16,128]{3,2,1,0:T(8,128)S(1)} %pad_maximum_fusion.1), channel_id=1, source_target_pairs={{1,0},{2,1},{3,2},{0,3},{5,4},{6,5},{7,6},{4,7},{9,8},{10,9},{11,1... | collective-permute-start | bytes 442376 | tf_op jit(solution)/shard_map/ppermute | solution.py:473
  47.5 19.1 %collective-permute-start.2 = (f32[4,6,3,8,128]{4,3,2,1,0:T(8,128)S(1)}, f32[4,6,3,8,128]{4,3,2,1,0:T(8,128)S(1)}, u32[]{:S(2)}, u32[]{:S(2)}) collective-permute-start(f32[4,6,3,8,128]{4,3,2,1,0:T(8,128)S(1)} %reduce_sum.9), channel_id=1, source_target_pairs={{16,0},{20,4},{24,8},{17,1},{21,5},{25,9},{18,2},{22,6},{26,10},{1... | collective-permute-start | bytes 884744 | tf_op jit(solution)/shard_map/ppermute | solution.py:463
  48.9 17.7 %collective-permute-start.4 = (f32[4,3,3,8,128]{4,3,2,1,0:T(8,128)S(1)}, f32[4,3,3,8,128]{4,3,2,1,0:T(8,128)S(1)}, u32[]{:S(2)}, u32[]{:S(2)}) collective-permute-start(f32[4,3,3,8,128]{4,3,2,1,0:T(8,128)S(1)} %get-tuple-element.37), channel_id=1, source_target_pairs={{12,8},{28,4},{13,9},{29,5},{14,10},{30,6},{15,11},{31,7}} | collective-permute-start | bytes 442376 | tf_op jit(solution)/shard_map/ppermute | solution.py:465
  49.5 17.1 %collective-permute-start.3 = (f32[4,3,3,8,128]{4,3,2,1,0:T(8,128)S(1)}, f32[4,3,3,8,128]{4,3,2,1,0:T(8,128)S(1)}, u32[]{:S(2)}, u32[]{:S(2)}) collective-permute-start(f32[4,3,3,8,128]{4,3,2,1,0:T(8,128)S(1)} %get-tuple-element.38), channel_id=1, source_target_pairs={{12,4},{28,8},{13,5},{29,9},{14,6},{30,10},{15,7},{31,11}} | collective-permute-start | bytes 442376 | tf_op jit(solution)/shard_map/ppermute | solution.py:464
  50.2 20.4 %collective-permute-start.9 = (f32[6,3,32,128]{3,2,1,0:T(8,128)S(1)}, f32[6,3,32,128]{3,2,1,0:T(8,128)S(1)}, u32[]{:S(2)}, u32[]{:S(2)}) collective-permute-start(f32[6,3,32,128]{3,2,1,0:T(8,128)S(1)} %get-tuple-element.26), channel_id=1, source_target_pairs={{0,4},{4,8},{8,12},{12,16},{16,20},{20,24},{24,28},{1,5},{5,9},{9,... | collective-permute-start | bytes 884744 | tf_op jit(solution)/shard_map/ppermute | solution.py:476
  54.9 17.1 %collective-permute-start.10 = (f32[6,3,32,128]{3,2,1,0:T(8,128)S(1)}, f32[6,3,32,128]{3,2,1,0:T(8,128)S(1)}, u32[]{:S(2)}, u32[]{:S(2)}) collective-permute-start(f32[6,3,32,128]{3,2,1,0:T(8,128)S(1)} %get-tuple-element.27), channel_id=1, source_target_pairs={{4,0},{8,4},{12,8},{16,12},{20,16},{24,20},{28,24},{5,1},{9,5},{13... | collective-permute-start | bytes 884744 | tf_op jit(solution)/shard_map/ppermute | solution.py:477
  66.7 15.3 %collective-permute-start.6 = (f32[4,6,3,8,128]{4,3,2,1,0:T(8,128)S(1)}, f32[4,6,3,8,128]{4,3,2,1,0:T(8,128)S(1)}, u32[]{:S(2)}, u32[]{:S(2)}) collective-permute-start(f32[4,6,3,8,128]{4,3,2,1,0:T(8,128)S(1)} %add.19.refs_0_), channel_id=1, source_target_pairs={{8,0},{9,1},{10,2},{11,3}} | collective-permute-start | bytes 884744 | tf_op jit(solution)/shard_map/ppermute | solution.py:483
  68.0 14.0 %collective-permute-start.5 = (f32[4,6,3,8,128]{4,3,2,1,0:T(8,128)S(1)}, f32[4,6,3,8,128]{4,3,2,1,0:T(8,128)S(1)}, u32[]{:S(2)}, u32[]{:S(2)}) collective-permute-start(f32[4,6,3,8,128]{4,3,2,1,0:T(8,128)S(1)} %add.19.refs_0_), channel_id=1, source_target_pairs={{4,0},{5,1},{6,2},{7,3}} | collective-permute-start | bytes 884744 | tf_op jit(solution)/shard_map/ppermute | solution.py:483
  69.3 12.5 %collective-permute-start.8 = (f32[4,3,3,8,128]{4,3,2,1,0:T(8,128)S(1)}, f32[4,3,3,8,128]{4,3,2,1,0:T(8,128)S(1)}, u32[]{:S(2)}, u32[]{:S(2)}) collective-permute-start(f32[4,3,3,8,128]{4,3,2,1,0:T(8,128)S(1)} %add.20), channel_id=1, source_target_pairs={{8,0},{9,1},{10,2},{11,3}} | collective-permute-start | bytes 442376 | tf_op jit(solution)/shard_map/ppermute | solution.py:483
  70.6 11.4 %collective-permute-start.7 = (f32[4,3,3,8,128]{4,3,2,1,0:T(8,128)S(1)}, f32[4,3,3,8,128]{4,3,2,1,0:T(8,128)S(1)}, u32[]{:S(2)}, u32[]{:S(2)}) collective-permute-start(f32[4,3,3,8,128]{4,3,2,1,0:T(8,128)S(1)} %add.20), channel_id=1, source_target_pairs={{4,0},{5,1},{6,2},{7,3}} | collective-permute-start | bytes 442376 | tf_op jit(solution)/shard_map/ppermute | solution.py:483

commit v5 on v4

--- a/solution.py
+++ b/solution.py
@@ -103,7 +103,7 @@
     ]
 
 
-def stream_kernel(flags, strength, q_ref, lo_ref, hi_ref, acc_in, out_ref, gf, gq, mx):
+def stream_kernel(flags, strength, q_ref, lo_ref, hi_ref, wall, span, out_ref, gf, gq, mx):
     nx = q_ref.shape[1]
 
     def mid(j):
@@ -124,13 +124,13 @@
         relax = (q[0] * share - q[5]) * (2.0 * p) / lag
         keep = 1.0 - 0.05 * strength[c]
         for v in range(6):
-            new = keep * q[v] - (0.05 / 12.0) * (acc_in[v, c] + total[v])
+            new = keep * q[v] - (0.05 / 12.0) * (wall[v, c] + span[v, c] + total[v])
             out_ref[v, c] = new + 0.05 * relax if v == 5 else new
 
     sweep(1, nx, side(lo_ref, flags[0], 0), mid, side(hi_ref, flags[1], nx - 1), put, gf, gq, mx)
 
 
-def span_kernel(nz, q_ref, lo_ref, hi_ref, acc_in, acc_ref, gf, gq, mx):
+def span_kernel(nz, q_ref, lo_ref, hi_ref, acc_ref, gf, gq, mx):
     def rows(j):
         return pl.ds(j, SUB, stride=nz)
 
@@ -142,7 +142,7 @@
 
     def put(c, total):
         for v in range(6):
-            acc_ref[v, rows(c), :] = acc_in[v, rows(c), :] + total[v]
+            acc_ref[v, rows(c), :] = total[v]
 
     sweep(3, nz, side(lo_ref), mid, side(hi_ref), put, gf, gq, mx)
 
@@ -199,21 +199,21 @@
         after, far(flat)).reshape(q.shape)
 
 
-def span_sweep(q, zlo, zhi, acc):
+def span_sweep(q, zlo, zhi):
     _, nx, nz, ny = q.shape
     flat = q.reshape(6, nx * nz, ny)
     cells = pl.BlockSpec((6, SUB * nz, ny), lambda t: (0, t, 0))
     side = pl.BlockSpec((3, 6, SUB, ny), lambda t: (0, 0, t, 0))
-    return call(functools.partial(span_kernel, nz), "span_sweep", flat, nx // SUB, [cells, side, side, cells], cells, scratch(nz))(
-        far(flat), zlo, zhi, far(acc.reshape(flat.shape))).reshape(q.shape)
-
-
-def stream_sweep(q, xlo, xhi, acc, edges, strength):
+    return call(functools.partial(span_kernel, nz), "span_sweep", flat, nx // SUB, [cells, side, side], cells, scratch(nz))(
+        far(flat), zlo, zhi).reshape(q.shape)
+
+
+def stream_sweep(q, xlo, xhi, wall, span, edges, strength):
     _, nx, nz, ny = q.shape
     cells = pl.BlockSpec((6, nx, SUB, ny), lambda t: (0, 0, t, 0))
     side = pl.BlockSpec((6, 3, SUB, ny), lambda t: (0, 0, t, 0))
-    return call(stream_kernel, "stream_sweep", q, nz // SUB, [SCALARS, SCALARS, cells, side, side, cells], cells, scratch(nx), pltpu.VMEM)(
-        edges, strength, far(q), xlo, xhi, far(acc))
+    return call(stream_kernel, "stream_sweep", q, nz // SUB, [SCALARS, SCALARS, cells, side, side, cells, cells], cells, scratch(nx), pltpu.VMEM)(
+        edges, strength, far(q), xlo, xhi, far(wall), far(span))
 
 
 BIT = 32
@@ -476,14 +476,14 @@
     xlo = lax.ppermute(slabs[0], GX, line)
     xhi = lax.ppermute(slabs[1], GX, [(j, i) for i, j in line])
     part = gather(part)
-    acc = span_sweep(state, zlo, zhi, acc)
-    part, acc = lax.optimization_barrier((part, acc))
+    span = span_sweep(state, zlo, zhi)
+    part, span = lax.optimization_barrier((part, span))
     if relay:
         part, extra = part
         owned = [part] + [lax.ppermute(t, GX, [(i, 0)]) for t in (part, extra) for i in (1, 2)]
     else:
         owned = [part] + [lax.ppermute(part, GX, [(i, 0)]) for i in range(1, low)]
-    new = stream_sweep(state, xlo, xhi, acc, edges, strength)
+    new = stream_sweep(state, xlo, xhi, acc, span, edges, strength)
     for other in range(1, -(-planes // nx)):
         owned = [jnp.where(me == other, lax.ppermute(t, GX, [(0, other)]), t) for t in owned]
     offset = jnp.reshape(me * nx // per, (1,))

time: 84.7 us -> 84.1 us (level)
  no operation moved by 1% of the time
where the time goes in v5:
time: 84.1 us; the launch traced here: 83.7 us
  Pallas kernels  52.4 us (62%)
  starting transfers between devices  22 us (26%)
  waiting for transfers between devices  6.15 us (7%)
  local copies, waits for them, and re-layouts  2.69 us (3%)
    pallas_call x1, Pallas kernels, feed(): pl.pallas_call(functools.partial(feed_kernel, first, count, chunk, depth,...  21.9 us
    pallas_call x1, Pallas kernels, wall_sweep(): call(wall_kernel, 'wall_sweep', flat, nx * nz // LANE, [SCALARS, cells],...  10 us
    pallas_call x1, Pallas kernels, span_sweep(): call(functools.partial(span_kernel, nz), 'span_sweep', flat, nx // SUB, [...  9.68 us
    pallas_call x1, Pallas kernels, stream_sweep(): call(stream_kernel, 'stream_sweep', q, nz // SUB, [SCALARS, SCALARS, cell...  8.47 us
    all_to_all x1, starting transfers between devices, spread(): lax.all_to_all(part, ('gl', 'gz'), split_axis=0, concat_axis=0, tiled=True)  6.43 us
    ppermute x4, starting transfers between devices, local(): lax.ppermute(t, GX, [(i, 0)])  5.17 us
    ppermute x1, starting transfers between devices, local(): xlo = lax.ppermute(slabs[0], GX, line)  4.63 us
    all_to_all x1, waiting for transfers between devices, spread(): lax.all_to_all(part, ('gl', 'gz'), split_axis=0, concat_axis=0, tiled=True)  4.02 us
  transfers between devices with their start and end apart: 12, of which 4 were waited for; matrix products, arithmetic and copies ran while one was open for 3% of the time, Pallas kernels for 34%

profile of v5, /device:TPU:0, one launch (start us, length us, event | category | flops | bytes accessed | tf_op | source)
XLA Modules:
  0.0 83.7 jit_solution(2060387952513007838)
XLA Ops:
  0.0 0.1 add_convert_fusion.after.flags
  0.1 0.7 copy-done
  0.7 21.9 %feed.1 = f32[4,4,6,3,8,128]{5,4,3,2,1,0:T(8,128)} custom-call(s32[1]{0:T(128)} %bitcast.1.base, s32[12]{0:T(128)S(1)} %copy-done, bf16[1024,256]{1,0:T(8,128)(2,1)} %constant.50.z_far, bf16[2,128,6,32,512]{4,3,2,1,0:T(8,128)(2,1)} %coeff_ref.1), custom_call_target="tpu_custom_call" | custom-call | flops 14092861440 | bytes 50331648 | tf_op jit(solution)/shard_map/feed/pallas_call | solution.py:361
  22.6 0.0 copy-start.1
  22.6 6.4 %all-to-all-start = ((f32[16,6,3,8,128]{4,3,2,1,0:T(8,128)}), f32[16,6,3,8,128]{4,3,2,1,0:T(8,128)S(1)}, u32[]{:S(2)}, u32[]{:S(2)}) async-start(f32[16,6,3,8,128]{4,3,2,1,0:T(8,128)} %bitcast.4), calls=%async_computation | async-start | bytes 2359296 | tf_op jit(solution)/shard_map/all_to_all | solution.py:447
  29.1 0.9 %copy.5 = f32[6,16,32,128]{3,1,0,2:T(8,128)S(1)} copy(f32[6,16,32,128]{3,2,1,0:T(8,128)S(1)} %copy-done.1) | data formatting | bytes 3145728 | tf_op jit(solution)/shard_map/optimization_barrier | solution.py:469
  30.1 0.5 collective-permute-start
  30.5 1.4 %collective-permute-start.1 = (f32[3,6,16,128]{3,2,1,0:T(8,128)S(1)}, f32[3,6,16,128]{3,2,1,0:T(8,128)S(1)}, u32[]{:S(2)}, u32[]{:S(2)}) collective-permute-start(f32[3,6,16,128]{3,2,1,0:T(8,128)S(1)} %pad_maximum_fusion.1), channel_id=1, source_target_pairs={{1,0},{2,1},{3,2},{0,3},{5,4},{6,5},{7,6},{4,7},{9,8},{10,9},{11,1... | collective-permute-start | bytes 442376 | tf_op jit(solution)/shard_map/ppermute | solution.py:473
  31.9 10.0 %wall_sweep.1 = f32[6,512,128]{2,1,0:T(8,128)} custom-call(s32[2]{0:T(128)S(1)} %add_convert_fusion.after.flags, f32[6,512,128]{2,1,0:T(8,128)} %bitcast.21), custom_call_target="tpu_custom_call" | custom-call | flops 275251200 | bytes 3145728 | tf_op jit(solution)/shard_map/wall_sweep/pallas_call | solution.py:198
  41.9 1.1 %fusion = (f32[6,3,32,128]{3,2,1,0:T(8,128)S(1)}, f32[6,3,32,128]{3,2,1,0:T(8,128)S(1)}) fusion(f32[6,16,32,128]{3,2,1,0:T(8,128)} %q_ref.1), kind=kLoop, calls=%fused_computation.12 | loop fusion | bytes 1179648 | tf_op jit(solution)/shard_map/slice | solution.py:470
  43.0 4.0 %all-to-all-done = f32[16,6,3,8,128]{4,3,2,1,0:T(8,128)S(1)} async-done(((f32[16,6,3,8,128]{4,3,2,1,0:T(8,128)}), f32[16,6,3,8,128]{4,3,2,1,0:T(8,128)S(1)}, u32[]{:S(2)}, u32[]{:S(2)}) %all-to-all-start) | async-done | bytes 1179680 | tf_op jit(solution)/shard_map/all_to_all | solution.py:447
  47.1 0.1 reduce_sum.9
  47.1 0.4 collective-permute-done.lo_ref
  47.5 0.0 collective-permute-done.1.hi_ref
  47.5 1.3 %collective-permute-start.2 = (f32[4,6,3,8,128]{4,3,2,1,0:T(8,128)S(1)}, f32[4,6,3,8,128]{4,3,2,1,0:T(8,128)S(1)}, u32[]{:S(2)}, u32[]{:S(2)}) collective-permute-start(f32[4,6,3,8,128]{4,3,2,1,0:T(8,128)S(1)} %reduce_sum.9), channel_id=1, source_target_pairs={{16,0},{20,4},{24,8},{17,1},{21,5},{25,9},{18,2},{22,6},{26,10},{1... | collective-permute-start | bytes 884744 | tf_op jit(solution)/shard_map/ppermute | solution.py:463
  48.9 0.7 collective-permute-start.4
  49.5 0.7 collective-permute-start.3
  50.2 4.6 %collective-permute-start.9 = (f32[6,3,32,128]{3,2,1,0:T(8,128)S(1)}, f32[6,3,32,128]{3,2,1,0:T(8,128)S(1)}, u32[]{:S(2)}, u32[]{:S(2)}) collective-permute-start(f32[6,3,32,128]{3,2,1,0:T(8,128)S(1)} %get-tuple-element.25), channel_id=1, source_target_pairs={{0,4},{4,8},{8,12},{12,16},{16,20},{20,24},{24,28},{1,5},{5,9},{9,... | collective-permute-start | bytes 884744 | tf_op jit(solution)/shard_map/ppermute | solution.py:476
  54.9 1.3 %collective-permute-start.10 = (f32[6,3,32,128]{3,2,1,0:T(8,128)S(1)}, f32[6,3,32,128]{3,2,1,0:T(8,128)S(1)}, u32[]{:S(2)}, u32[]{:S(2)}) collective-permute-start(f32[6,3,32,128]{3,2,1,0:T(8,128)S(1)} %get-tuple-element.26), channel_id=1, source_target_pairs={{4,0},{8,4},{12,8},{16,12},{20,16},{24,20},{28,24},{5,1},{9,5},{13... | collective-permute-start | bytes 884744 | tf_op jit(solution)/shard_map/ppermute | solution.py:477
  56.2 9.7 %span_sweep.1 = f32[6,512,128]{2,1,0:T(8,128)} custom-call(f32[6,512,128]{2,1,0:T(8,128)} %bitcast.22, f32[3,6,16,128]{3,2,1,0:T(8,128)S(1)} %collective-permute-done.lo_ref, f32[3,6,16,128]{3,2,1,0:T(8,128)S(1)} %collective-permute-done.1.hi_ref), custom_call_target="tpu_custom_call" | custom-call | flops 275251200 | bytes 3145728 | tf_op jit(solution)/shard_map/span_sweep/pallas_call | solution.py:207
  65.8 0.0 collective-permute-done.4
  65.9 0.6 collective-permute-done.2
  66.6 1.3 %collective-permute-start.6 = (f32[4,6,3,8,128]{4,3,2,1,0:T(8,128)S(1)}, f32[4,6,3,8,128]{4,3,2,1,0:T(8,128)S(1)}, u32[]{:S(2)}, u32[]{:S(2)}) collective-permute-start(f32[4,6,3,8,128]{4,3,2,1,0:T(8,128)S(1)} %add.19.refs_0_), channel_id=1, source_target_pairs={{8,0},{9,1},{10,2},{11,3}} | collective-permute-start | bytes 884744 | tf_op jit(solution)/shard_map/ppermute | solution.py:483
  67.9 1.3 %collective-permute-start.5 = (f32[4,6,3,8,128]{4,3,2,1,0:T(8,128)S(1)}, f32[4,6,3,8,128]{4,3,2,1,0:T(8,128)S(1)}, u32[]{:S(2)}, u32[]{:S(2)}) collective-permute-start(f32[4,6,3,8,128]{4,3,2,1,0:T(8,128)S(1)} %add.19.refs_0_), channel_id=1, source_target_pairs={{4,0},{5,1},{6,2},{7,3}} | collective-permute-start | bytes 884744 | tf_op jit(solution)/shard_map/ppermute | solution.py:483
  69.2 1.3 %collective-permute-start.8 = (f32[4,3,3,8,128]{4,3,2,1,0:T(8,128)S(1)}, f32[4,3,3,8,128]{4,3,2,1,0:T(8,128)S(1)}, u32[]{:S(2)}, u32[]{:S(2)}) collective-permute-start(f32[4,3,3,8,128]{4,3,2,1,0:T(8,128)S(1)} %add.20), channel_id=1, source_target_pairs={{8,0},{9,1},{10,2},{11,3}} | collective-permute-start | bytes 442376 | tf_op jit(solution)/shard_map/ppermute | solution.py:483
  70.5 0.0 collective-permute-done.9.lo_ref
  70.5 1.3 %collective-permute-start.7 = (f32[4,3,3,8,128]{4,3,2,1,0:T(8,128)S(1)}, f32[4,3,3,8,128]{4,3,2,1,0:T(8,128)S(1)}, u32[]{:S(2)}, u32[]{:S(2)}) collective-permute-start(f32[4,3,3,8,128]{4,3,2,1,0:T(8,128)S(1)} %add.20), channel_id=1, source_target_pairs={{4,0},{5,1},{6,2},{7,3}} | collective-permute-start | bytes 442376 | tf_op jit(solution)/shard_map/ppermute | solution.py:483
  71.8 8.5 %stream_sweep.1.refs_5_ = f32[6,16,32,128]{3,2,1,0:T(8,128)S(1)} custom-call(s32[2]{0:T(128)S(1)} %add_convert_fusion.after.flags, f32[16]{0:T(128)S(1)} %compare_select_fusion.strength, f32[6,16,32,128]{3,2,1,0:T(8,128)} %q_ref.1, f32[6,3,32,128]{3,2,1,0:T(8,128)S(1)} %collective-permute-done.9.lo_ref, ...), custom_call_target="tpu_custom_call" | custom-call | flops 275251200 | bytes 3145728 | tf_op jit(solution)/shard_map/stream_sweep/pallas_call | solution.py:215
  80.3 1.1 %collective-permute-done.8.refs_4_ = f32[4,3,3,8,128]{4,3,2,1,0:T(8,128)S(1)} collective-permute-done((f32[4,3,3,8,128]{4,3,2,1,0:T(8,128)S(1)}, f32[4,3,3,8,128]{4,3,2,1,0:T(8,128)S(1)}, u32[]{:S(2)}, u32[]{:S(2)}) %collective-permute-start.8) | collective-permute-done | bytes 147488 | tf_op jit(solution)/shard_map/ppermute | solution.py:483
  81.4 0.0 collective-permute-done.6.refs_2_
  81.4 0.0 collective-permute-done.5.refs_1_
  81.4 2.3 %force.1 = f32[6,16,32,128]{3,2,1,0:T(8,128)} custom-call(s32[1]{0:T(128)} %bitcast.offset, f32[16]{0:T(128)S(1)} %compare_select_fusion.strength, f32[4,6,3,8,128]{4,3,2,1,0:T(8,128)S(1)} %add.19.refs_0_, f32[4,6,3,8,128]{4,3,2,1,0:T(8,128)S(1)} %collective-permute-done.5.refs_1_, f32[4,6,3,8,128]{4,3,2,1,0:T(8,128)S(1)} %collective-permute-done.6.refs_2_, ...), custom_call_target="tpu_custom_call" | custom-call | tf_op jit(solution)/shard_map/force/pallas_call | solution.py:415
  (12 shorter events, 0.1 us)
Async XLA Ops:
  0.1 0.7 copy-start
  22.6 6.5 %copy-start.1 = (f32[6,16,32,128]{3,2,1,0:T(8,128)S(1)}, f32[6,16,32,128]{3,2,1,0:T(8,128)}, u32[]{:S(2)}) copy-start(f32[6,16,32,128]{3,2,1,0:T(8,128)} %q_ref.1) | copy-start | bytes 4718596
  22.6 24.4 %all-to-all-start = ((f32[16,6,3,8,128]{4,3,2,1,0:T(8,128)}), f32[16,6,3,8,128]{4,3,2,1,0:T(8,128)S(1)}, u32[]{:S(2)}, u32[]{:S(2)}) async-start(f32[16,6,3,8,128]{4,3,2,1,0:T(8,128)} %bitcast.4), calls=%async_computation | async-start | bytes 2359296 | tf_op jit(solution)/shard_map/all_to_all | solution.py:447
  30.1 17.5 %collective-permute-start = (f32[3,6,16,128]{3,2,1,0:T(8,128)S(1)}, f32[3,6,16,128]{3,2,1,0:T(8,128)S(1)}, u32[]{:S(2)}, u32[]{:S(2)}) collective-permute-start(f32[3,6,16,128]{3,2,1,0:T(8,128)S(1)} %pad_maximum_fusion), channel_id=1, source_target_pairs={{0,1},{1,2},{2,3},{3,0},{4,5},{5,6},{6,7},{7,4},{8,9},{9,10},{10,1... | collective-permute-start | bytes 442376 | tf_op jit(solution)/shard_map/ppermute | solution.py:472
  30.5 17.0 %collective-permute-start.1 = (f32[3,6,16,128]{3,2,1,0:T(8,128)S(1)}, f32[3,6,16,128]{3,2,1,0:T(8,128)S(1)}, u32[]{:S(2)}, u32[]{:S(2)}) collective-permute-start(f32[3,6,16,128]{3,2,1,0:T(8,128)S(1)} %pad_maximum_fusion.1), channel_id=1, source_target_pairs={{1,0},{2,1},{3,2},{0,3},{5,4},{6,5},{7,6},{4,7},{9,8},{10,9},{11,1... | collective-permute-start | bytes 442376 | tf_op jit(solution)/shard_map/ppermute | solution.py:473
  47.5 19.0 %collective-permute-start.2 = (f32[4,6,3,8,128]{4,3,2,1,0:T(8,128)S(1)}, f32[4,6,3,8,128]{4,3,2,1,0:T(8,128)S(1)}, u32[]{:S(2)}, u32[]{:S(2)}) collective-permute-start(f32[4,6,3,8,128]{4,3,2,1,0:T(8,128)S(1)} %reduce_sum.9), channel_id=1, source_target_pairs={{16,0},{20,4},{24,8},{17,1},{21,5},{25,9},{18,2},{22,6},{26,10},{1... | collective-permute-start | bytes 884744 | tf_op jit(solution)/shard_map/ppermute | solution.py:463
  48.9 17.0 %collective-permute-start.4 = (f32[4,3,3,8,128]{4,3,2,1,0:T(8,128)S(1)}, f32[4,3,3,8,128]{4,3,2,1,0:T(8,128)S(1)}, u32[]{:S(2)}, u32[]{:S(2)}) collective-permute-start(f32[4,3,3,8,128]{4,3,2,1,0:T(8,128)S(1)} %get-tuple-element.37), channel_id=1, source_target_pairs={{12,8},{28,4},{13,9},{29,5},{14,10},{30,6},{15,11},{31,7}} | collective-permute-start | bytes 442376 | tf_op jit(solution)/shard_map/ppermute | solution.py:465
  49.5 16.3 %collective-permute-start.3 = (f32[4,3,3,8,128]{4,3,2,1,0:T(8,128)S(1)}, f32[4,3,3,8,128]{4,3,2,1,0:T(8,128)S(1)}, u32[]{:S(2)}, u32[]{:S(2)}) collective-permute-start(f32[4,3,3,8,128]{4,3,2,1,0:T(8,128)S(1)} %get-tuple-element.38), channel_id=1, source_target_pairs={{12,4},{28,8},{13,5},{29,9},{14,6},{30,10},{15,7},{31,11}} | collective-permute-start | bytes 442376 | tf_op jit(solution)/shard_map/ppermute | solution.py:464
  50.2 20.2 %collective-permute-start.9 = (f32[6,3,32,128]{3,2,1,0:T(8,128)S(1)}, f32[6,3,32,128]{3,2,1,0:T(8,128)S(1)}, u32[]{:S(2)}, u32[]{:S(2)}) collective-permute-start(f32[6,3,32,128]{3,2,1,0:T(8,128)S(1)} %get-tuple-element.25), channel_id=1, source_target_pairs={{0,4},{4,8},{8,12},{12,16},{16,20},{20,24},{24,28},{1,5},{5,9},{9,... | collective-permute-start | bytes 884744 | tf_op jit(solution)/shard_map/ppermute | solution.py:476
  54.9 16.9 %collective-permute-start.10 = (f32[6,3,32,128]{3,2,1,0:T(8,128)S(1)}, f32[6,3,32,128]{3,2,1,0:T(8,128)S(1)}, u32[]{:S(2)}, u32[]{:S(2)}) collective-permute-start(f32[6,3,32,128]{3,2,1,0:T(8,128)S(1)} %get-tuple-element.26), channel_id=1, source_target_pairs={{4,0},{8,4},{12,8},{16,12},{20,16},{24,20},{28,24},{5,1},{9,5},{13... | collective-permute-start | bytes 884744 | tf_op jit(solution)/shard_map/ppermute | solution.py:477
  66.6 14.8 %collective-permute-start.6 = (f32[4,6,3,8,128]{4,3,2,1,0:T(8,128)S(1)}, f32[4,6,3,8,128]{4,3,2,1,0:T(8,128)S(1)}, u32[]{:S(2)}, u32[]{:S(2)}) collective-permute-start(f32[4,6,3,8,128]{4,3,2,1,0:T(8,128)S(1)} %add.19.refs_0_), channel_id=1, source_target_pairs={{8,0},{9,1},{10,2},{11,3}} | collective-permute-start | bytes 884744 | tf_op jit(solution)/shard_map/ppermute | solution.py:483
  67.9 13.5 %collective-permute-start.5 = (f32[4,6,3,8,128]{4,3,2,1,0:T(8,128)S(1)}, f32[4,6,3,8,128]{4,3,2,1,0:T(8,128)S(1)}, u32[]{:S(2)}, u32[]{:S(2)}) collective-permute-start(f32[4,6,3,8,128]{4,3,2,1,0:T(8,128)S(1)} %add.19.refs_0_), channel_id=1, source_target_pairs={{4,0},{5,1},{6,2},{7,3}} | collective-permute-start | bytes 884744 | tf_op jit(solution)/shard_map/ppermute | solution.py:483
  69.2 12.2 %collective-permute-start.8 = (f32[4,3,3,8,128]{4,3,2,1,0:T(8,128)S(1)}, f32[4,3,3,8,128]{4,3,2,1,0:T(8,128)S(1)}, u32[]{:S(2)}, u32[]{:S(2)}) collective-permute-start(f32[4,3,3,8,128]{4,3,2,1,0:T(8,128)S(1)} %add.20), channel_id=1, source_target_pairs={{8,0},{9,1},{10,2},{11,3}} | collective-permute-start | bytes 442376 | tf_op jit(solution)/shard_map/ppermute | solution.py:483
  70.5 10.9 %collective-permute-start.7 = (f32[4,3,3,8,128]{4,3,2,1,0:T(8,128)S(1)}, f32[4,3,3,8,128]{4,3,2,1,0:T(8,128)S(1)}, u32[]{:S(2)}, u32[]{:S(2)}) collective-permute-start(f32[4,3,3,8,128]{4,3,2,1,0:T(8,128)S(1)} %add.20), channel_id=1, source_target_pairs={{4,0},{5,1},{6,2},{7,3}} | collective-permute-start | bytes 442376 | tf_op jit(solution)/shard_map/ppermute | solution.py:483
